TPU v7x, 256 devices: a whole 4x4x8 slice. The times are simulated.
256 devices in a mesh: blk: 32 (over z, y), aux: 8 (over x, core).
Axes of the slice: x: 4, y: 4, z: 8, core: 2. Of those that a mesh axis runs over, the one named last changes fastest.
Arguments:
- pair_cols: int32 [32, 16], P('blk'), may hold values from 0 to 31, as said below
- pair_count: int32 [32], P('blk'), may hold values from 1 to 16, as said below
- integrals: bfloat16 [512, 32, 128, 128], P('blk', 'aux'), may hold values from -1 to 1
- coeffs: bfloat16 [4096, 512], P('blk'), may hold values from -8 to 8
Outputs:
- exchange: float32 [4096, 4096], P('blk', 'aux')
Inputs may be any that keep to these rules, and one draw needn't show every extreme that they name: `pair_cols`: entry s of row M is M for s = 0; within a row all entries are distinct blocks. `pair_count`: some row block lists all 16 slots.
All inputs are finite; a program needn't handle non-finite values.
Results may differ from a plain program's by a relative error of at most 0.00072.
Values may be sent and summed in bfloat16 or wider, within the bound.
No kernel may reach another device: no remote copies, remote signals or barrier semaphores. Data moves between devices by JAX's collectives and lax.ppermute only.
A program may use at most 64 MiB of HBM per device.

v0:
```python
import math

import jax
import jax.numpy as jnp
from jax import lax
from jax.sharding import PartitionSpec as P


def shards(pair_cols, pair_count, integrals, coeffs):
    width = integrals.shape[2]
    aux_here = integrals.shape[1]
    occupied = coeffs.shape[1]
    whole_coeffs = lax.all_gather(coeffs, "blk", axis=0, tiled=True)
    counted = pair_count[0]

    def add_pair(counter, total):
        column = pair_cols[0, counter]
        coeff_rows = lax.dynamic_slice_in_dim(whole_coeffs, column * width, width, 0)
        block_tile = lax.dynamic_index_in_dim(integrals, counter, 0, keepdims=False)
        return total + jnp.einsum(
            "pml,li->pmi", block_tile, coeff_rows, preferred_element_type=jnp.float32
        )

    started = jnp.zeros((aux_here, width, occupied), jnp.float32)
    halfway = lax.fori_loop(0, counted, add_pair, started).astype(jnp.bfloat16)
    partial_rows = jnp.einsum(
        "pmi,pni->mn",
        halfway,
        lax.all_gather(halfway, "blk", axis=1, tiled=True),
        preferred_element_type=jnp.float32,
    )
    scale = 1.0 / math.sqrt(aux_here * lax.axis_size("aux") * occupied)
    return lax.psum_scatter(partial_rows, "aux", scatter_dimension=1, tiled=True) * scale


def solution(mesh):
    placed = (P("blk", None), P("blk"), P("blk", "aux", None, None), P("blk", None))
    return jax.shard_map(
        shards, mesh=mesh, in_specs=placed, out_specs=P("blk", "aux"), check_vma=False
    )
```

profile of v0, /device:TPU:1, one launch (start us, length us, event | category | flops | bytes accessed | tf_op | source)
XLA Modules:
  0.0 367.7 jit_solution(13518986956076551042)
XLA Ops:
  6.5 0.0 all-gather.3.cloned.1.call-start
  6.5 0.7 all-gather.3.cloned.1.call-update
  7.3 0.0 all-gather.5.cloned.1.call-start
  7.3 85.7 %all-gather.3.cloned.1.call-done = bf16[4096,512]{1,0:T(8,128)(2,1)} async-done(((bf16[128,512]{1,0:T(8,128)(2,1)}), bf16[4096,512]{1,0:T(8,128)(2,1)}) %all-gather.3.cloned.1.call-update) | async-done | bytes 4194320 | tf_op jit(solution)/shard_map/all_gather | solution.py:13
  93.0 0.1 broadcast_in_dim.3
  93.1 36.0 %while.10 = (s32[]{:T(128)}, f32[4,128,512]{2,1,0:T(8,128)S(1)}, s32[]{:T(128)}, bf16[16,4,128,128]{3,2,1,0:T(8,128)(2,1)}, s32[1,16]{1,0:T(1,128)}, /*index=5*/...) while((s32[]{:T(128)}, f32[4,128,512]{2,1,0:T(8,128)S(1)}, s32[]{:T(128)}, ...), condition=%wide.region_1.2_spmd, body=%wide.region_0.1_spmd.sunk | while | flops 67371016 | bytes 2359493 | solution.py:25
  93.8 1.3 fusion.13
  96.9 1.3 convolution_add_fusion.2
  98.8 1.3 fusion.13
  101.9 1.3 convolution_add_fusion.2
  103.9 1.3 fusion.13
  107.0 1.3 convolution_add_fusion.2
  108.9 1.3 fusion.13
  112.0 1.3 convolution_add_fusion.2
  114.0 1.3 fusion.13
  117.1 1.3 convolution_add_fusion.2
  119.0 1.3 fusion.13
  122.1 1.3 convolution_add_fusion.2
  124.1 1.3 fusion.13
  127.2 1.3 convolution_add_fusion.2
  129.1 0.9 convert_element_type.3
  130.0 0.0 all-gather.5.cloned.1.call-update
  130.0 0.0 reduce-scatter.2.cloned.1.call-start
  130.0 185.6 %all-gather.5.cloned.1.call-done = bf16[4,4096,512]{2,1,0:T(8,128)(2,1)} async-done(((bf16[4,128,512]{2,1,0:T(8,128)(2,1)}), bf16[4,4096,512]{2,1,0:T(8,128)(2,1)}) %all-gather.5.cloned.1.call-update) | async-done | bytes 16777232 | tf_op jit(solution)/shard_map/all_gather | solution.py:29
  315.7 12.7 %convolution_bitcast_fusion = f32[128,4096]{1,0:T(8,128)} fusion(bf16[4,128,512]{2,1,0:T(8,128)(2,1)} %convert_element_type.3, bf16[4,4096,512]{2,1,0:T(8,128)(2,1)} %all-gather.5.cloned.1.call-done), kind=kOutput, calls=%fused_computation.7 | convolution fusion | flops 2147483648 | bytes 19398656 | tf_op jit(solution)/shard_map/pmi,pni->mn/dot_general | solution.py:26
  328.4 0.0 reduce-scatter.2.cloned.1.call-update
  328.4 31.1 %reduce-scatter.2.cloned.1.call-done = f32[128,512]{1,0:T(8,128)} async-done(((f32[128,4096]{1,0:T(8,128)}), f32[128,512]{1,0:T(8,128)}) %reduce-scatter.2.cloned.1.call-update) | async-done | bytes 262160 | tf_op jit(solution)/shard_map/reduce_scatter | solution.py:33
  359.5 1.7 broadcast_multiply_fusion
Async XLA Ops:
  6.5 86.4 %all-gather.3.cloned.1.call-start = ((), (), s32[]{:S(2)}) async-start(), calls=%async_computation.1 | async-start | bytes 4325376 | tf_op jit(solution)/shard_map/all_gather | solution.py:13
  7.3 308.4 %all-gather.5.cloned.1.call-start = ((), (), s32[]{:S(2)}) async-start(), calls=%async_computation.2 | async-start | bytes 17301504 | tf_op jit(solution)/shard_map/all_gather | solution.py:29
  130.0 229.5 %reduce-scatter.2.cloned.1.call-start = ((), (), s32[]{:S(2)}) async-start(), calls=%async_computation.3 | async-start | bytes 2359296 | tf_op jit(solution)/shard_map/reduce_scatter | solution.py:33
Sparse Core Ops, SparseCore 0:
  9.9 82.9 all-gather.2
  130.1 185.4 all-gather.4
  328.5 30.9 reduce-scatter.1
where the time goes:
time: 370 us; the launch traced here: 368 us
  waiting for transfers between devices  303 us (82%)
  matrix products  21.7 us (6%)
  loops' own time  18.1 us (5%)
  between operations  13.1 us (4%)
  other arithmetic  11.4 us (3%)
    all_gather x1, waiting for transfers between devices, shards(): lax.all_gather(halfway, 'blk', axis=1, tiled=True)  186 us
    all_gather x1, waiting for transfers between devices, shards(): whole_coeffs = lax.all_gather(coeffs, 'blk', axis=0, tiled=True)  85.7 us
    reduce_scatter x1, waiting for transfers between devices, shards(): lax.psum_scatter(partial_rows, 'aux', scatter_dimension=1, tiled=True)  31.1 us
    another operation x1, loops' own time, shards(): halfway = lax.fori_loop(0, counted, add_pair, started).astype(jnp.bfloat16)  18.1 us
    dot_general x1, matrix products, shards(): jnp.einsum('pmi,pni->mn', halfway, lax.all_gather(halfway, 'blk', axis=1,...  12.7 us
    dot_general x7, matrix products, add_pair(): jnp.einsum('pml,li->pmi', block_tile, coeff_rows, preferred_element_type=...  8.95 us
    mul x7, other arithmetic, add_pair(): column * width  8.91 us
  transfers between devices with their start and end apart: 3, of which 3 were waited for; matrix products, arithmetic and copies ran while one was open for 0% of the time, Pallas kernels for 0%

commit v1 on v0

v1 whole, which is shorter than its diff:
```python
import math

import jax
import jax.numpy as jnp
from jax import lax
from jax.experimental import pallas as pl
from jax.experimental.pallas import tpu as pltpu
from jax.sharding import Mesh, PartitionSpec as P

NZ, NY, NX, NC = 8, 4, 4, 2
SLOTS, BLOCK, NOCC, AUX_HERE = 16, 128, 512, 4
HALF_L = BLOCK // NC
SLICE = NOCC // NX
LIMIT = 40 * 1024 * 1024

VMEM = pl.BlockSpec(memory_space=pltpu.VMEM)
SMEM = pl.BlockSpec(memory_space=pltpu.SMEM)


def shift(x, axis, size, step):
    return lax.ppermute(x, axis, [(i, (i + step) % size) for i in range(size)])


def pick_kernel(cols, count, gathered, out):
    counted = count[0]
    for s in range(SLOTS):
        rows = gathered[cols[0, s]]
        out[s] = jnp.where(s < counted, rows, jnp.zeros_like(rows))


def pick(cols, count, gathered):
    return pl.pallas_call(
        pick_kernel,
        out_shape=jax.ShapeDtypeStruct((SLOTS, HALF_L, SLICE), jnp.bfloat16),
        in_specs=[SMEM, SMEM, VMEM],
        out_specs=VMEM,
        compiler_params=pltpu.CompilerParams(vmem_limit_bytes=LIMIT),
    )(cols, count, gathered)


def half_kernel(core, integrals, *refs):
    mine, other, out = refs[:NX], refs[NX:2 * NX], refs[2 * NX]
    first = core[0] == 0
    left = jnp.concatenate(
        [integrals[s].reshape(AUX_HERE * BLOCK, BLOCK) for s in range(SLOTS)], axis=1
    )
    for h in range(2):
        parts = []
        for d in (2 * h, 2 * h + 1):
            a, b = mine[d][...], other[d][...]
            top, low = jnp.where(first, a, b), jnp.where(first, b, a)
            parts.append(jnp.concatenate([top, low], axis=1).reshape(SLOTS * BLOCK, SLICE))
        right = jnp.concatenate(parts, axis=1)
        done = jnp.dot(left, right, preferred_element_type=jnp.float32).astype(jnp.bfloat16)
        for p in range(AUX_HERE):
            out[h, :, p * 2 * SLICE:(p + 1) * 2 * SLICE] = done[p * BLOCK:(p + 1) * BLOCK]


def half_transform(core, integrals, mine, other):
    return pl.pallas_call(
        half_kernel,
        out_shape=jax.ShapeDtypeStruct((2, BLOCK, AUX_HERE * 2 * SLICE), jnp.bfloat16),
        in_specs=[SMEM] + [VMEM] * (1 + 2 * NX),
        out_specs=VMEM,
        compiler_params=pltpu.CompilerParams(vmem_limit_bytes=LIMIT),
    )(core, integrals, *mine, *other)


def tile_kernel(place, *refs):
    out = refs[-1]
    g0, gm, gp, g2a, g2b = refs[:5]
    v = refs[5:-1]
    z, y, core = place[0], place[1], place[2]
    rows = [
        jnp.concatenate([g0[0], gm[0], gp[0], g2a[...]], axis=0),
        jnp.concatenate([g0[1], gm[1], gp[1], g2b[...]], axis=0),
    ]
    row_at = [y, lax.rem(y + 3, NY), lax.rem(y + 1, NY), lax.rem(y + 2, NY)]
    pairs = [
        ((v[1], v[2]), (-1, 1)),
        ((v[3], v[4]), (-2, 2)),
        ((v[5], v[6]), (-3, 3)),
        ((v[0], None), (0, 4)),
    ]
    dims = (((1,), (1,)), ((), ()))
    for (a, b), offsets in pairs:
        total = None
        for h in range(2):
            second = b[h] if b is not None else v[7 + h][...]
            columns = jnp.concatenate([a[h], second], axis=0)
            term = lax.dot_general(rows[h], columns, dims, preferred_element_type=jnp.float32)
            total = term if total is None else total + term
        for n, offset in enumerate(offsets):
            at = lax.rem(z + offset + NZ, NZ)
            x_at, side = lax.div(at, NC), lax.rem(lax.rem(at, NC) + core, NC)
            for r in range(NY):
                out[side, row_at[r] * NX + x_at] = total[
                    r * BLOCK:(r + 1) * BLOCK, n * BLOCK:(n + 1) * BLOCK
                ]


def tile_product(place, rows, columns):
    return pl.pallas_call(
        tile_kernel,
        out_shape=jax.ShapeDtypeStruct((NC, NY * NX, BLOCK, BLOCK), jnp.float32),
        in_specs=[SMEM] + [VMEM] * (len(rows) + len(columns)),
        out_specs=VMEM,
        compiler_params=pltpu.CompilerParams(vmem_limit_bytes=LIMIT),
    )(place, *rows, *columns)


def finish_kernel(scale, parts, out):
    for yy in range(NY):
        total = parts[yy * NX]
        for xx in range(1, NX):
            total = total + parts[yy * NX + xx]
        out[:, yy * BLOCK:(yy + 1) * BLOCK] = total * scale


def finish(parts, scale):
    def body(parts_ref, out):
        finish_kernel(scale, parts_ref, out)

    return pl.pallas_call(
        body,
        out_shape=jax.ShapeDtypeStruct((BLOCK, NY * BLOCK), jnp.float32),
        in_specs=[VMEM],
        out_specs=VMEM,
        compiler_params=pltpu.CompilerParams(vmem_limit_bytes=LIMIT),
    )(parts)


def shards(pair_cols, pair_count, integrals, coeffs):
    z, y = lax.axis_index("z"), lax.axis_index("y")
    x, core = lax.axis_index("x"), lax.axis_index("core")

    piece = lax.dynamic_slice(coeffs, (core * HALF_L, x * SLICE), (HALF_L, SLICE))
    gathered = lax.all_to_all(
        jnp.broadcast_to(piece[None], (NZ * NY, HALF_L, SLICE)), ("z", "y"), 0, 0, tiled=True
    )
    picked = pick(pair_cols, pair_count, gathered)
    mine = [picked] + [shift(picked, "x", NX, d) for d in (1, 3, 2)]
    other = [shift(m, "core", NC, 1) for m in mine]
    halfway = half_transform(core[None], integrals, mine, other)

    y_up, y_down = shift(halfway, "y", NY, 1), shift(halfway, "y", NY, -1)
    y_far = [shift(y_up[0], "y", NY, 1), shift(y_down[1], "y", NY, -1)]
    rows = [halfway, y_up, y_down] + y_far
    columns = [halfway]
    up = down = halfway
    for _ in range(3):
        up, down = shift(up, "z", NZ, 1), shift(down, "z", NZ, -1)
        columns += [up, down]
    columns += [shift(up[0], "z", NZ, 1), shift(down[1], "z", NZ, -1)]
    place = jnp.stack([z, y, core]).astype(jnp.int32)
    tile = tile_product(place, rows, columns)

    both = tile[0] + shift(tile[1], "core", NC, 1)
    parts = lax.all_to_all(both, ("y", "x"), 0, 0, tiled=True)
    scale = 1.0 / math.sqrt(AUX_HERE * NX * NC * NOCC)
    return finish(parts, scale)


def solution(mesh):
    grid = Mesh(mesh.devices.reshape(NZ, NY, NX, NC), ("z", "y", "x", "core"))
    blk, aux = ("z", "y"), ("x", "core")
    placed = (P(blk, None), P(blk), P(blk, aux, None, None), P(blk, None))
    return jax.shard_map(
        shards, mesh=grid, in_specs=placed, out_specs=P(blk, aux), check_vma=False
    )
```

time: 370 us -> 136 us (0.37)
  waiting for transfers between devices: 303 us -> 52 us
  starting transfers between devices: 0.08 us -> 45.4 us
  blocking collectives: 0 us -> 21.9 us
  matrix products: 21.7 us -> 0 us
  loops' own time: 18.1 us -> 0 us
  between operations: 13.1 us -> 0.75 us
  other arithmetic: 11.4 us -> 0.22 us
  local copies, waits for them, and re-layouts: 0.11 us -> 9.45 us
  Pallas kernels: 0 us -> 6.23 us
    all_gather x2 -> x0, waiting for transfers between devices: 271 us -> none  [the longest x1 186 us: shards(): lax.all_gather(halfway, 'blk', axis=1, tiled=True)]
    ppermute x0 -> x20, waiting for transfers between devices: none -> 36.4 us  [shift(): return lax.ppermute(x, axis, [(i, (i + step) % size) for i in range(size)])]
    ppermute x0 -> x20, starting transfers between devices: none -> 33.4 us  [shift(): return lax.ppermute(x, axis, [(i, (i + step) % size) for i in range(size)])]
    reduce_scatter x1 -> x0, waiting for transfers between devices: 31.1 us -> none  [shards(): lax.psum_scatter(partial_rows, 'aux', scatter_dimension=1, tiled=True)]
    all_to_all x0 -> x1, blocking collectives: none -> 21.9 us  [shards(): parts = lax.all_to_all(both, ('y', 'x'), 0, 0, tiled=True)]
    dot_general x8 -> x0, matrix products: 21.7 us -> none  [the longest x1 12.7 us: shards(): jnp.einsum('pmi,pni->mn', halfway, lax.all_gather(halfway, 'blk', axis=1,...]
    another operation x1 -> x0, loops' own time: 18.1 us -> none  [shards(): halfway = lax.fori_loop(0, counted, add_pair, started).astype(jnp.bfloat16)]
    all_to_all x0 -> x1, waiting for transfers between devices: none -> 15.6 us  [shards(): lax.all_to_all(jnp.broadcast_to(piece[None], (NZ * NY, HALF_L, SLICE)), (...]
  transfers between devices with their start and end apart: 3 -> 21, of which waited for: 3 -> 10; matrix products, arithmetic and copies ran while one was open for 0% -> 2% of each run, Pallas kernels for 0% -> 0%
where the time goes in v1:
time: 136 us
  waiting for transfers between devices  52 us (38%)
  starting transfers between devices  45.4 us (33%)
  blocking collectives  21.9 us (16%)
  local copies, waits for them, and re-layouts  9.45 us (7%)
  Pallas kernels  6.23 us (5%)
    ppermute x20, waiting for transfers between devices, shift(): return lax.ppermute(x, axis, [(i, (i + step) % size) for i in range(size)])  36.4 us
    ppermute x20, starting transfers between devices, shift(): return lax.ppermute(x, axis, [(i, (i + step) % size) for i in range(size)])  33.4 us
    all_to_all x1, blocking collectives, shards(): parts = lax.all_to_all(both, ('y', 'x'), 0, 0, tiled=True)  21.9 us
    all_to_all x1, waiting for transfers between devices, shards(): lax.all_to_all(jnp.broadcast_to(piece[None], (NZ * NY, HALF_L, SLICE)), (...  15.6 us
    all_to_all x1, starting transfers between devices, shards(): lax.all_to_all(jnp.broadcast_to(piece[None], (NZ * NY, HALF_L, SLICE)), (...  12 us
    unnamed x16, local copies, waits for them, and re-layouts  4.6 us
    pallas_call x1, Pallas kernels, tile_product(): pl.pallas_call(tile_kernel, out_shape=jax.ShapeDtypeStruct((NC, NY * NX,...  3.57 us
  transfers between devices with their start and end apart: 21, of which 10 were waited for; matrix products, arithmetic and copies ran while one was open for 2% of the time, Pallas kernels for 0%

profile of v1, /device:TPU:1, one launch (start us, length us, event | category | flops | bytes accessed | tf_op | source)
XLA Modules:
  0.0 136.0 jit_solution(8188404884394322645)
XLA Ops:
  0.0 0.9 dynamic_slice.3
  0.9 0.9 broadcast_in_dim.2
  1.8 12.0 %all-to-all-start = ((bf16[32,64,128]{2,1,0:T(8,128)(2,1)}), bf16[32,64,128]{2,1,0:T(8,128)(2,1)S(1)}, u32[]{:S(2)}, u32[]{:S(2)}) async-start(bf16[32,64,128]{2,1,0:T(8,128)(2,1)} %broadcast_in_dim.2), calls=%async_computation | async-start | bytes 1048576 | tf_op jit(solution)/shard_map/all_to_all | solution.py:138
  14.5 15.6 %all-to-all-done.gathered = bf16[32,64,128]{2,1,0:T(8,128)(2,1)S(1)} async-done(((bf16[32,64,128]{2,1,0:T(8,128)(2,1)}), bf16[32,64,128]{2,1,0:T(8,128)(2,1)S(1)}, u32[]{:S(2)}, u32[]{:S(2)}) %all-to-all-start) | async-done | bytes 524320 | tf_op jit(solution)/shard_map/all_to_all | solution.py:138
  30.1 0.7 copy-done.7
  30.8 0.6 shard_map.46.refs_0_
  31.4 2.8 %collective-permute-start.2 = (bf16[16,64,128]{2,1,0:T(8,128)(2,1)S(1)}, bf16[16,64,128]{2,1,0:T(8,128)(2,1)S(1)}, u32[]{:S(2)}, u32[]{:S(2)}) collective-permute-start(bf16[16,64,128]{2,1,0:T(8,128)(2,1)S(1)} %shard_map.46.refs_0_), channel_id=1, source_target_pairs={{0,4},{2,6},{4,0},{6,2},{1,5},{3,7},{5,1},{7,3},{8,12},{10,14},{12... | collective-permute-start | bytes 786440 | tf_op jit(solution)/shard_map/ppermute | solution.py:21
  34.2 0.9 collective-permute-start.1
  35.1 0.6 collective-permute-start
  35.7 3.2 %collective-permute-start.3 = (bf16[16,64,128]{2,1,0:T(8,128)(2,1)S(1)}, bf16[16,64,128]{2,1,0:T(8,128)(2,1)S(1)}, u32[]{:S(2)}, u32[]{:S(2)}) collective-permute-start(bf16[16,64,128]{2,1,0:T(8,128)(2,1)S(1)} %shard_map.46.refs_0_), channel_id=1, source_target_pairs={{0,1},{1,0},{2,3},{3,2},{4,5},{5,4},{6,7},{7,6},{8,9},{9,8},{10,11... | collective-permute-start | bytes 786440 | tf_op jit(solution)/shard_map/ppermute | solution.py:21
  38.9 0.0 collective-permute-done.2.refs_3_
  38.9 5.7 %collective-permute-start.6 = (bf16[16,64,128]{2,1,0:T(8,128)(2,1)S(1)}, bf16[16,64,128]{2,1,0:T(8,128)(2,1)S(1)}, u32[]{:S(2)}, u32[]{:S(2)}) collective-permute-start(bf16[16,64,128]{2,1,0:T(8,128)(2,1)S(1)} %collective-permute-done.2.refs_3_), channel_id=1, source_target_pairs={{0,1},{1,0},{2,3},{3,2},{4,5},{5,4},{6,7},{7,6},{8,9},{9,8},{10,11... | collective-permute-start | bytes 786440 | tf_op jit(solution)/shard_map/ppermute | solution.py:21
  44.6 0.7 collective-permute-done.1.refs_2_
  45.3 2.2 %collective-permute-start.5 = (bf16[16,64,128]{2,1,0:T(8,128)(2,1)S(1)}, bf16[16,64,128]{2,1,0:T(8,128)(2,1)S(1)}, u32[]{:S(2)}, u32[]{:S(2)}) collective-permute-start(bf16[16,64,128]{2,1,0:T(8,128)(2,1)S(1)} %collective-permute-done.1.refs_2_), channel_id=1, source_target_pairs={{0,1},{1,0},{2,3},{3,2},{4,5},{5,4},{6,7},{7,6},{8,9},{9,8},{10,11... | collective-permute-start | bytes 786440 | tf_op jit(solution)/shard_map/ppermute | solution.py:21
  47.5 0.0 collective-permute-done.refs_1_
  47.5 0.2 collective-permute-start.4
  47.6 0.0 collective-permute-done.3.refs_4_
  47.6 0.0 collective-permute-done.6.refs_7_
  47.6 1.0 collective-permute-done.5.refs_6_
  48.6 0.4 collective-permute-done.4.refs_5_
  49.0 0.0 copy-done
  49.0 1.3 shard_map.47.refs_0_.refs_5_
  50.3 0.1 collective-permute-start.12
  50.4 1.5 %collective-permute-start.11 = (bf16[2,128,1024]{2,1,0:T(8,128)(2,1)S(1)}, bf16[2,128,1024]{2,1,0:T(8,128)(2,1)S(1)}, u32[]{:S(2)}, u32[]{:S(2)}) collective-permute-start(bf16[2,128,1024]{2,1,0:T(8,128)(2,1)S(1)} %shard_map.47.refs_0_.refs_5_), channel_id=1, source_target_pairs={{0,32},{32,64},{64,96},{96,128},{128,160},{160,192},{192,224},{224... | collective-permute-start | bytes 1572872 | tf_op jit(solution)/shard_map/ppermute | solution.py:21
  51.8 11.7 %collective-permute-done.12.refs_7_ = bf16[2,128,1024]{2,1,0:T(8,128)(2,1)S(1)} collective-permute-done((bf16[2,128,1024]{2,1,0:T(8,128)(2,1)S(1)}, bf16[2,128,1024]{2,1,0:T(8,128)(2,1)S(1)}, u32[]{:S(2)}, u32[]{:S(2)}) %collective-permute-start.12) | collective-permute-done | bytes 524320 | tf_op jit(solution)/shard_map/ppermute | solution.py:21
  63.5 1.5 %collective-permute-start.14 = (bf16[2,128,1024]{2,1,0:T(8,128)(2,1)S(1)}, bf16[2,128,1024]{2,1,0:T(8,128)(2,1)S(1)}, u32[]{:S(2)}, u32[]{:S(2)}) collective-permute-start(bf16[2,128,1024]{2,1,0:T(8,128)(2,1)S(1)} %collective-permute-done.12.refs_7_), channel_id=1, source_target_pairs={{0,224},{32,0},{64,32},{96,64},{128,96},{160,128},{192,160},{224,1... | collective-permute-start | bytes 1572872 | tf_op jit(solution)/shard_map/ppermute | solution.py:21
  65.0 0.0 collective-permute-done.11.refs_6_
  65.0 0.0 collective-permute-start.13
  65.1 0.8 copy-done.1
  65.9 2.0 %collective-permute-start.8 = (bf16[2,128,1024]{2,1,0:T(8,128)(2,1)S(1)}, bf16[2,128,1024]{2,1,0:T(8,128)(2,1)S(1)}, u32[]{:S(2)}, u32[]{:S(2)}) collective-permute-start(bf16[2,128,1024]{2,1,0:T(8,128)(2,1)S(1)} %shard_map.47.refs_0_.refs_5_), channel_id=1, source_target_pairs={{0,24},{8,0},{16,8},{24,16},{1,25},{9,1},{17,9},{25,17},{2,26},{10... | collective-permute-start | bytes 1572872 | tf_op jit(solution)/shard_map/ppermute | solution.py:21
  67.9 0.0 collective-permute-start.7
  67.9 7.8 %collective-permute-done.14.refs_9_ = bf16[2,128,1024]{2,1,0:T(8,128)(2,1)S(1)} collective-permute-done((bf16[2,128,1024]{2,1,0:T(8,128)(2,1)S(1)}, bf16[2,128,1024]{2,1,0:T(8,128)(2,1)S(1)}, u32[]{:S(2)}, u32[]{:S(2)}) %collective-permute-start.14) | collective-permute-done | bytes 524320 | tf_op jit(solution)/shard_map/ppermute | solution.py:21
  75.7 3.1 %collective-permute-start.16 = (bf16[2,128,1024]{2,1,0:T(8,128)(2,1)S(1)}, bf16[2,128,1024]{2,1,0:T(8,128)(2,1)S(1)}, u32[]{:S(2)}, u32[]{:S(2)}) collective-permute-start(bf16[2,128,1024]{2,1,0:T(8,128)(2,1)S(1)} %collective-permute-done.14.refs_9_), channel_id=1, source_target_pairs={{0,224},{32,0},{64,32},{96,64},{128,96},{160,128},{192,160},{224,1... | collective-permute-start | bytes 1572872 | tf_op jit(solution)/shard_map/ppermute | solution.py:21
  78.8 0.0 collective-permute-done.13.refs_8_
  78.8 0.0 collective-permute-start.15
  78.8 0.0 collective-permute-done.8.refs_2_
  78.8 0.8 slice_bitcast_fusion.4
  79.6 2.0 %collective-permute-start.10 = (bf16[128,1024]{1,0:T(8,128)(2,1)}, bf16[128,1024]{1,0:T(8,128)(2,1)S(1)}, u32[]{:S(2)}, u32[]{:S(2)}) collective-permute-start(bf16[128,1024]{1,0:T(8,128)(2,1)} %slice_bitcast_fusion.4), channel_id=1, source_target_pairs={{0,24},{8,0},{16,8},{24,16},{1,25},{9,1},{17,9},{25,17},{2,26},{10... | collective-permute-start | bytes 786440 | tf_op jit(solution)/shard_map/ppermute | solution.py:21
  81.7 0.0 collective-permute-done.7.refs_1_
  81.7 0.7 slice_bitcast_fusion.5
  82.4 0.0 collective-permute-start.9
  82.4 5.9 %collective-permute-done.16.refs_11_ = bf16[2,128,1024]{2,1,0:T(8,128)(2,1)S(1)} collective-permute-done((bf16[2,128,1024]{2,1,0:T(8,128)(2,1)S(1)}, bf16[2,128,1024]{2,1,0:T(8,128)(2,1)S(1)}, u32[]{:S(2)}, u32[]{:S(2)}) %collective-permute-start.16) | collective-permute-done | bytes 524320 | tf_op jit(solution)/shard_map/ppermute | solution.py:21
  88.2 0.7 slice_bitcast_fusion.2
  89.0 3.4 %collective-permute-start.18 = (bf16[128,1024]{1,0:T(8,128)(2,1)}, bf16[128,1024]{1,0:T(8,128)(2,1)}, u32[]{:S(2)}, u32[]{:S(2)}) collective-permute-start(bf16[128,1024]{1,0:T(8,128)(2,1)} %slice_bitcast_fusion.2), channel_id=1, source_target_pairs={{0,224},{32,0},{64,32},{96,64},{128,96},{160,128},{192,160},{224,1... | collective-permute-start | bytes 786440 | tf_op jit(solution)/shard_map/ppermute | solution.py:21
  92.4 0.0 collective-permute-done.15.refs_10_
  92.4 0.0 copy-done.3
  92.4 0.7 slice_bitcast_fusion.3
  93.1 0.0 copy-done.5
  93.1 0.0 collective-permute-start.17
  93.1 0.1 pad_add_fusion.place
  93.2 0.0 collective-permute-done.10.refs_4_
  93.2 0.0 collective-permute-done.9.refs_3_
  93.2 2.8 %collective-permute-done.18.refs_13_ = bf16[128,1024]{1,0:T(8,128)(2,1)} collective-permute-done((bf16[128,1024]{1,0:T(8,128)(2,1)}, bf16[128,1024]{1,0:T(8,128)(2,1)}, u32[]{:S(2)}, u32[]{:S(2)}) %collective-permute-start.18) | collective-permute-done | bytes 262176 | tf_op jit(solution)/shard_map/ppermute | solution.py:21
  96.0 3.8 %collective-permute-done.17.refs_12_ = bf16[128,1024]{1,0:T(8,128)(2,1)} collective-permute-done((bf16[128,1024]{1,0:T(8,128)(2,1)}, bf16[128,1024]{1,0:T(8,128)(2,1)}, u32[]{:S(2)}, u32[]{:S(2)}) %collective-permute-start.17) | collective-permute-done | bytes 262176 | tf_op jit(solution)/shard_map/ppermute | solution.py:21
  99.9 1.0 copy-done.2
  100.9 1.0 copy-done.4
  102.0 1.0 copy-done.6
  103.0 3.6 %shard_map.48 = f32[2,16,128,128]{3,2,1,0:T(8,128)S(1)} custom-call(s32[3]{0:T(128)S(1)} %pad_add_fusion.place, bf16[2,128,1024]{2,1,0:T(8,128)(2,1)S(1)} %shard_map.47.refs_0_.refs_5_, bf16[2,128,1024]{2,1,0:T(8,128)(2,1)S(1)} %collective-permute-done.7.refs_1_, bf16[2,128,1024]{2,1,0:T(8,128)(2,1)S(1)} %collective-permute-done.8.refs_2_, ...), custom_call_target="tpu_custom_call" | custom-call | tf_op jit(solution)/shard_map/pallas_call | solution.py:103
  106.6 0.1 slice_bitcast_fusion
  106.7 4.2 %collective-permute-start.19 = (f32[16,128,128]{2,1,0:T(8,128)S(1)}, f32[16,128,128]{2,1,0:T(8,128)S(1)}, u32[]{:S(2)}, u32[]{:S(2)}) collective-permute-start(f32[16,128,128]{2,1,0:T(8,128)S(1)} %slice_bitcast_fusion), channel_id=1, source_target_pairs={{0,1},{1,0},{2,3},{3,2},{4,5},{5,4},{6,7},{7,6},{8,9},{9,8},{10,11... | collective-permute-start | bytes 3145736 | tf_op jit(solution)/shard_map/ppermute | solution.py:21
  110.9 2.3 %collective-permute-done.19 = f32[16,128,128]{2,1,0:T(8,128)S(1)} collective-permute-done((f32[16,128,128]{2,1,0:T(8,128)S(1)}, f32[16,128,128]{2,1,0:T(8,128)S(1)}, u32[]{:S(2)}, u32[]{:S(2)}) %collective-permute-start.19) | collective-permute-done | bytes 1048608 | tf_op jit(solution)/shard_map/ppermute | solution.py:21
  113.2 0.1 fusion
  113.3 21.9 %all_to_all.10.parts_ref = f32[16,128,128]{2,1,0:T(8,128)S(1)} all-to-all(f32[16,128,128]{2,1,0:T(8,128)S(1)} %fusion), channel_id=1, replica_groups=mesh['z'=8,'y'=4,'x'=4,'core'=2] {'y','x'}, dimensions={0} | all-to-all | bytes 2097152 | tf_op jit(solution)/shard_map/all_to_all | solution.py:159
  135.3 0.8 shard_map.49
  (8 shorter events, 0.0 us)
Async XLA Ops:
  0.0 49.0 %copy-start = (bf16[16,4,128,128]{3,2,1,0:T(8,128)(2,1)S(1)}, bf16[16,4,128,128]{3,2,1,0:T(8,128)(2,1)}, u32[]{:S(2)}) copy-start(bf16[16,4,128,128]{3,2,1,0:T(8,128)(2,1)} %integrals.1) | copy-start | bytes 6291460
  1.8 28.3 %all-to-all-start = ((bf16[32,64,128]{2,1,0:T(8,128)(2,1)}), bf16[32,64,128]{2,1,0:T(8,128)(2,1)S(1)}, u32[]{:S(2)}, u32[]{:S(2)}) async-start(bf16[32,64,128]{2,1,0:T(8,128)(2,1)} %broadcast_in_dim.2), calls=%async_computation | async-start | bytes 1048576 | tf_op jit(solution)/shard_map/all_to_all | solution.py:138
  30.1 0.7 copy-start.7
  31.4 7.5 %collective-permute-start.2 = (bf16[16,64,128]{2,1,0:T(8,128)(2,1)S(1)}, bf16[16,64,128]{2,1,0:T(8,128)(2,1)S(1)}, u32[]{:S(2)}, u32[]{:S(2)}) collective-permute-start(bf16[16,64,128]{2,1,0:T(8,128)(2,1)S(1)} %shard_map.46.refs_0_), channel_id=1, source_target_pairs={{0,4},{2,6},{4,0},{6,2},{1,5},{3,7},{5,1},{7,3},{8,12},{10,14},{12... | collective-permute-start | bytes 786440 | tf_op jit(solution)/shard_map/ppermute | solution.py:21
  34.2 11.1 %collective-permute-start.1 = (bf16[16,64,128]{2,1,0:T(8,128)(2,1)S(1)}, bf16[16,64,128]{2,1,0:T(8,128)(2,1)S(1)}, u32[]{:S(2)}, u32[]{:S(2)}) collective-permute-start(bf16[16,64,128]{2,1,0:T(8,128)(2,1)S(1)} %shard_map.46.refs_0_), channel_id=1, source_target_pairs={{0,6},{2,0},{4,2},{6,4},{1,7},{3,1},{5,3},{7,5},{8,14},{10,8},{12,... | collective-permute-start | bytes 786440 | tf_op jit(solution)/shard_map/ppermute | solution.py:21
  35.1 12.4 %collective-permute-start = (bf16[16,64,128]{2,1,0:T(8,128)(2,1)S(1)}, bf16[16,64,128]{2,1,0:T(8,128)(2,1)S(1)}, u32[]{:S(2)}, u32[]{:S(2)}) collective-permute-start(bf16[16,64,128]{2,1,0:T(8,128)(2,1)S(1)} %shard_map.46.refs_0_), channel_id=1, source_target_pairs={{0,2},{2,4},{4,6},{6,0},{1,3},{3,5},{5,7},{7,1},{8,10},{10,12},{12... | collective-permute-start | bytes 786440 | tf_op jit(solution)/shard_map/ppermute | solution.py:21
  35.7 11.9 %collective-permute-start.3 = (bf16[16,64,128]{2,1,0:T(8,128)(2,1)S(1)}, bf16[16,64,128]{2,1,0:T(8,128)(2,1)S(1)}, u32[]{:S(2)}, u32[]{:S(2)}) collective-permute-start(bf16[16,64,128]{2,1,0:T(8,128)(2,1)S(1)} %shard_map.46.refs_0_), channel_id=1, source_target_pairs={{0,1},{1,0},{2,3},{3,2},{4,5},{5,4},{6,7},{7,6},{8,9},{9,8},{10,11... | collective-permute-start | bytes 786440 | tf_op jit(solution)/shard_map/ppermute | solution.py:21
  38.9 8.7 %collective-permute-start.6 = (bf16[16,64,128]{2,1,0:T(8,128)(2,1)S(1)}, bf16[16,64,128]{2,1,0:T(8,128)(2,1)S(1)}, u32[]{:S(2)}, u32[]{:S(2)}) collective-permute-start(bf16[16,64,128]{2,1,0:T(8,128)(2,1)S(1)} %collective-permute-done.2.refs_3_), channel_id=1, source_target_pairs={{0,1},{1,0},{2,3},{3,2},{4,5},{5,4},{6,7},{7,6},{8,9},{9,8},{10,11... | collective-permute-start | bytes 786440 | tf_op jit(solution)/shard_map/ppermute | solution.py:21
  45.3 3.3 %collective-permute-start.5 = (bf16[16,64,128]{2,1,0:T(8,128)(2,1)S(1)}, bf16[16,64,128]{2,1,0:T(8,128)(2,1)S(1)}, u32[]{:S(2)}, u32[]{:S(2)}) collective-permute-start(bf16[16,64,128]{2,1,0:T(8,128)(2,1)S(1)} %collective-permute-done.1.refs_2_), channel_id=1, source_target_pairs={{0,1},{1,0},{2,3},{3,2},{4,5},{5,4},{6,7},{7,6},{8,9},{9,8},{10,11... | collective-permute-start | bytes 786440 | tf_op jit(solution)/shard_map/ppermute | solution.py:21
  47.5 1.5 %collective-permute-start.4 = (bf16[16,64,128]{2,1,0:T(8,128)(2,1)S(1)}, bf16[16,64,128]{2,1,0:T(8,128)(2,1)S(1)}, u32[]{:S(2)}, u32[]{:S(2)}) collective-permute-start(bf16[16,64,128]{2,1,0:T(8,128)(2,1)S(1)} %collective-permute-done.refs_1_), channel_id=1, source_target_pairs={{0,1},{1,0},{2,3},{3,2},{4,5},{5,4},{6,7},{7,6},{8,9},{9,8},{10,11... | collective-permute-start | bytes 786440 | tf_op jit(solution)/shard_map/ppermute | solution.py:21
  50.3 13.2 %collective-permute-start.12 = (bf16[2,128,1024]{2,1,0:T(8,128)(2,1)S(1)}, bf16[2,128,1024]{2,1,0:T(8,128)(2,1)S(1)}, u32[]{:S(2)}, u32[]{:S(2)}) collective-permute-start(bf16[2,128,1024]{2,1,0:T(8,128)(2,1)S(1)} %shard_map.47.refs_0_.refs_5_), channel_id=1, source_target_pairs={{0,224},{32,0},{64,32},{96,64},{128,96},{160,128},{192,160},{224,1... | collective-permute-start | bytes 1572872 | tf_op jit(solution)/shard_map/ppermute | solution.py:21
  50.4 14.7 %collective-permute-start.11 = (bf16[2,128,1024]{2,1,0:T(8,128)(2,1)S(1)}, bf16[2,128,1024]{2,1,0:T(8,128)(2,1)S(1)}, u32[]{:S(2)}, u32[]{:S(2)}) collective-permute-start(bf16[2,128,1024]{2,1,0:T(8,128)(2,1)S(1)} %shard_map.47.refs_0_.refs_5_), channel_id=1, source_target_pairs={{0,32},{32,64},{64,96},{96,128},{128,160},{160,192},{192,224},{224... | collective-permute-start | bytes 1572872 | tf_op jit(solution)/shard_map/ppermute | solution.py:21
  63.5 12.2 %collective-permute-start.14 = (bf16[2,128,1024]{2,1,0:T(8,128)(2,1)S(1)}, bf16[2,128,1024]{2,1,0:T(8,128)(2,1)S(1)}, u32[]{:S(2)}, u32[]{:S(2)}) collective-permute-start(bf16[2,128,1024]{2,1,0:T(8,128)(2,1)S(1)} %collective-permute-done.12.refs_7_), channel_id=1, source_target_pairs={{0,224},{32,0},{64,32},{96,64},{128,96},{160,128},{192,160},{224,1... | collective-permute-start | bytes 1572872 | tf_op jit(solution)/shard_map/ppermute | solution.py:21
  65.0 13.8 %collective-permute-start.13 = (bf16[2,128,1024]{2,1,0:T(8,128)(2,1)S(1)}, bf16[2,128,1024]{2,1,0:T(8,128)(2,1)S(1)}, u32[]{:S(2)}, u32[]{:S(2)}) collective-permute-start(bf16[2,128,1024]{2,1,0:T(8,128)(2,1)S(1)} %collective-permute-done.11.refs_6_), channel_id=1, source_target_pairs={{0,32},{32,64},{64,96},{96,128},{128,160},{160,192},{192,224},{224... | collective-permute-start | bytes 1572872 | tf_op jit(solution)/shard_map/ppermute | solution.py:21
  65.1 0.8 copy-start.1
  65.9 13.0 %collective-permute-start.8 = (bf16[2,128,1024]{2,1,0:T(8,128)(2,1)S(1)}, bf16[2,128,1024]{2,1,0:T(8,128)(2,1)S(1)}, u32[]{:S(2)}, u32[]{:S(2)}) collective-permute-start(bf16[2,128,1024]{2,1,0:T(8,128)(2,1)S(1)} %shard_map.47.refs_0_.refs_5_), channel_id=1, source_target_pairs={{0,24},{8,0},{16,8},{24,16},{1,25},{9,1},{17,9},{25,17},{2,26},{10... | collective-permute-start | bytes 1572872 | tf_op jit(solution)/shard_map/ppermute | solution.py:21
  67.9 13.8 %collective-permute-start.7 = (bf16[2,128,1024]{2,1,0:T(8,128)(2,1)S(1)}, bf16[2,128,1024]{2,1,0:T(8,128)(2,1)S(1)}, u32[]{:S(2)}, u32[]{:S(2)}) collective-permute-start(bf16[2,128,1024]{2,1,0:T(8,128)(2,1)S(1)} %shard_map.47.refs_0_.refs_5_), channel_id=1, source_target_pairs={{0,8},{8,16},{16,24},{24,0},{1,9},{9,17},{17,25},{25,1},{2,10},{10... | collective-permute-start | bytes 1572872 | tf_op jit(solution)/shard_map/ppermute | solution.py:21
  75.7 16.7 %copy-start.3 = (bf16[2,128,1024]{2,1,0:T(8,128)(2,1)}, bf16[2,128,1024]{2,1,0:T(8,128)(2,1)S(1)}, u32[]{:S(2)}) copy-start(bf16[2,128,1024]{2,1,0:T(8,128)(2,1)S(1)} %collective-permute-done.14.refs_9_) | copy-start | bytes 1572868
  75.7 12.5 %collective-permute-start.16 = (bf16[2,128,1024]{2,1,0:T(8,128)(2,1)S(1)}, bf16[2,128,1024]{2,1,0:T(8,128)(2,1)S(1)}, u32[]{:S(2)}, u32[]{:S(2)}) collective-permute-start(bf16[2,128,1024]{2,1,0:T(8,128)(2,1)S(1)} %collective-permute-done.14.refs_9_), channel_id=1, source_target_pairs={{0,224},{32,0},{64,32},{96,64},{128,96},{160,128},{192,160},{224,1... | collective-permute-start | bytes 1572872 | tf_op jit(solution)/shard_map/ppermute | solution.py:21
  78.8 14.3 %copy-start.5 = (bf16[2,128,1024]{2,1,0:T(8,128)(2,1)}, bf16[2,128,1024]{2,1,0:T(8,128)(2,1)S(1)}, u32[]{:S(2)}) copy-start(bf16[2,128,1024]{2,1,0:T(8,128)(2,1)S(1)} %collective-permute-done.13.refs_8_) | copy-start | bytes 1572868
  78.8 13.6 %collective-permute-start.15 = (bf16[2,128,1024]{2,1,0:T(8,128)(2,1)S(1)}, bf16[2,128,1024]{2,1,0:T(8,128)(2,1)S(1)}, u32[]{:S(2)}, u32[]{:S(2)}) collective-permute-start(bf16[2,128,1024]{2,1,0:T(8,128)(2,1)S(1)} %collective-permute-done.13.refs_8_), channel_id=1, source_target_pairs={{0,32},{32,64},{64,96},{96,128},{128,160},{160,192},{192,224},{224... | collective-permute-start | bytes 1572872 | tf_op jit(solution)/shard_map/ppermute | solution.py:21
  79.6 13.6 %collective-permute-start.10 = (bf16[128,1024]{1,0:T(8,128)(2,1)}, bf16[128,1024]{1,0:T(8,128)(2,1)S(1)}, u32[]{:S(2)}, u32[]{:S(2)}) collective-permute-start(bf16[128,1024]{1,0:T(8,128)(2,1)} %slice_bitcast_fusion.4), channel_id=1, source_target_pairs={{0,24},{8,0},{16,8},{24,16},{1,25},{9,1},{17,9},{25,17},{2,26},{10... | collective-permute-start | bytes 786440 | tf_op jit(solution)/shard_map/ppermute | solution.py:21
  82.4 10.8 %collective-permute-start.9 = (bf16[128,1024]{1,0:T(8,128)(2,1)}, bf16[128,1024]{1,0:T(8,128)(2,1)}, u32[]{:S(2)}, u32[]{:S(2)}) collective-permute-start(bf16[128,1024]{1,0:T(8,128)(2,1)} %slice_bitcast_fusion.5), channel_id=1, source_target_pairs={{0,8},{8,16},{16,24},{24,0},{1,9},{9,17},{17,25},{25,1},{2,10},{10... | collective-permute-start | bytes 786440 | tf_op jit(solution)/shard_map/ppermute | solution.py:21
  89.0 7.0 %collective-permute-start.18 = (bf16[128,1024]{1,0:T(8,128)(2,1)}, bf16[128,1024]{1,0:T(8,128)(2,1)}, u32[]{:S(2)}, u32[]{:S(2)}) collective-permute-start(bf16[128,1024]{1,0:T(8,128)(2,1)} %slice_bitcast_fusion.2), channel_id=1, source_target_pairs={{0,224},{32,0},{64,32},{96,64},{128,96},{160,128},{192,160},{224,1... | collective-permute-start | bytes 786440 | tf_op jit(solution)/shard_map/ppermute | solution.py:21
  93.1 6.7 %collective-permute-start.17 = (bf16[128,1024]{1,0:T(8,128)(2,1)}, bf16[128,1024]{1,0:T(8,128)(2,1)}, u32[]{:S(2)}, u32[]{:S(2)}) collective-permute-start(bf16[128,1024]{1,0:T(8,128)(2,1)} %slice_bitcast_fusion.3), channel_id=1, source_target_pairs={{0,32},{32,64},{64,96},{96,128},{128,160},{160,192},{192,224},{224... | collective-permute-start | bytes 786440 | tf_op jit(solution)/shard_map/ppermute | solution.py:21
  99.9 1.0 copy-start.2
  100.9 1.0 copy-start.4
  102.0 1.0 copy-start.6
  106.7 6.5 %collective-permute-start.19 = (f32[16,128,128]{2,1,0:T(8,128)S(1)}, f32[16,128,128]{2,1,0:T(8,128)S(1)}, u32[]{:S(2)}, u32[]{:S(2)}) collective-permute-start(f32[16,128,128]{2,1,0:T(8,128)S(1)} %slice_bitcast_fusion), channel_id=1, source_target_pairs={{0,1},{1,0},{2,3},{3,2},{4,5},{5,4},{6,7},{7,6},{8,9},{9,8},{10,11... | collective-permute-start | bytes 3145736 | tf_op jit(solution)/shard_map/ppermute | solution.py:21

commit v2 on v0

v2 whole, which is shorter than its diff:
```python
import functools
import math

import jax
import jax.numpy as jnp
from jax import lax
from jax.experimental import pallas as pl
from jax.experimental.pallas import tpu as pltpu
from jax.sharding import Mesh, PartitionSpec as P

NZ, NY, NX, NC = 8, 4, 4, 2
SLOTS, BLOCK, NOCC, AUX_HERE = 16, 128, 512, 4
HALF_L = BLOCK // NC
SLICE = NOCC // NX
CHUNK = AUX_HERE * SLICE
ROWS = AUX_HERE * BLOCK
LIMIT = 24 * 1024 * 1024
VMEM = pl.BlockSpec(memory_space=pltpu.VMEM)
SMEM = pl.BlockSpec(memory_space=pltpu.SMEM)


def call(body, out_shape, scalars, arrays, flops=None, aliases=None):
    return pl.pallas_call(
        body,
        out_shape=out_shape,
        in_specs=[SMEM] * len(scalars) + [VMEM] * len(arrays),
        out_specs=jax.tree.map(lambda _: VMEM, out_shape),
        cost_estimate=flops and pl.CostEstimate(flops=flops, bytes_accessed=12000000, transcendentals=0),
        input_output_aliases=aliases or {},
        compiler_params=pltpu.CompilerParams(vmem_limit_bytes=LIMIT),
    )(*scalars, *arrays)


def bf16(*shape):
    return jax.ShapeDtypeStruct(shape, jnp.bfloat16)


def shift(x, axis, size, step):
    return lax.ppermute(x, axis, [(i, (i + step) % size) for i in range(size)])


def mirrored(x, axis, size, step):
    pairs = []
    for i in range(size):
        pairs.append((i * NC, (i + step) % size * NC))
        pairs.append((i * NC + 1, (i - step) % size * NC + 1))
    return lax.ppermute(x, (axis, "core"), pairs)


def swap_cores(x):
    return shift(x, "core", NC, 1)


def pick_kernel(info, *refs):
    gathered, out = refs[:NY], refs[NY]
    counted, y = info[SLOTS], info[SLOTS + 1]
    for s in range(SLOTS):
        column = info[s]
        z_at, y_at = lax.div(column, NY), lax.rem(column, NY)
        from_y = lax.rem(y - y_at + NY, NY)
        rows = gathered[0][z_at]
        for d in range(1, NY):
            rows = jnp.where(from_y == d, gathered[d][z_at], rows)
        out[s] = jnp.where(s < counted, rows, jnp.zeros_like(rows))


def load_kernel(source, out, done):
    copy = pltpu.make_async_copy(source, out, done)
    copy.start()
    copy.wait()


def load(source):
    return pl.pallas_call(
        load_kernel,
        out_shape=jax.ShapeDtypeStruct(source.shape, source.dtype),
        in_specs=[pl.BlockSpec(memory_space=pl.ANY)],
        out_specs=VMEM,
        scratch_shapes=[pltpu.SemaphoreType.DMA],
        compiler_params=pltpu.CompilerParams(vmem_limit_bytes=LIMIT),
    )(source)


def half(core, integrals, mine, other):
    first = core[0] == 0
    left = jnp.concatenate(
        [integrals[s].reshape(ROWS, BLOCK) for s in range(SLOTS)], axis=1
    )
    parts = []
    for m, o in zip(mine, other):
        a, b = m[...], o[...]
        top, low = jnp.where(first, a, b), jnp.where(first, b, a)
        parts.append(jnp.concatenate([top, low], axis=1).reshape(SLOTS * BLOCK, SLICE))
    right = parts[0] if len(parts) == 1 else jnp.concatenate(parts, axis=1)
    return jnp.dot(left, right, preferred_element_type=jnp.float32).astype(jnp.bfloat16)


def half_kernel(core, integrals, *refs):
    out = refs[-1]
    done = half(core, integrals, refs[:NX], refs[NX:2 * NX])
    for p in range(AUX_HERE):
        at = slice(p % 2 * NOCC, (p % 2 + 1) * NOCC)
        out[p // 2, :, at] = done[p * BLOCK:(p + 1) * BLOCK]


def place_of(place, offset):
    z, core = place[0], place[2]
    at = lax.rem(z + offset + NZ, NZ)
    return lax.div(at, NC), lax.rem(lax.rem(at, NC) + core, NC)


def times(rows, columns):
    return lax.dot_general(
        rows, columns, (((1,), (1,)), ((), ())), preferred_element_type=jnp.float32
    )


def row_places(place):
    y, sign = place[1], 1 - 2 * place[2]
    return [y] + [lax.rem(y + d * sign + NY, NY) for d in (-1, 1, 2)]


def put(place, out, total, offsets):
    row_at = row_places(place)
    for n, offset in enumerate(offsets):
        x_at, side = place_of(place, offset)
        for r in range(NY):
            at = row_at[r] * NX + x_at
            out[side, at] = total[r * BLOCK:(r + 1) * BLOCK, n * BLOCK:(n + 1) * BLOCK]


def product(grows, blocks):
    total = None
    for h in range(2):
        rows = jnp.concatenate([g[h] for g in grows], axis=0)
        columns = [block[h][0] for block in blocks]
        columns = columns[0] if len(columns) == 1 else jnp.concatenate(columns, axis=0)
        term = times(rows, columns)
        total = term if total is None else total + term
    return total


def first_kernel(place, *refs):
    grows, out = refs[:4], refs[4]
    own = grows[0]
    put(place, out, product(grows, [(own.at[pl.ds(0, 1)], own.at[pl.ds(1, 1)])]), (0,))


def pair_kernel(k, place, *refs):
    grows, columns, out = refs[:4], refs[4:8], refs[9]
    put(place, out, product(grows, [columns[0:2], columns[2:4]]), (-k, k))


def last_kernel(place, *refs):
    grows, columns, out = refs[:4], refs[4:8], refs[9]
    total = None
    for h in range(2):
        rows = jnp.concatenate([g[h] for g in grows], axis=0)
        block = jnp.concatenate([columns[2 * h][0], columns[2 * h + 1][0]], axis=0)
        term = times(rows, block)
        total = term if total is None else total + term
    put(place, out, total, (4,))


def finish_kernel(parts, out):
    scale = 1.0 / math.sqrt(AUX_HERE * NX * NC * NOCC)
    for yy in range(NY):
        total = parts[yy * NX]
        for xx in range(1, NX):
            total = total + parts[yy * NX + xx]
        out[:, yy * BLOCK:(yy + 1) * BLOCK] = total * scale


def shards(pair_cols, pair_count, integrals, coeffs):
    z, y = lax.axis_index("z"), lax.axis_index("y")
    x, core = lax.axis_index("x"), lax.axis_index("core")
    core_at = core[None].astype(jnp.int32)
    place = jnp.stack([z, y, core]).astype(jnp.int32)

    info = jnp.concatenate([pair_cols[0], pair_count, y[None].astype(jnp.int32)])
    loaded = load(integrals)

    piece = lax.dynamic_slice(coeffs, (core * HALF_L, x * SLICE), (HALF_L, SLICE))
    along_z = lax.all_to_all(
        jnp.broadcast_to(piece[None], (NZ, HALF_L, SLICE)), "z", 0, 0, tiled=True
    )
    along_z, loaded, info = lax.optimization_barrier((along_z, loaded, info))
    gathered = [along_z] + [shift(along_z, "y", NY, d) for d in (1, 2, 3)]
    picked = call(
        pick_kernel, bf16(SLOTS, HALF_L, SLICE),
        [info], gathered,
    )
    slices = [picked] + [shift(picked, "x", NX, d) for d in (1, 3, 2)]
    halfway = call(
        half_kernel, bf16(2, BLOCK, 2 * CHUNK), [core_at], [loaded] + slices + [swap_cores(m) for m in slices]
    )
    halves = [lax.slice_in_dim(halfway, h, h + 1, axis=0) for h in range(2)]
    ups, downs = list(halves), list(halves)
    y_a, y_b = mirrored(halfway, "y", NY, 1), mirrored(halfway, "y", NY, -1)
    y_far = mirrored(y_a, "y", NY, 1)
    columns = []
    for step in range(3):
        for h in range(2):
            up, down = shift(ups[h], "z", NZ, 1), shift(downs[h], "z", NZ, -1)
            if h == 1 and step == 1:
                up, down, y_a, y_b = lax.optimization_barrier((up, down, y_a, y_b))
            ups[h], downs[h] = up, down
        columns.append([(ups[0], ups[1]), (downs[0], downs[1])])
    last = []
    for h in range(2):
        low = shift(ups[h][:, :BLOCK // 2], "z", NZ, 1)
        high = shift(downs[h][:, BLOCK // 2:], "z", NZ, -1)
        last.append((low, high))
    rows = [halfway, y_a, y_b, y_far]

    tiles = jax.ShapeDtypeStruct((NC, NY * NX, BLOCK, BLOCK), jnp.float32)
    tile = call(first_kernel, tiles, [place], rows, flops=270000000)
    for k in range(3):
        blocks = [half for pair in columns[k] for half in pair]
        tile = call(
            functools.partial(pair_kernel, k + 1), tiles, [place], rows + blocks + [tile],
            flops=540000000, aliases={9: 0},
        )
    blocks = [half for pair in last for half in pair]
    tile = call(last_kernel, tiles, [place], rows + blocks + [tile], aliases={9: 0})

    both = tile[0] + swap_cores(tile[1])
    parts = lax.all_to_all(both, ("y", "x"), 0, 0, tiled=True)
    return call(
        finish_kernel, jax.ShapeDtypeStruct((BLOCK, NY * BLOCK), jnp.float32), [], [parts]
    )


def solution(mesh):
    grid = Mesh(mesh.devices.reshape(NZ, NY, NX, NC), ("z", "y", "x", "core"))
    blk, aux = ("z", "y"), ("x", "core")
    placed = (P(blk, None), P(blk), P(blk, aux, None, None), P(blk, None))
    return jax.shard_map(
        shards, mesh=grid, in_specs=placed, out_specs=P(blk, aux), check_vma=False
    )
```

time: 370 us -> 122 us (0.33)
  waiting for transfers between devices: 303 us -> 31.5 us
  starting transfers between devices: 0.08 us -> 52.2 us
  matrix products: 21.7 us -> 0 us
  blocking collectives: 0 us -> 21.3 us
  loops' own time: 18.1 us -> 0 us
  between operations: 13.1 us -> 0.88 us
  other arithmetic: 11.4 us -> 0.29 us
  Pallas kernels: 0 us -> 9.98 us
  local copies, waits for them, and re-layouts: 0.11 us -> 5.75 us
    all_gather x2 -> x0, waiting for transfers between devices: 271 us -> none  [the longest x1 186 us: shards(): lax.all_gather(halfway, 'blk', axis=1, tiled=True)]
    ppermute x0 -> x30, starting transfers between devices: none -> 43.2 us  [the longest x27 38.9 us: shift(): return lax.ppermute(x, axis, [(i, (i + step) % size) for i in range(size)])]
    reduce_scatter x1 -> x0, waiting for transfers between devices: 31.1 us -> none  [shards(): lax.psum_scatter(partial_rows, 'aux', scatter_dimension=1, tiled=True)]
    ppermute x0 -> x30, waiting for transfers between devices: none -> 26.7 us  [the longest x27 26.7 us: shift(): return lax.ppermute(x, axis, [(i, (i + step) % size) for i in range(size)])]
    dot_general x8 -> x0, matrix products: 21.7 us -> none  [the longest x1 12.7 us: shards(): jnp.einsum('pmi,pni->mn', halfway, lax.all_gather(halfway, 'blk', axis=1,...]
    all_to_all x0 -> x1, blocking collectives: none -> 21.3 us  [shards(): parts = lax.all_to_all(both, ('y', 'x'), 0, 0, tiled=True)]
    another operation x1 -> x0, loops' own time: 18.1 us -> none  [shards(): halfway = lax.fori_loop(0, counted, add_pair, started).astype(jnp.bfloat16)]
    mul x8 -> x0, other arithmetic: 10.6 us -> none  [the longest x7 8.91 us: add_pair(): column * width]
  transfers between devices with their start and end apart: 3 -> 31, of which waited for: 3 -> 14; matrix products, arithmetic and copies ran while one was open for 0% -> 0% of each run, Pallas kernels for 0% -> 5%
where the time goes in v2:
time: 122 us
  starting transfers between devices  52.2 us (43%)
  waiting for transfers between devices  31.5 us (26%)
  blocking collectives  21.3 us (17%)
  Pallas kernels  9.98 us (8%)
  local copies, waits for them, and re-layouts  5.75 us (5%)
    ppermute x27, starting transfers between devices, shift(): return lax.ppermute(x, axis, [(i, (i + step) % size) for i in range(size)])  38.9 us
    ppermute x27, waiting for transfers between devices, shift(): return lax.ppermute(x, axis, [(i, (i + step) % size) for i in range(size)])  26.7 us
    all_to_all x1, blocking collectives, shards(): parts = lax.all_to_all(both, ('y', 'x'), 0, 0, tiled=True)  21.3 us
    pallas_call x8, Pallas kernels, call(): pl.pallas_call(body, out_shape=out_shape, in_specs=[SMEM] * len(scalars)...  9.83 us
    all_to_all x1, starting transfers between devices, shards(): lax.all_to_all(jnp.broadcast_to(piece[None], (NZ, HALF_L, SLICE)), 'z', 0...  9.01 us
    all_to_all x1, waiting for transfers between devices, shards(): lax.all_to_all(jnp.broadcast_to(piece[None], (NZ, HALF_L, SLICE)), 'z', 0...  4.79 us
    ppermute x3, starting transfers between devices, mirrored(): return lax.ppermute(x, (axis, 'core'), pairs)  4.28 us
    unnamed x16, local copies, waits for them, and re-layouts  4.2 us
  transfers between devices with their start and end apart: 31, of which 14 were waited for; matrix products, arithmetic and copies ran while one was open for 0% of the time, Pallas kernels for 5%

profile of v2, /device:TPU:1, one launch (start us, length us, event | category | flops | bytes accessed | tf_op | source)
XLA Modules:
  0.0 121.9 jit_solution(9829057875874998945)
XLA Ops:
  0.0 0.7 dynamic_slice.3
  0.7 0.7 broadcast_in_dim.2
  1.4 9.0 %all-to-all-start = ((bf16[8,64,128]{2,1,0:T(8,128)(2,1)}), bf16[8,64,128]{2,1,0:T(8,128)(2,1)S(1)}, u32[]{:S(2)}, u32[]{:S(2)}) async-start(bf16[8,64,128]{2,1,0:T(8,128)(2,1)} %broadcast_in_dim.2), calls=%async_computation | async-start | bytes 262144 | tf_op jit(solution)/shard_map/all_to_all | solution.py:184
  11.1 0.0 copy-start
  11.1 1.6 %copy-done = bf16[16,4,128,128]{3,2,1,0:T(8,128)(2,1)S(1)} copy-done((bf16[16,4,128,128]{3,2,1,0:T(8,128)(2,1)S(1)}, bf16[16,4,128,128]{3,2,1,0:T(8,128)(2,1)}, u32[]{:S(2)}) %copy-start) | copy-done | bytes 2097176
  12.7 0.1 shard_map.46.integrals
  12.8 0.5 copy-done.7
  13.3 0.1 pad_add_fusion.1.info
  13.4 4.8 %all-to-all-done.refs_0_ = bf16[8,64,128]{2,1,0:T(8,128)(2,1)S(1)} async-done(((bf16[8,64,128]{2,1,0:T(8,128)(2,1)}), bf16[8,64,128]{2,1,0:T(8,128)(2,1)S(1)}, u32[]{:S(2)}, u32[]{:S(2)}) %all-to-all-start) | async-done | bytes 131104 | tf_op jit(solution)/shard_map/all_to_all | solution.py:184
  18.2 1.3 %collective-permute-start = (bf16[8,64,128]{2,1,0:T(8,128)(2,1)S(1)}, bf16[8,64,128]{2,1,0:T(8,128)(2,1)S(1)}, u32[]{:S(2)}, u32[]{:S(2)}) collective-permute-start(bf16[8,64,128]{2,1,0:T(8,128)(2,1)S(1)} %all-to-all-done.refs_0_), channel_id=1, source_target_pairs={{0,8},{8,16},{16,24},{24,0},{1,9},{9,17},{17,25},{25,1},{2,10},{10... | collective-permute-start | bytes 393224 | tf_op jit(solution)/shard_map/ppermute | solution.py:39
  19.5 2.6 %collective-permute-start.1 = (bf16[8,64,128]{2,1,0:T(8,128)(2,1)S(1)}, bf16[8,64,128]{2,1,0:T(8,128)(2,1)S(1)}, u32[]{:S(2)}, u32[]{:S(2)}) collective-permute-start(bf16[8,64,128]{2,1,0:T(8,128)(2,1)S(1)} %all-to-all-done.refs_0_), channel_id=1, source_target_pairs={{0,16},{8,24},{16,0},{24,8},{1,17},{9,25},{17,1},{25,9},{2,18},{10... | collective-permute-start | bytes 393224 | tf_op jit(solution)/shard_map/ppermute | solution.py:39
  22.1 1.1 collective-permute-start.2
  23.2 0.1 collective-permute-done.refs_1_
  23.3 2.7 %collective-permute-done.1.refs_2_ = bf16[8,64,128]{2,1,0:T(8,128)(2,1)S(1)} collective-permute-done((bf16[8,64,128]{2,1,0:T(8,128)(2,1)S(1)}, bf16[8,64,128]{2,1,0:T(8,128)(2,1)S(1)}, u32[]{:S(2)}, u32[]{:S(2)}) %collective-permute-start.1) | collective-permute-done | bytes 131104 | tf_op jit(solution)/shard_map/ppermute | solution.py:39
  26.0 0.8 collective-permute-done.2.refs_3_
  26.7 0.7 shard_map.47.refs_0_
  27.5 1.3 %collective-permute-start.3 = (bf16[16,64,128]{2,1,0:T(8,128)(2,1)S(1)}, bf16[16,64,128]{2,1,0:T(8,128)(2,1)S(1)}, u32[]{:S(2)}, u32[]{:S(2)}) collective-permute-start(bf16[16,64,128]{2,1,0:T(8,128)(2,1)S(1)} %shard_map.47.refs_0_), channel_id=1, source_target_pairs={{0,2},{2,4},{4,6},{6,0},{1,3},{3,5},{5,7},{7,1},{8,10},{10,12},{12... | collective-permute-start | bytes 786440 | tf_op jit(solution)/shard_map/ppermute | solution.py:39
  28.8 1.5 %collective-permute-start.4 = (bf16[16,64,128]{2,1,0:T(8,128)(2,1)S(1)}, bf16[16,64,128]{2,1,0:T(8,128)(2,1)S(1)}, u32[]{:S(2)}, u32[]{:S(2)}) collective-permute-start(bf16[16,64,128]{2,1,0:T(8,128)(2,1)S(1)} %shard_map.47.refs_0_), channel_id=1, source_target_pairs={{0,6},{2,0},{4,2},{6,4},{1,7},{3,1},{5,3},{7,5},{8,14},{10,8},{12,... | collective-permute-start | bytes 786440 | tf_op jit(solution)/shard_map/ppermute | solution.py:39
  30.2 1.5 %collective-permute-start.5 = (bf16[16,64,128]{2,1,0:T(8,128)(2,1)S(1)}, bf16[16,64,128]{2,1,0:T(8,128)(2,1)S(1)}, u32[]{:S(2)}, u32[]{:S(2)}) collective-permute-start(bf16[16,64,128]{2,1,0:T(8,128)(2,1)S(1)} %shard_map.47.refs_0_), channel_id=1, source_target_pairs={{0,4},{2,6},{4,0},{6,2},{1,5},{3,7},{5,1},{7,3},{8,12},{10,14},{12... | collective-permute-start | bytes 786440 | tf_op jit(solution)/shard_map/ppermute | solution.py:39
  31.8 4.0 %collective-permute-start.6 = (bf16[16,64,128]{2,1,0:T(8,128)(2,1)S(1)}, bf16[16,64,128]{2,1,0:T(8,128)(2,1)S(1)}, u32[]{:S(2)}, u32[]{:S(2)}) collective-permute-start(bf16[16,64,128]{2,1,0:T(8,128)(2,1)S(1)} %shard_map.47.refs_0_), channel_id=1, source_target_pairs={{0,1},{1,0},{2,3},{3,2},{4,5},{5,4},{6,7},{7,6},{8,9},{9,8},{10,11... | collective-permute-start | bytes 786440 | tf_op jit(solution)/shard_map/ppermute | solution.py:39
  35.8 5.3 %collective-permute-start.7 = (bf16[16,64,128]{2,1,0:T(8,128)(2,1)S(1)}, bf16[16,64,128]{2,1,0:T(8,128)(2,1)S(1)}, u32[]{:S(2)}, u32[]{:S(2)}) collective-permute-start(bf16[16,64,128]{2,1,0:T(8,128)(2,1)S(1)} %collective-permute-done.3.refs_1_), channel_id=1, source_target_pairs={{0,1},{1,0},{2,3},{3,2},{4,5},{5,4},{6,7},{7,6},{8,9},{9,8},{10,11... | collective-permute-start | bytes 786440 | tf_op jit(solution)/shard_map/ppermute | solution.py:39
  41.1 0.0 collective-permute-start.8
  41.1 3.0 %collective-permute-start.9 = (bf16[16,64,128]{2,1,0:T(8,128)(2,1)S(1)}, bf16[16,64,128]{2,1,0:T(8,128)(2,1)S(1)}, u32[]{:S(2)}, u32[]{:S(2)}) collective-permute-start(bf16[16,64,128]{2,1,0:T(8,128)(2,1)S(1)} %collective-permute-done.5.refs_3_), channel_id=1, source_target_pairs={{0,1},{1,0},{2,3},{3,2},{4,5},{5,4},{6,7},{7,6},{8,9},{9,8},{10,11... | collective-permute-start | bytes 786440 | tf_op jit(solution)/shard_map/ppermute | solution.py:39
  44.1 1.1 collective-permute-done.9.refs_7_
  45.2 1.3 %shard_map.48.refs_0_ = bf16[2,128,1024]{2,1,0:T(8,128)(2,1)S(1)} custom-call(s32[1]{0:T(128)} %bitcast.2.core, bf16[16,4,128,128]{3,2,1,0:T(8,128)(2,1)S(1)} %shard_map.46.integrals, bf16[16,64,128]{2,1,0:T(8,128)(2,1)S(1)} %shard_map.47.refs_0_, bf16[16,64,128]{2,1,0:T(8,128)(2,1)S(1)} %collective-permute-done.3.refs_1_, ...), custom_call_target="tpu_custom_call" | custom-call | tf_op jit(solution)/shard_map/pallas_call | solution.py:23
  46.6 0.9 collective-permute-start.10
  47.5 1.8 %collective-permute-start.12 = (bf16[1,128,1024]{2,1,0:T(8,128)(2,1)S(1)}, bf16[1,128,1024]{2,1,0:T(8,128)(2,1)S(1)}, u32[]{:S(2)}, u32[]{:S(2)}) collective-permute-start(bf16[1,128,1024]{2,1,0:T(8,128)(2,1)S(1)} %get-tuple-element.20), channel_id=1, source_target_pairs={{0,224},{32,0},{64,32},{96,64},{128,96},{160,128},{192,160},{224,1... | collective-permute-start | bytes 786440 | tf_op jit(solution)/shard_map/ppermute | solution.py:39
  49.4 2.2 %collective-permute-start.14 = (bf16[2,128,1024]{2,1,0:T(8,128)(2,1)S(1)}, bf16[2,128,1024]{2,1,0:T(8,128)(2,1)S(1)}, u32[]{:S(2)}, u32[]{:S(2)}) collective-permute-start(bf16[2,128,1024]{2,1,0:T(8,128)(2,1)S(1)} %shard_map.48.refs_0_), channel_id=1, source_target_pairs={{0,8},{1,25},{8,16},{9,1},{16,24},{17,9},{24,0},{25,17},{2,10},{3,... | collective-permute-start | bytes 1572872 | tf_op jit(solution)/shard_map/ppermute | solution.py:47
  51.6 3.8 %collective-permute-done.10.refs_5_ = bf16[1,128,1024]{2,1,0:T(8,128)(2,1)S(1)} collective-permute-done((bf16[1,128,1024]{2,1,0:T(8,128)(2,1)S(1)}, bf16[1,128,1024]{2,1,0:T(8,128)(2,1)S(1)}, u32[]{:S(2)}, u32[]{:S(2)}) %collective-permute-start.10) | collective-permute-done | bytes 262176 | tf_op jit(solution)/shard_map/ppermute | solution.py:39
  55.4 0.0 collective-permute-start.21
  55.4 1.5 %collective-permute-start.11 = (bf16[1,128,1024]{2,1,0:T(8,128)(2,1)S(1)}, bf16[1,128,1024]{2,1,0:T(8,128)(2,1)}, u32[]{:S(2)}, u32[]{:S(2)}) collective-permute-start(bf16[1,128,1024]{2,1,0:T(8,128)(2,1)S(1)} %collective-permute-done.10.refs_5_), channel_id=1, source_target_pairs={{0,32},{32,64},{64,96},{96,128},{128,160},{160,192},{192,224},{224... | collective-permute-start | bytes 786440 | tf_op jit(solution)/shard_map/ppermute | solution.py:39
  56.9 4.3 %collective-permute-done.17.refs_4_ = bf16[1,128,1024]{2,1,0:T(8,128)(2,1)S(1)} collective-permute-done((bf16[1,128,1024]{2,1,0:T(8,128)(2,1)S(1)}, bf16[1,128,1024]{2,1,0:T(8,128)(2,1)S(1)}, u32[]{:S(2)}, u32[]{:S(2)}) %collective-permute-start.17) | collective-permute-done | bytes 262176 | tf_op jit(solution)/shard_map/ppermute | solution.py:39
  61.2 0.7 copy-done.1
  61.9 1.5 %collective-permute-start.18 = (bf16[1,128,1024]{2,1,0:T(8,128)(2,1)S(1)}, bf16[1,128,1024]{2,1,0:T(8,128)(2,1)}, u32[]{:S(2)}, u32[]{:S(2)}) collective-permute-start(bf16[1,128,1024]{2,1,0:T(8,128)(2,1)S(1)} %collective-permute-done.17.refs_4_), channel_id=1, source_target_pairs={{0,32},{32,64},{64,96},{96,128},{128,160},{160,192},{192,224},{224... | collective-permute-start | bytes 786440 | tf_op jit(solution)/shard_map/ppermute | solution.py:39
  63.3 0.7 copy-done.3
  64.0 2.9 %collective-permute-done.11.refs_5_ = bf16[1,128,1024]{2,1,0:T(8,128)(2,1)} collective-permute-done((bf16[1,128,1024]{2,1,0:T(8,128)(2,1)S(1)}, bf16[1,128,1024]{2,1,0:T(8,128)(2,1)}, u32[]{:S(2)}, u32[]{:S(2)}) %collective-permute-start.11) | collective-permute-done | bytes 262176 | tf_op jit(solution)/shard_map/ppermute | solution.py:39
  66.9 0.7 copy-done.5
  67.6 2.1 %collective-permute-start.16 = (bf16[2,128,1024]{2,1,0:T(8,128)(2,1)S(1)}, bf16[2,128,1024]{2,1,0:T(8,128)(2,1)S(1)}, u32[]{:S(2)}, u32[]{:S(2)}) collective-permute-start(bf16[2,128,1024]{2,1,0:T(8,128)(2,1)S(1)} %collective-permute-done.14.refs_1_), channel_id=1, source_target_pairs={{0,8},{1,25},{8,16},{9,1},{16,24},{17,9},{24,0},{25,17},{2,10},{3,... | collective-permute-start | bytes 1572872 | tf_op jit(solution)/shard_map/ppermute | solution.py:47
  69.7 1.5 %collective-permute-start.25 = (bf16[1,128,1024]{2,1,0:T(8,128)(2,1)}, bf16[1,128,1024]{2,1,0:T(8,128)(2,1)S(1)}, u32[]{:S(2)}, u32[]{:S(2)}) collective-permute-start(bf16[1,128,1024]{2,1,0:T(8,128)(2,1)} %collective-permute-done.11.refs_5_), channel_id=1, source_target_pairs={{0,32},{32,64},{64,96},{96,128},{128,160},{160,192},{192,224},{224... | collective-permute-start | bytes 786440 | tf_op jit(solution)/shard_map/ppermute | solution.py:39
  71.1 1.2 collective-permute-start.27
  72.4 0.3 collective-permute-start.19
  72.6 0.4 collective-permute-done.22.refs_6_
  73.1 2.0 %collective-permute-start.23 = (bf16[1,128,1024]{2,1,0:T(8,128)(2,1)}, bf16[1,128,1024]{2,1,0:T(8,128)(2,1)S(1)}, u32[]{:S(2)}, u32[]{:S(2)}) collective-permute-start(bf16[1,128,1024]{2,1,0:T(8,128)(2,1)} %collective-permute-done.22.refs_6_), channel_id=1, source_target_pairs={{0,224},{32,0},{64,32},{96,64},{128,96},{160,128},{192,160},{224,1... | collective-permute-start | bytes 786440 | tf_op jit(solution)/shard_map/ppermute | solution.py:39
  75.0 0.1 pad_add_fusion.place
  75.1 3.3 %collective-permute-done.25.refs_5_ = bf16[1,128,1024]{2,1,0:T(8,128)(2,1)S(1)} collective-permute-done((bf16[1,128,1024]{2,1,0:T(8,128)(2,1)}, bf16[1,128,1024]{2,1,0:T(8,128)(2,1)S(1)}, u32[]{:S(2)}, u32[]{:S(2)}) %collective-permute-start.25) | collective-permute-done | bytes 262176 | tf_op jit(solution)/shard_map/ppermute | solution.py:39
  78.5 0.2 collective-permute-start.26
  78.7 1.1 collective-permute-done.27.refs_7_
  79.8 1.6 %collective-permute-start.28 = (bf16[1,64,1024]{2,1,0:T(8,128)(2,1)S(1)}, bf16[1,64,1024]{2,1,0:T(8,128)(2,1)S(1)}, u32[]{:S(2)}, u32[]{:S(2)}) collective-permute-start(bf16[1,64,1024]{2,1,0:T(8,128)(2,1)S(1)} %slice.37), channel_id=1, source_target_pairs={{0,224},{32,0},{64,32},{96,64},{128,96},{160,128},{192,160},{224,1... | collective-permute-start | bytes 393224 | tf_op jit(solution)/shard_map/ppermute | solution.py:39
  81.3 2.8 %collective-permute-done.19.refs_4_ = bf16[1,128,1024]{2,1,0:T(8,128)(2,1)S(1)} collective-permute-done((bf16[1,128,1024]{2,1,0:T(8,128)(2,1)}, bf16[1,128,1024]{2,1,0:T(8,128)(2,1)S(1)}, u32[]{:S(2)}, u32[]{:S(2)}) %collective-permute-start.19) | collective-permute-done | bytes 262176 | tf_op jit(solution)/shard_map/ppermute | solution.py:39
  84.1 0.2 collective-permute-start.20
  84.3 1.1 collective-permute-done.23.refs_6_
  85.4 0.0 copy-start.4
  85.4 1.8 %collective-permute-start.24 = (bf16[1,64,1024]{2,1,0:T(8,128)(2,1)S(1)}, bf16[1,64,1024]{2,1,0:T(8,128)(2,1)S(1)}, u32[]{:S(2)}, u32[]{:S(2)}) collective-permute-start(bf16[1,64,1024]{2,1,0:T(8,128)(2,1)S(1)} %slice.35), channel_id=1, source_target_pairs={{0,224},{32,0},{64,32},{96,64},{128,96},{160,128},{192,160},{224,1... | collective-permute-start | bytes 393224 | tf_op jit(solution)/shard_map/ppermute | solution.py:39
  87.2 1.2 %shard_map.49.refs_8_ = f32[2,16,128,128]{3,2,1,0:T(8,128)S(1)} custom-call(s32[3]{0:T(128)S(1)} %pad_add_fusion.place, bf16[2,128,1024]{2,1,0:T(8,128)(2,1)S(1)} %shard_map.48.refs_0_, bf16[2,128,1024]{2,1,0:T(8,128)(2,1)S(1)} %collective-permute-done.14.refs_1_, bf16[2,128,1024]{2,1,0:T(8,128)(2,1)S(1)} %collective-permute-done.15.refs_2_, ...), custom_call_target="tpu_custom_call" | custom-call | flops 270000000 | bytes 12000000 | tf_op jit(solution)/shard_map/pallas_call | solution.py:23
  88.5 1.3 %shard_map.50.refs_8_ = f32[2,16,128,128]{3,2,1,0:T(8,128)S(1)} custom-call(s32[3]{0:T(128)S(1)} %pad_add_fusion.place, bf16[2,128,1024]{2,1,0:T(8,128)(2,1)S(1)} %shard_map.48.refs_0_, bf16[2,128,1024]{2,1,0:T(8,128)(2,1)S(1)} %collective-permute-done.14.refs_1_, ...), custom_call_target="tpu_custom_call", output_to_operand_aliasing={{}: (9, {})} | custom-call | flops 540000000 | bytes 12000000 | tf_op jit(solution)/shard_map/pallas_call | solution.py:23
  89.8 2.0 %shard_map.51.refs_8_ = f32[2,16,128,128]{3,2,1,0:T(8,128)S(1)} custom-call(s32[3]{0:T(128)S(1)} %pad_add_fusion.place, bf16[2,128,1024]{2,1,0:T(8,128)(2,1)S(1)} %shard_map.48.refs_0_, bf16[2,128,1024]{2,1,0:T(8,128)(2,1)S(1)} %collective-permute-done.14.refs_1_, ...), custom_call_target="tpu_custom_call", output_to_operand_aliasing={{}: (9, {})} | custom-call | flops 540000000 | bytes 12000000 | tf_op jit(solution)/shard_map/pallas_call | solution.py:23
  91.7 1.3 %shard_map.52.refs_8_ = f32[2,16,128,128]{3,2,1,0:T(8,128)S(1)} custom-call(s32[3]{0:T(128)S(1)} %pad_add_fusion.place, bf16[2,128,1024]{2,1,0:T(8,128)(2,1)S(1)} %shard_map.48.refs_0_, bf16[2,128,1024]{2,1,0:T(8,128)(2,1)S(1)} %collective-permute-done.14.refs_1_, ...), custom_call_target="tpu_custom_call", output_to_operand_aliasing={{}: (9, {})} | custom-call | flops 540000000 | bytes 12000000 | tf_op jit(solution)/shard_map/pallas_call | solution.py:23
  93.1 1.2 %shard_map.53 = f32[2,16,128,128]{3,2,1,0:T(8,128)S(1)} custom-call(s32[3]{0:T(128)S(1)} %pad_add_fusion.place, bf16[2,128,1024]{2,1,0:T(8,128)(2,1)S(1)} %shard_map.48.refs_0_, bf16[2,128,1024]{2,1,0:T(8,128)(2,1)S(1)} %collective-permute-done.14.refs_1_, bf16[2,128,1024]{2,1,0:T(8,128)(2,1)S(1)} %collective-permute-done.15.refs_2_, ...), custom_call_target="tpu_custom_call", output_to_operand_aliasing={{}: (9, {})} | custom-call | tf_op jit(solution)/shard_map/pallas_call | solution.py:23
  94.3 0.1 slice_bitcast_fusion
  94.4 3.0 %collective-permute-start.29 = (f32[16,128,128]{2,1,0:T(8,128)S(1)}, f32[16,128,128]{2,1,0:T(8,128)S(1)}, u32[]{:S(2)}, u32[]{:S(2)}) collective-permute-start(f32[16,128,128]{2,1,0:T(8,128)S(1)} %slice_bitcast_fusion), channel_id=1, source_target_pairs={{0,1},{1,0},{2,3},{3,2},{4,5},{5,4},{6,7},{7,6},{8,9},{9,8},{10,11... | collective-permute-start | bytes 3145736 | tf_op jit(solution)/shard_map/ppermute | solution.py:39
  97.4 2.3 %collective-permute-done.29 = f32[16,128,128]{2,1,0:T(8,128)S(1)} collective-permute-done((f32[16,128,128]{2,1,0:T(8,128)S(1)}, f32[16,128,128]{2,1,0:T(8,128)S(1)}, u32[]{:S(2)}, u32[]{:S(2)}) %collective-permute-start.29) | collective-permute-done | bytes 1048608 | tf_op jit(solution)/shard_map/ppermute | solution.py:39
  99.7 0.1 fusion
  99.8 21.3 %all_to_all.10.parts = f32[16,128,128]{2,1,0:T(8,128)S(1)} all-to-all(f32[16,128,128]{2,1,0:T(8,128)S(1)} %fusion), channel_id=1, replica_groups=mesh['z'=8,'y'=4,'x'=4,'core'=2] {'y','x'}, dimensions={0} | all-to-all | bytes 2097152 | tf_op jit(solution)/shard_map/all_to_all | solution.py:228
  121.2 0.8 shard_map.54
  (35 shorter events, 0.1 us)
Async XLA Ops:
  1.4 16.8 %all-to-all-start = ((bf16[8,64,128]{2,1,0:T(8,128)(2,1)}), bf16[8,64,128]{2,1,0:T(8,128)(2,1)S(1)}, u32[]{:S(2)}, u32[]{:S(2)}) async-start(bf16[8,64,128]{2,1,0:T(8,128)(2,1)} %broadcast_in_dim.2), calls=%async_computation | async-start | bytes 262144 | tf_op jit(solution)/shard_map/all_to_all | solution.py:184
  11.1 1.6 %copy-start = (bf16[16,4,128,128]{3,2,1,0:T(8,128)(2,1)S(1)}, bf16[16,4,128,128]{3,2,1,0:T(8,128)(2,1)}, u32[]{:S(2)}) copy-start(bf16[16,4,128,128]{3,2,1,0:T(8,128)(2,1)} %source.1) | copy-start | bytes 6291460
  12.7 0.7 copy-start.7
  18.2 5.1 %collective-permute-start = (bf16[8,64,128]{2,1,0:T(8,128)(2,1)S(1)}, bf16[8,64,128]{2,1,0:T(8,128)(2,1)S(1)}, u32[]{:S(2)}, u32[]{:S(2)}) collective-permute-start(bf16[8,64,128]{2,1,0:T(8,128)(2,1)S(1)} %all-to-all-done.refs_0_), channel_id=1, source_target_pairs={{0,8},{8,16},{16,24},{24,0},{1,9},{9,17},{17,25},{25,1},{2,10},{10... | collective-permute-start | bytes 393224 | tf_op jit(solution)/shard_map/ppermute | solution.py:39
  19.5 6.5 %collective-permute-start.1 = (bf16[8,64,128]{2,1,0:T(8,128)(2,1)S(1)}, bf16[8,64,128]{2,1,0:T(8,128)(2,1)S(1)}, u32[]{:S(2)}, u32[]{:S(2)}) collective-permute-start(bf16[8,64,128]{2,1,0:T(8,128)(2,1)S(1)} %all-to-all-done.refs_0_), channel_id=1, source_target_pairs={{0,16},{8,24},{16,0},{24,8},{1,17},{9,25},{17,1},{25,9},{2,18},{10... | collective-permute-start | bytes 393224 | tf_op jit(solution)/shard_map/ppermute | solution.py:39
  22.1 4.6 %collective-permute-start.2 = (bf16[8,64,128]{2,1,0:T(8,128)(2,1)S(1)}, bf16[8,64,128]{2,1,0:T(8,128)(2,1)S(1)}, u32[]{:S(2)}, u32[]{:S(2)}) collective-permute-start(bf16[8,64,128]{2,1,0:T(8,128)(2,1)S(1)} %all-to-all-done.refs_0_), channel_id=1, source_target_pairs={{0,24},{8,0},{16,8},{24,16},{1,25},{9,1},{17,9},{25,17},{2,26},{10... | collective-permute-start | bytes 393224 | tf_op jit(solution)/shard_map/ppermute | solution.py:39
  27.5 8.3 %collective-permute-start.3 = (bf16[16,64,128]{2,1,0:T(8,128)(2,1)S(1)}, bf16[16,64,128]{2,1,0:T(8,128)(2,1)S(1)}, u32[]{:S(2)}, u32[]{:S(2)}) collective-permute-start(bf16[16,64,128]{2,1,0:T(8,128)(2,1)S(1)} %shard_map.47.refs_0_), channel_id=1, source_target_pairs={{0,2},{2,4},{4,6},{6,0},{1,3},{3,5},{5,7},{7,1},{8,10},{10,12},{12... | collective-permute-start | bytes 786440 | tf_op jit(solution)/shard_map/ppermute | solution.py:39
  28.8 12.4 %collective-permute-start.4 = (bf16[16,64,128]{2,1,0:T(8,128)(2,1)S(1)}, bf16[16,64,128]{2,1,0:T(8,128)(2,1)S(1)}, u32[]{:S(2)}, u32[]{:S(2)}) collective-permute-start(bf16[16,64,128]{2,1,0:T(8,128)(2,1)S(1)} %shard_map.47.refs_0_), channel_id=1, source_target_pairs={{0,6},{2,0},{4,2},{6,4},{1,7},{3,1},{5,3},{7,5},{8,14},{10,8},{12,... | collective-permute-start | bytes 786440 | tf_op jit(solution)/shard_map/ppermute | solution.py:39
  30.2 10.9 %collective-permute-start.5 = (bf16[16,64,128]{2,1,0:T(8,128)(2,1)S(1)}, bf16[16,64,128]{2,1,0:T(8,128)(2,1)S(1)}, u32[]{:S(2)}, u32[]{:S(2)}) collective-permute-start(bf16[16,64,128]{2,1,0:T(8,128)(2,1)S(1)} %shard_map.47.refs_0_), channel_id=1, source_target_pairs={{0,4},{2,6},{4,0},{6,2},{1,5},{3,7},{5,1},{7,3},{8,12},{10,14},{12... | collective-permute-start | bytes 786440 | tf_op jit(solution)/shard_map/ppermute | solution.py:39
  31.8 12.3 %collective-permute-start.6 = (bf16[16,64,128]{2,1,0:T(8,128)(2,1)S(1)}, bf16[16,64,128]{2,1,0:T(8,128)(2,1)S(1)}, u32[]{:S(2)}, u32[]{:S(2)}) collective-permute-start(bf16[16,64,128]{2,1,0:T(8,128)(2,1)S(1)} %shard_map.47.refs_0_), channel_id=1, source_target_pairs={{0,1},{1,0},{2,3},{3,2},{4,5},{5,4},{6,7},{7,6},{8,9},{9,8},{10,11... | collective-permute-start | bytes 786440 | tf_op jit(solution)/shard_map/ppermute | solution.py:39
  35.8 8.3 %collective-permute-start.7 = (bf16[16,64,128]{2,1,0:T(8,128)(2,1)S(1)}, bf16[16,64,128]{2,1,0:T(8,128)(2,1)S(1)}, u32[]{:S(2)}, u32[]{:S(2)}) collective-permute-start(bf16[16,64,128]{2,1,0:T(8,128)(2,1)S(1)} %collective-permute-done.3.refs_1_), channel_id=1, source_target_pairs={{0,1},{1,0},{2,3},{3,2},{4,5},{5,4},{6,7},{7,6},{8,9},{9,8},{10,11... | collective-permute-start | bytes 786440 | tf_op jit(solution)/shard_map/ppermute | solution.py:39
  41.1 3.0 %collective-permute-start.8 = (bf16[16,64,128]{2,1,0:T(8,128)(2,1)S(1)}, bf16[16,64,128]{2,1,0:T(8,128)(2,1)S(1)}, u32[]{:S(2)}, u32[]{:S(2)}) collective-permute-start(bf16[16,64,128]{2,1,0:T(8,128)(2,1)S(1)} %collective-permute-done.4.refs_2_), channel_id=1, source_target_pairs={{0,1},{1,0},{2,3},{3,2},{4,5},{5,4},{6,7},{7,6},{8,9},{9,8},{10,11... | collective-permute-start | bytes 786440 | tf_op jit(solution)/shard_map/ppermute | solution.py:39
  41.1 4.1 %collective-permute-start.9 = (bf16[16,64,128]{2,1,0:T(8,128)(2,1)S(1)}, bf16[16,64,128]{2,1,0:T(8,128)(2,1)S(1)}, u32[]{:S(2)}, u32[]{:S(2)}) collective-permute-start(bf16[16,64,128]{2,1,0:T(8,128)(2,1)S(1)} %collective-permute-done.5.refs_3_), channel_id=1, source_target_pairs={{0,1},{1,0},{2,3},{3,2},{4,5},{5,4},{6,7},{7,6},{8,9},{9,8},{10,11... | collective-permute-start | bytes 786440 | tf_op jit(solution)/shard_map/ppermute | solution.py:39
  46.6 8.8 %collective-permute-start.10 = (bf16[1,128,1024]{2,1,0:T(8,128)(2,1)S(1)}, bf16[1,128,1024]{2,1,0:T(8,128)(2,1)S(1)}, u32[]{:S(2)}, u32[]{:S(2)}) collective-permute-start(bf16[1,128,1024]{2,1,0:T(8,128)(2,1)S(1)} %get-tuple-element.20), channel_id=1, source_target_pairs={{0,32},{32,64},{64,96},{96,128},{128,160},{160,192},{192,224},{224... | collective-permute-start | bytes 786440 | tf_op jit(solution)/shard_map/ppermute | solution.py:39
  47.5 7.9 %collective-permute-start.12 = (bf16[1,128,1024]{2,1,0:T(8,128)(2,1)S(1)}, bf16[1,128,1024]{2,1,0:T(8,128)(2,1)S(1)}, u32[]{:S(2)}, u32[]{:S(2)}) collective-permute-start(bf16[1,128,1024]{2,1,0:T(8,128)(2,1)S(1)} %get-tuple-element.20), channel_id=1, source_target_pairs={{0,224},{32,0},{64,32},{96,64},{128,96},{160,128},{192,160},{224,1... | collective-permute-start | bytes 786440 | tf_op jit(solution)/shard_map/ppermute | solution.py:39
  49.4 18.3 %collective-permute-start.14 = (bf16[2,128,1024]{2,1,0:T(8,128)(2,1)S(1)}, bf16[2,128,1024]{2,1,0:T(8,128)(2,1)S(1)}, u32[]{:S(2)}, u32[]{:S(2)}) collective-permute-start(bf16[2,128,1024]{2,1,0:T(8,128)(2,1)S(1)} %shard_map.48.refs_0_), channel_id=1, source_target_pairs={{0,8},{1,25},{8,16},{9,1},{16,24},{17,9},{24,0},{25,17},{2,10},{3,... | collective-permute-start | bytes 1572872 | tf_op jit(solution)/shard_map/ppermute | solution.py:47
  51.6 9.6 %collective-permute-start.17 = (bf16[1,128,1024]{2,1,0:T(8,128)(2,1)S(1)}, bf16[1,128,1024]{2,1,0:T(8,128)(2,1)S(1)}, u32[]{:S(2)}, u32[]{:S(2)}) collective-permute-start(bf16[1,128,1024]{2,1,0:T(8,128)(2,1)S(1)} %get-tuple-element.19), channel_id=1, source_target_pairs={{0,32},{32,64},{64,96},{96,128},{128,160},{160,192},{192,224},{224... | collective-permute-start | bytes 786440 | tf_op jit(solution)/shard_map/ppermute | solution.py:39
  51.6 18.1 %collective-permute-start.15 = (bf16[2,128,1024]{2,1,0:T(8,128)(2,1)S(1)}, bf16[2,128,1024]{2,1,0:T(8,128)(2,1)S(1)}, u32[]{:S(2)}, u32[]{:S(2)}) collective-permute-start(bf16[2,128,1024]{2,1,0:T(8,128)(2,1)S(1)} %shard_map.48.refs_0_), channel_id=1, source_target_pairs={{0,24},{1,9},{8,0},{9,17},{16,8},{17,25},{24,16},{25,1},{2,26},{3,... | collective-permute-start | bytes 1572872 | tf_op jit(solution)/shard_map/ppermute | solution.py:47
  55.4 6.5 %collective-permute-start.21 = (bf16[1,128,1024]{2,1,0:T(8,128)(2,1)S(1)}, bf16[1,128,1024]{2,1,0:T(8,128)(2,1)S(1)}, u32[]{:S(2)}, u32[]{:S(2)}) collective-permute-start(bf16[1,128,1024]{2,1,0:T(8,128)(2,1)S(1)} %get-tuple-element.19), channel_id=1, source_target_pairs={{0,224},{32,0},{64,32},{96,64},{128,96},{160,128},{192,160},{224,1... | collective-permute-start | bytes 786440 | tf_op jit(solution)/shard_map/ppermute | solution.py:39
  55.4 11.5 %collective-permute-start.11 = (bf16[1,128,1024]{2,1,0:T(8,128)(2,1)S(1)}, bf16[1,128,1024]{2,1,0:T(8,128)(2,1)}, u32[]{:S(2)}, u32[]{:S(2)}) collective-permute-start(bf16[1,128,1024]{2,1,0:T(8,128)(2,1)S(1)} %collective-permute-done.10.refs_5_), channel_id=1, source_target_pairs={{0,32},{32,64},{64,96},{96,128},{128,160},{160,192},{192,224},{224... | collective-permute-start | bytes 786440 | tf_op jit(solution)/shard_map/ppermute | solution.py:39
  61.2 8.5 %collective-permute-start.13 = (bf16[1,128,1024]{2,1,0:T(8,128)(2,1)S(1)}, bf16[1,128,1024]{2,1,0:T(8,128)(2,1)}, u32[]{:S(2)}, u32[]{:S(2)}) collective-permute-start(bf16[1,128,1024]{2,1,0:T(8,128)(2,1)S(1)} %collective-permute-done.12.refs_7_), channel_id=1, source_target_pairs={{0,224},{32,0},{64,32},{96,64},{128,96},{160,128},{192,160},{224,1... | collective-permute-start | bytes 786440 | tf_op jit(solution)/shard_map/ppermute | solution.py:39
  61.2 0.7 copy-start.1
  61.9 10.5 %collective-permute-start.18 = (bf16[1,128,1024]{2,1,0:T(8,128)(2,1)S(1)}, bf16[1,128,1024]{2,1,0:T(8,128)(2,1)}, u32[]{:S(2)}, u32[]{:S(2)}) collective-permute-start(bf16[1,128,1024]{2,1,0:T(8,128)(2,1)S(1)} %collective-permute-done.17.refs_4_), channel_id=1, source_target_pairs={{0,32},{32,64},{64,96},{96,128},{128,160},{160,192},{192,224},{224... | collective-permute-start | bytes 786440 | tf_op jit(solution)/shard_map/ppermute | solution.py:39
  63.3 0.7 copy-start.3
  66.9 6.2 %collective-permute-start.22 = (bf16[1,128,1024]{2,1,0:T(8,128)(2,1)S(1)}, bf16[1,128,1024]{2,1,0:T(8,128)(2,1)}, u32[]{:S(2)}, u32[]{:S(2)}) collective-permute-start(bf16[1,128,1024]{2,1,0:T(8,128)(2,1)S(1)} %collective-permute-done.21.refs_6_), channel_id=1, source_target_pairs={{0,224},{32,0},{64,32},{96,64},{128,96},{160,128},{192,160},{224,1... | collective-permute-start | bytes 786440 | tf_op jit(solution)/shard_map/ppermute | solution.py:39
  66.9 0.7 copy-start.5
  67.6 19.6 %collective-permute-start.16 = (bf16[2,128,1024]{2,1,0:T(8,128)(2,1)S(1)}, bf16[2,128,1024]{2,1,0:T(8,128)(2,1)S(1)}, u32[]{:S(2)}, u32[]{:S(2)}) collective-permute-start(bf16[2,128,1024]{2,1,0:T(8,128)(2,1)S(1)} %collective-permute-done.14.refs_1_), channel_id=1, source_target_pairs={{0,8},{1,25},{8,16},{9,1},{16,24},{17,9},{24,0},{25,17},{2,10},{3,... | collective-permute-start | bytes 1572872 | tf_op jit(solution)/shard_map/ppermute | solution.py:47
  69.7 8.8 %collective-permute-start.25 = (bf16[1,128,1024]{2,1,0:T(8,128)(2,1)}, bf16[1,128,1024]{2,1,0:T(8,128)(2,1)S(1)}, u32[]{:S(2)}, u32[]{:S(2)}) collective-permute-start(bf16[1,128,1024]{2,1,0:T(8,128)(2,1)} %collective-permute-done.11.refs_5_), channel_id=1, source_target_pairs={{0,32},{32,64},{64,96},{96,128},{128,160},{160,192},{192,224},{224... | collective-permute-start | bytes 786440 | tf_op jit(solution)/shard_map/ppermute | solution.py:39
  71.1 8.6 %collective-permute-start.27 = (bf16[1,128,1024]{2,1,0:T(8,128)(2,1)}, bf16[1,128,1024]{2,1,0:T(8,128)(2,1)S(1)}, u32[]{:S(2)}, u32[]{:S(2)}) collective-permute-start(bf16[1,128,1024]{2,1,0:T(8,128)(2,1)} %collective-permute-done.13.refs_7_), channel_id=1, source_target_pairs={{0,224},{32,0},{64,32},{96,64},{128,96},{160,128},{192,160},{224,1... | collective-permute-start | bytes 786440 | tf_op jit(solution)/shard_map/ppermute | solution.py:39
  72.4 11.7 %collective-permute-start.19 = (bf16[1,128,1024]{2,1,0:T(8,128)(2,1)}, bf16[1,128,1024]{2,1,0:T(8,128)(2,1)S(1)}, u32[]{:S(2)}, u32[]{:S(2)}) collective-permute-start(bf16[1,128,1024]{2,1,0:T(8,128)(2,1)} %collective-permute-done.18.refs_4_), channel_id=1, source_target_pairs={{0,32},{32,64},{64,96},{96,128},{128,160},{160,192},{192,224},{224... | collective-permute-start | bytes 786440 | tf_op jit(solution)/shard_map/ppermute | solution.py:39
  73.1 12.3 %collective-permute-start.23 = (bf16[1,128,1024]{2,1,0:T(8,128)(2,1)}, bf16[1,128,1024]{2,1,0:T(8,128)(2,1)S(1)}, u32[]{:S(2)}, u32[]{:S(2)}) collective-permute-start(bf16[1,128,1024]{2,1,0:T(8,128)(2,1)} %collective-permute-done.22.refs_6_), channel_id=1, source_target_pairs={{0,224},{32,0},{64,32},{96,64},{128,96},{160,128},{192,160},{224,1... | collective-permute-start | bytes 786440 | tf_op jit(solution)/shard_map/ppermute | solution.py:39
  78.5 14.6 %collective-permute-start.26 = (bf16[1,64,1024]{2,1,0:T(8,128)(2,1)S(1)}, bf16[1,64,1024]{2,1,0:T(8,128)(2,1)S(1)}, u32[]{:S(2)}, u32[]{:S(2)}) collective-permute-start(bf16[1,64,1024]{2,1,0:T(8,128)(2,1)S(1)} %slice.36), channel_id=1, source_target_pairs={{0,32},{32,64},{64,96},{96,128},{128,160},{160,192},{192,224},{224... | collective-permute-start | bytes 393224 | tf_op jit(solution)/shard_map/ppermute | solution.py:39
  79.8 13.3 %collective-permute-start.28 = (bf16[1,64,1024]{2,1,0:T(8,128)(2,1)S(1)}, bf16[1,64,1024]{2,1,0:T(8,128)(2,1)S(1)}, u32[]{:S(2)}, u32[]{:S(2)}) collective-permute-start(bf16[1,64,1024]{2,1,0:T(8,128)(2,1)S(1)} %slice.37), channel_id=1, source_target_pairs={{0,224},{32,0},{64,32},{96,64},{128,96},{160,128},{192,160},{224,1... | collective-permute-start | bytes 393224 | tf_op jit(solution)/shard_map/ppermute | solution.py:39
  84.1 9.0 %collective-permute-start.20 = (bf16[1,64,1024]{2,1,0:T(8,128)(2,1)S(1)}, bf16[1,64,1024]{2,1,0:T(8,128)(2,1)S(1)}, u32[]{:S(2)}, u32[]{:S(2)}) collective-permute-start(bf16[1,64,1024]{2,1,0:T(8,128)(2,1)S(1)} %slice.34), channel_id=1, source_target_pairs={{0,32},{32,64},{64,96},{96,128},{128,160},{160,192},{192,224},{224... | collective-permute-start | bytes 393224 | tf_op jit(solution)/shard_map/ppermute | solution.py:39
  85.4 3.1 %copy-start.2 = (bf16[1,128,1024]{2,1,0:T(8,128)(2,1)S(1)}, bf16[1,128,1024]{2,1,0:T(8,128)(2,1)}, u32[]{:S(2)}) copy-start(bf16[1,128,1024]{2,1,0:T(8,128)(2,1)} %copy-done.1) | copy-start | bytes 786436
  85.4 3.1 %copy-start.4 = (bf16[1,128,1024]{2,1,0:T(8,128)(2,1)S(1)}, bf16[1,128,1024]{2,1,0:T(8,128)(2,1)}, u32[]{:S(2)}) copy-start(bf16[1,128,1024]{2,1,0:T(8,128)(2,1)} %copy-done.3) | copy-start | bytes 786436
  85.4 3.1 %copy-start.6 = (bf16[1,128,1024]{2,1,0:T(8,128)(2,1)S(1)}, bf16[1,128,1024]{2,1,0:T(8,128)(2,1)}, u32[]{:S(2)}) copy-start(bf16[1,128,1024]{2,1,0:T(8,128)(2,1)} %copy-done.5) | copy-start | bytes 786436
  85.4 7.7 %collective-permute-start.24 = (bf16[1,64,1024]{2,1,0:T(8,128)(2,1)S(1)}, bf16[1,64,1024]{2,1,0:T(8,128)(2,1)S(1)}, u32[]{:S(2)}, u32[]{:S(2)}) collective-permute-start(bf16[1,64,1024]{2,1,0:T(8,128)(2,1)S(1)} %slice.35), channel_id=1, source_target_pairs={{0,224},{32,0},{64,32},{96,64},{128,96},{160,128},{192,160},{224,1... | collective-permute-start | bytes 393224 | tf_op jit(solution)/shard_map/ppermute | solution.py:39
  94.4 5.3 %collective-permute-start.29 = (f32[16,128,128]{2,1,0:T(8,128)S(1)}, f32[16,128,128]{2,1,0:T(8,128)S(1)}, u32[]{:S(2)}, u32[]{:S(2)}) collective-permute-start(f32[16,128,128]{2,1,0:T(8,128)S(1)} %slice_bitcast_fusion), channel_id=1, source_target_pairs={{0,1},{1,0},{2,3},{3,2},{4,5},{5,4},{6,7},{7,6},{8,9},{9,8},{10,11... | collective-permute-start | bytes 3145736 | tf_op jit(solution)/shard_map/ppermute | solution.py:39

commit v3 on v2

--- a/solution.py
+++ b/solution.py
@@ -14,6 +14,7 @@
 SLICE = NOCC // NX
 CHUNK = AUX_HERE * SLICE
 ROWS = AUX_HERE * BLOCK
+STEPS, PAD = 32000.0, 16
 LIMIT = 24 * 1024 * 1024
 VMEM = pl.BlockSpec(memory_space=pltpu.VMEM)
 SMEM = pl.BlockSpec(memory_space=pltpu.SMEM)
@@ -146,29 +147,45 @@
     put(place, out, product(grows, [(own.at[pl.ds(0, 1)], own.at[pl.ds(1, 1)])]), (0,))
 
 
-def pair_kernel(k, place, *refs):
-    grows, columns, out = refs[:4], refs[4:8], refs[9]
-    put(place, out, product(grows, [columns[0:2], columns[2:4]]), (-k, k))
-
-
-def last_kernel(place, *refs):
-    grows, columns, out = refs[:4], refs[4:8], refs[9]
+def early_kernel(place, *refs):
+    grows, columns, out = refs[:4], refs[4:12], refs[13]
+    blocks = [columns[2 * n:2 * n + 2] for n in range(4)]
+    put(place, out, product(grows, blocks), (-1, 1, -2, 2))
+
+
+def late_kernel(place, *refs):
+    grows, columns, out = refs[:4], refs[4:12], refs[13]
+    put(place, out, product(grows, [columns[0:2], columns[2:4]]), (-3, 3))
     total = None
     for h in range(2):
         rows = jnp.concatenate([g[h] for g in grows], axis=0)
-        block = jnp.concatenate([columns[2 * h][0], columns[2 * h + 1][0]], axis=0)
+        block = jnp.concatenate([columns[4 + 2 * h][0], columns[5 + 2 * h][0]], axis=0)
         term = times(rows, block)
         total = term if total is None else total + term
     put(place, out, total, (4,))
 
 
+def encode_kernel(kept, got, out):
+    for n in range(NY * NX):
+        total = kept[0, n] + got[n]
+        top = jnp.maximum(jnp.max(jnp.abs(total), axis=0, keepdims=True), 2.0 ** -120)
+        power = jnp.ceil(jnp.log2(top))
+        scaled = jnp.floor(total * jnp.exp2(-power) * STEPS + 0.5)
+        out[n, :BLOCK] = scaled.astype(jnp.int32).astype(jnp.int16)
+        power = jnp.broadcast_to(power, (PAD, BLOCK))
+        out[n, BLOCK:] = power.astype(jnp.int32).astype(jnp.int16)
+
+
 def finish_kernel(parts, out):
-    scale = 1.0 / math.sqrt(AUX_HERE * NX * NC * NOCC)
+    scale = 1.0 / math.sqrt(AUX_HERE * NX * NC * NOCC) / STEPS
     for yy in range(NY):
-        total = parts[yy * NX]
-        for xx in range(1, NX):
-            total = total + parts[yy * NX + xx]
-        out[:, yy * BLOCK:(yy + 1) * BLOCK] = total * scale
+        total = None
+        for xx in range(NX):
+            part = parts.at[yy * NX + xx]
+            power = part[BLOCK:].astype(jnp.int32).astype(jnp.float32)[:1]
+            term = part[:BLOCK].astype(jnp.int32).astype(jnp.float32) * (jnp.exp2(power) * scale)
+            total = term if total is None else total + term
+        out[:, yy * BLOCK:(yy + 1) * BLOCK] = total
 
 
 def shards(pair_cols, pair_count, integrals, coeffs):
@@ -214,18 +231,21 @@
     rows = [halfway, y_a, y_b, y_far]
 
     tiles = jax.ShapeDtypeStruct((NC, NY * NX, BLOCK, BLOCK), jnp.float32)
+    def blocks(pairs):
+        return [half for pair in pairs for half in pair]
+
     tile = call(first_kernel, tiles, [place], rows, flops=270000000)
-    for k in range(3):
-        blocks = [half for pair in columns[k] for half in pair]
-        tile = call(
-            functools.partial(pair_kernel, k + 1), tiles, [place], rows + blocks + [tile],
-            flops=540000000, aliases={9: 0},
-        )
-    blocks = [half for pair in last for half in pair]
-    tile = call(last_kernel, tiles, [place], rows + blocks + [tile], aliases={9: 0})
-
-    both = tile[0] + swap_cores(tile[1])
-    parts = lax.all_to_all(both, ("y", "x"), 0, 0, tiled=True)
+    tile = call(
+        early_kernel, tiles, [place], rows + blocks(columns[0] + columns[1]) + [tile],
+        flops=1080000000, aliases={13: 0},
+    )
+    tile = call(late_kernel, tiles, [place], rows + blocks(columns[2] + last) + [tile], aliases={13: 0})
+
+    coded = call(
+        encode_kernel, jax.ShapeDtypeStruct((NY * NX, BLOCK + PAD, BLOCK), jnp.int16), [],
+        [tile, swap_cores(tile[1])],
+    )
+    parts = lax.all_to_all(coded, ("y", "x"), 0, 0, tiled=True)
     return call(
         finish_kernel, jax.ShapeDtypeStruct((BLOCK, NY * BLOCK), jnp.float32), [], [parts]
     )

time: 122 us -> 117 us (0.959)
  blocking collectives: 21.3 us -> 16.8 us
    all_to_all x1, blocking collectives: 21.3 us -> 16.8 us  [shards(): parts = lax.all_to_all(coded, ('y', 'x'), 0, 0, tiled=True)]
    pallas_call x8 -> x7, Pallas kernels: 9.83 us -> 8.89 us  [call(): pl.pallas_call(body, out_shape=out_shape, in_specs=[SMEM] * len(scalars)...]
  transfers between devices with their start and end apart: 31 -> 31, of which waited for: 14 -> 14; matrix products, arithmetic and copies ran while one was open for 0% -> 0% of each run, Pallas kernels for 5% -> 3%
where the time goes in v3:
time: 117 us; the launch traced here: 116 us
  starting transfers between devices  52.2 us (45%)
  waiting for transfers between devices  31.6 us (27%)
  blocking collectives  16.8 us (14%)
  Pallas kernels  9.04 us (8%)
  local copies, waits for them, and re-layouts  5.74 us (5%)
    ppermute x27, starting transfers between devices, shift(): return lax.ppermute(x, axis, [(i, (i + step) % size) for i in range(size)])  38.9 us
    ppermute x27, waiting for transfers between devices, shift(): return lax.ppermute(x, axis, [(i, (i + step) % size) for i in range(size)])  26.8 us
    all_to_all x1, blocking collectives, shards(): parts = lax.all_to_all(coded, ('y', 'x'), 0, 0, tiled=True)  16.8 us
    all_to_all x1, starting transfers between devices, shards(): lax.all_to_all(jnp.broadcast_to(piece[None], (NZ, HALF_L, SLICE)), 'z', 0...  9.01 us
    pallas_call x7, Pallas kernels, call(): pl.pallas_call(body, out_shape=out_shape, in_specs=[SMEM] * len(scalars)...  8.89 us
    all_to_all x1, waiting for transfers between devices, shards(): lax.all_to_all(jnp.broadcast_to(piece[None], (NZ, HALF_L, SLICE)), 'z', 0...  4.79 us
    ppermute x3, starting transfers between devices, mirrored(): return lax.ppermute(x, (axis, 'core'), pairs)  4.28 us
    unnamed x16, local copies, waits for them, and re-layouts  4.2 us
  transfers between devices with their start and end apart: 31, of which 14 were waited for; matrix products, arithmetic and copies ran while one was open for 0% of the time, Pallas kernels for 3%

profile of v3, /device:TPU:1, one launch (start us, length us, event | category | flops | bytes accessed | tf_op | source)
XLA Modules:
  0.0 116.3 jit_solution(15250721843967665132)
XLA Ops:
  0.0 0.7 dynamic_slice.3
  0.7 0.7 broadcast_in_dim.2
  1.4 9.0 %all-to-all-start = ((bf16[8,64,128]{2,1,0:T(8,128)(2,1)}), bf16[8,64,128]{2,1,0:T(8,128)(2,1)S(1)}, u32[]{:S(2)}, u32[]{:S(2)}) async-start(bf16[8,64,128]{2,1,0:T(8,128)(2,1)} %broadcast_in_dim.2), calls=%async_computation | async-start | bytes 262144 | tf_op jit(solution)/shard_map/all_to_all | solution.py:201
  11.1 0.0 copy-start
  11.1 1.6 %copy-done = bf16[16,4,128,128]{3,2,1,0:T(8,128)(2,1)S(1)} copy-done((bf16[16,4,128,128]{3,2,1,0:T(8,128)(2,1)S(1)}, bf16[16,4,128,128]{3,2,1,0:T(8,128)(2,1)}, u32[]{:S(2)}) %copy-start) | copy-done | bytes 2097176
  12.7 0.1 shard_map.46.integrals
  12.8 0.5 copy-done.7
  13.3 0.1 pad_add_fusion.1.info
  13.4 4.8 %all-to-all-done.refs_0_ = bf16[8,64,128]{2,1,0:T(8,128)(2,1)S(1)} async-done(((bf16[8,64,128]{2,1,0:T(8,128)(2,1)}), bf16[8,64,128]{2,1,0:T(8,128)(2,1)S(1)}, u32[]{:S(2)}, u32[]{:S(2)}) %all-to-all-start) | async-done | bytes 131104 | tf_op jit(solution)/shard_map/all_to_all | solution.py:201
  18.2 1.3 %collective-permute-start = (bf16[8,64,128]{2,1,0:T(8,128)(2,1)S(1)}, bf16[8,64,128]{2,1,0:T(8,128)(2,1)S(1)}, u32[]{:S(2)}, u32[]{:S(2)}) collective-permute-start(bf16[8,64,128]{2,1,0:T(8,128)(2,1)S(1)} %all-to-all-done.refs_0_), channel_id=1, source_target_pairs={{0,8},{8,16},{16,24},{24,0},{1,9},{9,17},{17,25},{25,1},{2,10},{10... | collective-permute-start | bytes 393224 | tf_op jit(solution)/shard_map/ppermute | solution.py:40
  19.5 2.6 %collective-permute-start.1 = (bf16[8,64,128]{2,1,0:T(8,128)(2,1)S(1)}, bf16[8,64,128]{2,1,0:T(8,128)(2,1)S(1)}, u32[]{:S(2)}, u32[]{:S(2)}) collective-permute-start(bf16[8,64,128]{2,1,0:T(8,128)(2,1)S(1)} %all-to-all-done.refs_0_), channel_id=1, source_target_pairs={{0,16},{8,24},{16,0},{24,8},{1,17},{9,25},{17,1},{25,9},{2,18},{10... | collective-permute-start | bytes 393224 | tf_op jit(solution)/shard_map/ppermute | solution.py:40
  22.1 1.1 collective-permute-start.2
  23.2 0.1 collective-permute-done.refs_1_
  23.3 2.7 %collective-permute-done.1.refs_2_ = bf16[8,64,128]{2,1,0:T(8,128)(2,1)S(1)} collective-permute-done((bf16[8,64,128]{2,1,0:T(8,128)(2,1)S(1)}, bf16[8,64,128]{2,1,0:T(8,128)(2,1)S(1)}, u32[]{:S(2)}, u32[]{:S(2)}) %collective-permute-start.1) | collective-permute-done | bytes 131104 | tf_op jit(solution)/shard_map/ppermute | solution.py:40
  26.0 0.8 collective-permute-done.2.refs_3_
  26.7 0.7 shard_map.47.refs_0_
  27.5 1.3 %collective-permute-start.3 = (bf16[16,64,128]{2,1,0:T(8,128)(2,1)S(1)}, bf16[16,64,128]{2,1,0:T(8,128)(2,1)S(1)}, u32[]{:S(2)}, u32[]{:S(2)}) collective-permute-start(bf16[16,64,128]{2,1,0:T(8,128)(2,1)S(1)} %shard_map.47.refs_0_), channel_id=1, source_target_pairs={{0,2},{2,4},{4,6},{6,0},{1,3},{3,5},{5,7},{7,1},{8,10},{10,12},{12... | collective-permute-start | bytes 786440 | tf_op jit(solution)/shard_map/ppermute | solution.py:40
  28.8 1.5 %collective-permute-start.4 = (bf16[16,64,128]{2,1,0:T(8,128)(2,1)S(1)}, bf16[16,64,128]{2,1,0:T(8,128)(2,1)S(1)}, u32[]{:S(2)}, u32[]{:S(2)}) collective-permute-start(bf16[16,64,128]{2,1,0:T(8,128)(2,1)S(1)} %shard_map.47.refs_0_), channel_id=1, source_target_pairs={{0,6},{2,0},{4,2},{6,4},{1,7},{3,1},{5,3},{7,5},{8,14},{10,8},{12,... | collective-permute-start | bytes 786440 | tf_op jit(solution)/shard_map/ppermute | solution.py:40
  30.2 1.5 %collective-permute-start.5 = (bf16[16,64,128]{2,1,0:T(8,128)(2,1)S(1)}, bf16[16,64,128]{2,1,0:T(8,128)(2,1)S(1)}, u32[]{:S(2)}, u32[]{:S(2)}) collective-permute-start(bf16[16,64,128]{2,1,0:T(8,128)(2,1)S(1)} %shard_map.47.refs_0_), channel_id=1, source_target_pairs={{0,4},{2,6},{4,0},{6,2},{1,5},{3,7},{5,1},{7,3},{8,12},{10,14},{12... | collective-permute-start | bytes 786440 | tf_op jit(solution)/shard_map/ppermute | solution.py:40
  31.8 4.0 %collective-permute-start.6 = (bf16[16,64,128]{2,1,0:T(8,128)(2,1)S(1)}, bf16[16,64,128]{2,1,0:T(8,128)(2,1)S(1)}, u32[]{:S(2)}, u32[]{:S(2)}) collective-permute-start(bf16[16,64,128]{2,1,0:T(8,128)(2,1)S(1)} %shard_map.47.refs_0_), channel_id=1, source_target_pairs={{0,1},{1,0},{2,3},{3,2},{4,5},{5,4},{6,7},{7,6},{8,9},{9,8},{10,11... | collective-permute-start | bytes 786440 | tf_op jit(solution)/shard_map/ppermute | solution.py:40
  35.8 0.0 collective-permute-done.3.refs_1_
  35.8 5.3 %collective-permute-start.7 = (bf16[16,64,128]{2,1,0:T(8,128)(2,1)S(1)}, bf16[16,64,128]{2,1,0:T(8,128)(2,1)S(1)}, u32[]{:S(2)}, u32[]{:S(2)}) collective-permute-start(bf16[16,64,128]{2,1,0:T(8,128)(2,1)S(1)} %collective-permute-done.3.refs_1_), channel_id=1, source_target_pairs={{0,1},{1,0},{2,3},{3,2},{4,5},{5,4},{6,7},{7,6},{8,9},{9,8},{10,11... | collective-permute-start | bytes 786440 | tf_op jit(solution)/shard_map/ppermute | solution.py:40
  41.1 0.0 collective-permute-start.8
  41.1 0.0 collective-permute-done.5.refs_3_
  41.1 3.0 %collective-permute-start.9 = (bf16[16,64,128]{2,1,0:T(8,128)(2,1)S(1)}, bf16[16,64,128]{2,1,0:T(8,128)(2,1)S(1)}, u32[]{:S(2)}, u32[]{:S(2)}) collective-permute-start(bf16[16,64,128]{2,1,0:T(8,128)(2,1)S(1)} %collective-permute-done.5.refs_3_), channel_id=1, source_target_pairs={{0,1},{1,0},{2,3},{3,2},{4,5},{5,4},{6,7},{7,6},{8,9},{9,8},{10,11... | collective-permute-start | bytes 786440 | tf_op jit(solution)/shard_map/ppermute | solution.py:40
  44.1 1.1 collective-permute-done.9.refs_7_
  45.2 1.3 %shard_map.48.refs_0_ = bf16[2,128,1024]{2,1,0:T(8,128)(2,1)S(1)} custom-call(s32[1]{0:T(128)} %bitcast.2.core, bf16[16,4,128,128]{3,2,1,0:T(8,128)(2,1)S(1)} %shard_map.46.integrals, bf16[16,64,128]{2,1,0:T(8,128)(2,1)S(1)} %shard_map.47.refs_0_, bf16[16,64,128]{2,1,0:T(8,128)(2,1)S(1)} %collective-permute-done.3.refs_1_, ...), custom_call_target="tpu_custom_call" | custom-call | tf_op jit(solution)/shard_map/pallas_call | solution.py:24
  46.6 0.9 collective-permute-start.10
  47.5 1.8 %collective-permute-start.12 = (bf16[1,128,1024]{2,1,0:T(8,128)(2,1)S(1)}, bf16[1,128,1024]{2,1,0:T(8,128)(2,1)S(1)}, u32[]{:S(2)}, u32[]{:S(2)}) collective-permute-start(bf16[1,128,1024]{2,1,0:T(8,128)(2,1)S(1)} %get-tuple-element.20), channel_id=1, source_target_pairs={{0,224},{32,0},{64,32},{96,64},{128,96},{160,128},{192,160},{224,1... | collective-permute-start | bytes 786440 | tf_op jit(solution)/shard_map/ppermute | solution.py:40
  49.4 2.2 %collective-permute-start.14 = (bf16[2,128,1024]{2,1,0:T(8,128)(2,1)S(1)}, bf16[2,128,1024]{2,1,0:T(8,128)(2,1)S(1)}, u32[]{:S(2)}, u32[]{:S(2)}) collective-permute-start(bf16[2,128,1024]{2,1,0:T(8,128)(2,1)S(1)} %shard_map.48.refs_0_), channel_id=1, source_target_pairs={{0,8},{1,25},{8,16},{9,1},{16,24},{17,9},{24,0},{25,17},{2,10},{3,... | collective-permute-start | bytes 1572872 | tf_op jit(solution)/shard_map/ppermute | solution.py:48
  51.6 0.0 collective-permute-start.17
  51.6 3.8 %collective-permute-done.10.refs_5_ = bf16[1,128,1024]{2,1,0:T(8,128)(2,1)S(1)} collective-permute-done((bf16[1,128,1024]{2,1,0:T(8,128)(2,1)S(1)}, bf16[1,128,1024]{2,1,0:T(8,128)(2,1)S(1)}, u32[]{:S(2)}, u32[]{:S(2)}) %collective-permute-start.10) | collective-permute-done | bytes 262176 | tf_op jit(solution)/shard_map/ppermute | solution.py:40
  55.4 0.0 collective-permute-start.21
  55.4 1.5 %collective-permute-start.11 = (bf16[1,128,1024]{2,1,0:T(8,128)(2,1)S(1)}, bf16[1,128,1024]{2,1,0:T(8,128)(2,1)}, u32[]{:S(2)}, u32[]{:S(2)}) collective-permute-start(bf16[1,128,1024]{2,1,0:T(8,128)(2,1)S(1)} %collective-permute-done.10.refs_5_), channel_id=1, source_target_pairs={{0,32},{32,64},{64,96},{96,128},{128,160},{160,192},{192,224},{224... | collective-permute-start | bytes 786440 | tf_op jit(solution)/shard_map/ppermute | solution.py:40
  56.9 4.3 %collective-permute-done.17.refs_4_ = bf16[1,128,1024]{2,1,0:T(8,128)(2,1)S(1)} collective-permute-done((bf16[1,128,1024]{2,1,0:T(8,128)(2,1)S(1)}, bf16[1,128,1024]{2,1,0:T(8,128)(2,1)S(1)}, u32[]{:S(2)}, u32[]{:S(2)}) %collective-permute-start.17) | collective-permute-done | bytes 262176 | tf_op jit(solution)/shard_map/ppermute | solution.py:40
  61.2 0.7 copy-done.1
  61.9 1.5 %collective-permute-start.18 = (bf16[1,128,1024]{2,1,0:T(8,128)(2,1)S(1)}, bf16[1,128,1024]{2,1,0:T(8,128)(2,1)}, u32[]{:S(2)}, u32[]{:S(2)}) collective-permute-start(bf16[1,128,1024]{2,1,0:T(8,128)(2,1)S(1)} %collective-permute-done.17.refs_4_), channel_id=1, source_target_pairs={{0,32},{32,64},{64,96},{96,128},{128,160},{160,192},{192,224},{224... | collective-permute-start | bytes 786440 | tf_op jit(solution)/shard_map/ppermute | solution.py:40
  63.3 0.7 copy-done.3
  64.0 2.9 %collective-permute-done.11.refs_9_ = bf16[1,128,1024]{2,1,0:T(8,128)(2,1)} collective-permute-done((bf16[1,128,1024]{2,1,0:T(8,128)(2,1)S(1)}, bf16[1,128,1024]{2,1,0:T(8,128)(2,1)}, u32[]{:S(2)}, u32[]{:S(2)}) %collective-permute-start.11) | collective-permute-done | bytes 262176 | tf_op jit(solution)/shard_map/ppermute | solution.py:40
  66.9 0.7 copy-done.5
  67.6 2.1 %collective-permute-start.16 = (bf16[2,128,1024]{2,1,0:T(8,128)(2,1)S(1)}, bf16[2,128,1024]{2,1,0:T(8,128)(2,1)S(1)}, u32[]{:S(2)}, u32[]{:S(2)}) collective-permute-start(bf16[2,128,1024]{2,1,0:T(8,128)(2,1)S(1)} %collective-permute-done.14.refs_1_), channel_id=1, source_target_pairs={{0,8},{1,25},{8,16},{9,1},{16,24},{17,9},{24,0},{25,17},{2,10},{3,... | collective-permute-start | bytes 1572872 | tf_op jit(solution)/shard_map/ppermute | solution.py:48
  69.7 1.5 %collective-permute-start.20 = (bf16[1,128,1024]{2,1,0:T(8,128)(2,1)}, bf16[1,128,1024]{2,1,0:T(8,128)(2,1)S(1)}, u32[]{:S(2)}, u32[]{:S(2)}) collective-permute-start(bf16[1,128,1024]{2,1,0:T(8,128)(2,1)} %collective-permute-done.11.refs_9_), channel_id=1, source_target_pairs={{0,32},{32,64},{64,96},{96,128},{128,160},{160,192},{192,224},{224... | collective-permute-start | bytes 786440 | tf_op jit(solution)/shard_map/ppermute | solution.py:40
  71.1 1.2 %collective-permute-start.24 = (bf16[1,128,1024]{2,1,0:T(8,128)(2,1)}, bf16[1,128,1024]{2,1,0:T(8,128)(2,1)S(1)}, u32[]{:S(2)}, u32[]{:S(2)}) collective-permute-start(bf16[1,128,1024]{2,1,0:T(8,128)(2,1)} %collective-permute-done.13.refs_11_), channel_id=1, source_target_pairs={{0,224},{32,0},{64,32},{96,64},{128,96},{160,128},{192,160},{224,1... | collective-permute-start | bytes 786440 | tf_op jit(solution)/shard_map/ppermute | solution.py:40
  72.4 0.3 collective-permute-start.19
  72.6 0.4 collective-permute-done.22.refs_10_
  73.1 2.0 %collective-permute-start.23 = (bf16[1,128,1024]{2,1,0:T(8,128)(2,1)}, bf16[1,128,1024]{2,1,0:T(8,128)(2,1)S(1)}, u32[]{:S(2)}, u32[]{:S(2)}) collective-permute-start(bf16[1,128,1024]{2,1,0:T(8,128)(2,1)} %collective-permute-done.22.refs_10_), channel_id=1, source_target_pairs={{0,224},{32,0},{64,32},{96,64},{128,96},{160,128},{192,160},{224,1... | collective-permute-start | bytes 786440 | tf_op jit(solution)/shard_map/ppermute | solution.py:40
  75.0 3.4 %collective-permute-done.20.refs_5_ = bf16[1,128,1024]{2,1,0:T(8,128)(2,1)S(1)} collective-permute-done((bf16[1,128,1024]{2,1,0:T(8,128)(2,1)}, bf16[1,128,1024]{2,1,0:T(8,128)(2,1)S(1)}, u32[]{:S(2)}, u32[]{:S(2)}) %collective-permute-start.20) | collective-permute-done | bytes 262176 | tf_op jit(solution)/shard_map/ppermute | solution.py:40
  78.5 0.2 collective-permute-start.27
  78.7 1.1 collective-permute-done.24.refs_7_
  79.8 1.6 %collective-permute-start.28 = (bf16[1,64,1024]{2,1,0:T(8,128)(2,1)S(1)}, bf16[1,64,1024]{2,1,0:T(8,128)(2,1)S(1)}, u32[]{:S(2)}, u32[]{:S(2)}) collective-permute-start(bf16[1,64,1024]{2,1,0:T(8,128)(2,1)S(1)} %slice.33), channel_id=1, source_target_pairs={{0,224},{32,0},{64,32},{96,64},{128,96},{160,128},{192,160},{224,1... | collective-permute-start | bytes 393224 | tf_op jit(solution)/shard_map/ppermute | solution.py:40
  81.3 2.8 %collective-permute-done.19.refs_4_ = bf16[1,128,1024]{2,1,0:T(8,128)(2,1)S(1)} collective-permute-done((bf16[1,128,1024]{2,1,0:T(8,128)(2,1)}, bf16[1,128,1024]{2,1,0:T(8,128)(2,1)S(1)}, u32[]{:S(2)}, u32[]{:S(2)}) %collective-permute-start.19) | collective-permute-done | bytes 262176 | tf_op jit(solution)/shard_map/ppermute | solution.py:40
  84.1 0.2 collective-permute-start.25
  84.3 1.1 collective-permute-done.23.refs_6_
  85.4 1.8 %collective-permute-start.26 = (bf16[1,64,1024]{2,1,0:T(8,128)(2,1)S(1)}, bf16[1,64,1024]{2,1,0:T(8,128)(2,1)S(1)}, u32[]{:S(2)}, u32[]{:S(2)}) collective-permute-start(bf16[1,64,1024]{2,1,0:T(8,128)(2,1)S(1)} %slice.31), channel_id=1, source_target_pairs={{0,224},{32,0},{64,32},{96,64},{128,96},{160,128},{192,160},{224,1... | collective-permute-start | bytes 393224 | tf_op jit(solution)/shard_map/ppermute | solution.py:40
  87.2 0.1 pad_add_fusion.place
  87.2 1.2 %shard_map.49.refs_12_ = f32[2,16,128,128]{3,2,1,0:T(8,128)S(1)} custom-call(s32[3]{0:T(128)S(1)} %pad_add_fusion.place, bf16[2,128,1024]{2,1,0:T(8,128)(2,1)S(1)} %shard_map.48.refs_0_, bf16[2,128,1024]{2,1,0:T(8,128)(2,1)S(1)} %collective-permute-done.14.refs_1_, bf16[2,128,1024]{2,1,0:T(8,128)(2,1)S(1)} %collective-permute-done.15.refs_2_, ...), custom_call_target="tpu_custom_call" | custom-call | flops 270000000 | bytes 12000000 | tf_op jit(solution)/shard_map/pallas_call | solution.py:24
  88.5 2.5 %shard_map.50.refs_12_ = f32[2,16,128,128]{3,2,1,0:T(8,128)S(1)} custom-call(s32[3]{0:T(128)S(1)} %pad_add_fusion.place, bf16[2,128,1024]{2,1,0:T(8,128)(2,1)S(1)} %shard_map.48.refs_0_, bf16[2,128,1024]{2,1,0:T(8,128)(2,1)S(1)} %collective-permute-done.14.refs_1_, ...), custom_call_target="tpu_custom_call", output_to_operand_aliasing={{}: (13, {})} | custom-call | flops 1080000000 | bytes 12000000 | tf_op jit(solution)/shard_map/pallas_call | solution.py:24
  91.1 1.8 %shard_map.51.kept = f32[2,16,128,128]{3,2,1,0:T(8,128)S(1)} custom-call(s32[3]{0:T(128)S(1)} %pad_add_fusion.place, bf16[2,128,1024]{2,1,0:T(8,128)(2,1)S(1)} %shard_map.48.refs_0_, bf16[2,128,1024]{2,1,0:T(8,128)(2,1)S(1)} %collective-permute-done.14.refs_1_, ...), custom_call_target="tpu_custom_call", output_to_operand_aliasing={{}: (13, {})} | custom-call | tf_op jit(solution)/shard_map/pallas_call | solution.py:24
  93.0 0.1 slice_bitcast_fusion
  93.1 3.0 %collective-permute-start.29 = (f32[16,128,128]{2,1,0:T(8,128)S(1)}, f32[16,128,128]{2,1,0:T(8,128)S(1)}, u32[]{:S(2)}, u32[]{:S(2)}) collective-permute-start(f32[16,128,128]{2,1,0:T(8,128)S(1)} %slice_bitcast_fusion), channel_id=1, source_target_pairs={{0,1},{1,0},{2,3},{3,2},{4,5},{5,4},{6,7},{7,6},{8,9},{9,8},{10,11... | collective-permute-start | bytes 3145736 | tf_op jit(solution)/shard_map/ppermute | solution.py:40
  96.0 2.3 %collective-permute-done.29.got = f32[16,128,128]{2,1,0:T(8,128)S(1)} collective-permute-done((f32[16,128,128]{2,1,0:T(8,128)S(1)}, f32[16,128,128]{2,1,0:T(8,128)S(1)}, u32[]{:S(2)}, u32[]{:S(2)}) %collective-permute-start.29) | collective-permute-done | bytes 1048608 | tf_op jit(solution)/shard_map/ppermute | solution.py:40
  98.3 0.4 shard_map.52
  98.7 16.8 %all_to_all.10.parts = s16[16,144,128]{2,1,0:T(8,128)(2,1)S(1)} all-to-all(s16[16,144,128]{2,1,0:T(8,128)(2,1)S(1)} %shard_map.52), channel_id=1, replica_groups=mesh['z'=8,'y'=4,'x'=4,'core'=2] {'y','x'}, dimensions={0} | all-to-all | bytes 1179648 | tf_op jit(solution)/shard_map/all_to_all | solution.py:248
  115.5 0.8 shard_map.53
  (33 shorter events, 0.1 us)
Async XLA Ops:
  1.4 16.8 %all-to-all-start = ((bf16[8,64,128]{2,1,0:T(8,128)(2,1)}), bf16[8,64,128]{2,1,0:T(8,128)(2,1)S(1)}, u32[]{:S(2)}, u32[]{:S(2)}) async-start(bf16[8,64,128]{2,1,0:T(8,128)(2,1)} %broadcast_in_dim.2), calls=%async_computation | async-start | bytes 262144 | tf_op jit(solution)/shard_map/all_to_all | solution.py:201
  11.1 1.6 %copy-start = (bf16[16,4,128,128]{3,2,1,0:T(8,128)(2,1)S(1)}, bf16[16,4,128,128]{3,2,1,0:T(8,128)(2,1)}, u32[]{:S(2)}) copy-start(bf16[16,4,128,128]{3,2,1,0:T(8,128)(2,1)} %source.1) | copy-start | bytes 6291460
  12.7 0.7 copy-start.7
  18.2 5.1 %collective-permute-start = (bf16[8,64,128]{2,1,0:T(8,128)(2,1)S(1)}, bf16[8,64,128]{2,1,0:T(8,128)(2,1)S(1)}, u32[]{:S(2)}, u32[]{:S(2)}) collective-permute-start(bf16[8,64,128]{2,1,0:T(8,128)(2,1)S(1)} %all-to-all-done.refs_0_), channel_id=1, source_target_pairs={{0,8},{8,16},{16,24},{24,0},{1,9},{9,17},{17,25},{25,1},{2,10},{10... | collective-permute-start | bytes 393224 | tf_op jit(solution)/shard_map/ppermute | solution.py:40
  19.5 6.5 %collective-permute-start.1 = (bf16[8,64,128]{2,1,0:T(8,128)(2,1)S(1)}, bf16[8,64,128]{2,1,0:T(8,128)(2,1)S(1)}, u32[]{:S(2)}, u32[]{:S(2)}) collective-permute-start(bf16[8,64,128]{2,1,0:T(8,128)(2,1)S(1)} %all-to-all-done.refs_0_), channel_id=1, source_target_pairs={{0,16},{8,24},{16,0},{24,8},{1,17},{9,25},{17,1},{25,9},{2,18},{10... | collective-permute-start | bytes 393224 | tf_op jit(solution)/shard_map/ppermute | solution.py:40
  22.1 4.6 %collective-permute-start.2 = (bf16[8,64,128]{2,1,0:T(8,128)(2,1)S(1)}, bf16[8,64,128]{2,1,0:T(8,128)(2,1)S(1)}, u32[]{:S(2)}, u32[]{:S(2)}) collective-permute-start(bf16[8,64,128]{2,1,0:T(8,128)(2,1)S(1)} %all-to-all-done.refs_0_), channel_id=1, source_target_pairs={{0,24},{8,0},{16,8},{24,16},{1,25},{9,1},{17,9},{25,17},{2,26},{10... | collective-permute-start | bytes 393224 | tf_op jit(solution)/shard_map/ppermute | solution.py:40
  27.5 8.3 %collective-permute-start.3 = (bf16[16,64,128]{2,1,0:T(8,128)(2,1)S(1)}, bf16[16,64,128]{2,1,0:T(8,128)(2,1)S(1)}, u32[]{:S(2)}, u32[]{:S(2)}) collective-permute-start(bf16[16,64,128]{2,1,0:T(8,128)(2,1)S(1)} %shard_map.47.refs_0_), channel_id=1, source_target_pairs={{0,2},{2,4},{4,6},{6,0},{1,3},{3,5},{5,7},{7,1},{8,10},{10,12},{12... | collective-permute-start | bytes 786440 | tf_op jit(solution)/shard_map/ppermute | solution.py:40
  28.8 12.4 %collective-permute-start.4 = (bf16[16,64,128]{2,1,0:T(8,128)(2,1)S(1)}, bf16[16,64,128]{2,1,0:T(8,128)(2,1)S(1)}, u32[]{:S(2)}, u32[]{:S(2)}) collective-permute-start(bf16[16,64,128]{2,1,0:T(8,128)(2,1)S(1)} %shard_map.47.refs_0_), channel_id=1, source_target_pairs={{0,6},{2,0},{4,2},{6,4},{1,7},{3,1},{5,3},{7,5},{8,14},{10,8},{12,... | collective-permute-start | bytes 786440 | tf_op jit(solution)/shard_map/ppermute | solution.py:40
  30.2 10.9 %collective-permute-start.5 = (bf16[16,64,128]{2,1,0:T(8,128)(2,1)S(1)}, bf16[16,64,128]{2,1,0:T(8,128)(2,1)S(1)}, u32[]{:S(2)}, u32[]{:S(2)}) collective-permute-start(bf16[16,64,128]{2,1,0:T(8,128)(2,1)S(1)} %shard_map.47.refs_0_), channel_id=1, source_target_pairs={{0,4},{2,6},{4,0},{6,2},{1,5},{3,7},{5,1},{7,3},{8,12},{10,14},{12... | collective-permute-start | bytes 786440 | tf_op jit(solution)/shard_map/ppermute | solution.py:40
  31.8 12.3 %collective-permute-start.6 = (bf16[16,64,128]{2,1,0:T(8,128)(2,1)S(1)}, bf16[16,64,128]{2,1,0:T(8,128)(2,1)S(1)}, u32[]{:S(2)}, u32[]{:S(2)}) collective-permute-start(bf16[16,64,128]{2,1,0:T(8,128)(2,1)S(1)} %shard_map.47.refs_0_), channel_id=1, source_target_pairs={{0,1},{1,0},{2,3},{3,2},{4,5},{5,4},{6,7},{7,6},{8,9},{9,8},{10,11... | collective-permute-start | bytes 786440 | tf_op jit(solution)/shard_map/ppermute | solution.py:40
  35.8 8.3 %collective-permute-start.7 = (bf16[16,64,128]{2,1,0:T(8,128)(2,1)S(1)}, bf16[16,64,128]{2,1,0:T(8,128)(2,1)S(1)}, u32[]{:S(2)}, u32[]{:S(2)}) collective-permute-start(bf16[16,64,128]{2,1,0:T(8,128)(2,1)S(1)} %collective-permute-done.3.refs_1_), channel_id=1, source_target_pairs={{0,1},{1,0},{2,3},{3,2},{4,5},{5,4},{6,7},{7,6},{8,9},{9,8},{10,11... | collective-permute-start | bytes 786440 | tf_op jit(solution)/shard_map/ppermute | solution.py:40
  41.1 3.0 %collective-permute-start.8 = (bf16[16,64,128]{2,1,0:T(8,128)(2,1)S(1)}, bf16[16,64,128]{2,1,0:T(8,128)(2,1)S(1)}, u32[]{:S(2)}, u32[]{:S(2)}) collective-permute-start(bf16[16,64,128]{2,1,0:T(8,128)(2,1)S(1)} %collective-permute-done.4.refs_2_), channel_id=1, source_target_pairs={{0,1},{1,0},{2,3},{3,2},{4,5},{5,4},{6,7},{7,6},{8,9},{9,8},{10,11... | collective-permute-start | bytes 786440 | tf_op jit(solution)/shard_map/ppermute | solution.py:40
  41.1 4.1 %collective-permute-start.9 = (bf16[16,64,128]{2,1,0:T(8,128)(2,1)S(1)}, bf16[16,64,128]{2,1,0:T(8,128)(2,1)S(1)}, u32[]{:S(2)}, u32[]{:S(2)}) collective-permute-start(bf16[16,64,128]{2,1,0:T(8,128)(2,1)S(1)} %collective-permute-done.5.refs_3_), channel_id=1, source_target_pairs={{0,1},{1,0},{2,3},{3,2},{4,5},{5,4},{6,7},{7,6},{8,9},{9,8},{10,11... | collective-permute-start | bytes 786440 | tf_op jit(solution)/shard_map/ppermute | solution.py:40
  46.6 8.8 %collective-permute-start.10 = (bf16[1,128,1024]{2,1,0:T(8,128)(2,1)S(1)}, bf16[1,128,1024]{2,1,0:T(8,128)(2,1)S(1)}, u32[]{:S(2)}, u32[]{:S(2)}) collective-permute-start(bf16[1,128,1024]{2,1,0:T(8,128)(2,1)S(1)} %get-tuple-element.20), channel_id=1, source_target_pairs={{0,32},{32,64},{64,96},{96,128},{128,160},{160,192},{192,224},{224... | collective-permute-start | bytes 786440 | tf_op jit(solution)/shard_map/ppermute | solution.py:40
  47.5 7.9 %collective-permute-start.12 = (bf16[1,128,1024]{2,1,0:T(8,128)(2,1)S(1)}, bf16[1,128,1024]{2,1,0:T(8,128)(2,1)S(1)}, u32[]{:S(2)}, u32[]{:S(2)}) collective-permute-start(bf16[1,128,1024]{2,1,0:T(8,128)(2,1)S(1)} %get-tuple-element.20), channel_id=1, source_target_pairs={{0,224},{32,0},{64,32},{96,64},{128,96},{160,128},{192,160},{224,1... | collective-permute-start | bytes 786440 | tf_op jit(solution)/shard_map/ppermute | solution.py:40
  49.4 18.3 %collective-permute-start.14 = (bf16[2,128,1024]{2,1,0:T(8,128)(2,1)S(1)}, bf16[2,128,1024]{2,1,0:T(8,128)(2,1)S(1)}, u32[]{:S(2)}, u32[]{:S(2)}) collective-permute-start(bf16[2,128,1024]{2,1,0:T(8,128)(2,1)S(1)} %shard_map.48.refs_0_), channel_id=1, source_target_pairs={{0,8},{1,25},{8,16},{9,1},{16,24},{17,9},{24,0},{25,17},{2,10},{3,... | collective-permute-start | bytes 1572872 | tf_op jit(solution)/shard_map/ppermute | solution.py:48
  51.6 9.6 %collective-permute-start.17 = (bf16[1,128,1024]{2,1,0:T(8,128)(2,1)S(1)}, bf16[1,128,1024]{2,1,0:T(8,128)(2,1)S(1)}, u32[]{:S(2)}, u32[]{:S(2)}) collective-permute-start(bf16[1,128,1024]{2,1,0:T(8,128)(2,1)S(1)} %get-tuple-element.19), channel_id=1, source_target_pairs={{0,32},{32,64},{64,96},{96,128},{128,160},{160,192},{192,224},{224... | collective-permute-start | bytes 786440 | tf_op jit(solution)/shard_map/ppermute | solution.py:40
  51.6 18.1 %collective-permute-start.15 = (bf16[2,128,1024]{2,1,0:T(8,128)(2,1)S(1)}, bf16[2,128,1024]{2,1,0:T(8,128)(2,1)S(1)}, u32[]{:S(2)}, u32[]{:S(2)}) collective-permute-start(bf16[2,128,1024]{2,1,0:T(8,128)(2,1)S(1)} %shard_map.48.refs_0_), channel_id=1, source_target_pairs={{0,24},{1,9},{8,0},{9,17},{16,8},{17,25},{24,16},{25,1},{2,26},{3,... | collective-permute-start | bytes 1572872 | tf_op jit(solution)/shard_map/ppermute | solution.py:48
  55.4 6.5 %collective-permute-start.21 = (bf16[1,128,1024]{2,1,0:T(8,128)(2,1)S(1)}, bf16[1,128,1024]{2,1,0:T(8,128)(2,1)S(1)}, u32[]{:S(2)}, u32[]{:S(2)}) collective-permute-start(bf16[1,128,1024]{2,1,0:T(8,128)(2,1)S(1)} %get-tuple-element.19), channel_id=1, source_target_pairs={{0,224},{32,0},{64,32},{96,64},{128,96},{160,128},{192,160},{224,1... | collective-permute-start | bytes 786440 | tf_op jit(solution)/shard_map/ppermute | solution.py:40
  55.4 11.5 %collective-permute-start.11 = (bf16[1,128,1024]{2,1,0:T(8,128)(2,1)S(1)}, bf16[1,128,1024]{2,1,0:T(8,128)(2,1)}, u32[]{:S(2)}, u32[]{:S(2)}) collective-permute-start(bf16[1,128,1024]{2,1,0:T(8,128)(2,1)S(1)} %collective-permute-done.10.refs_5_), channel_id=1, source_target_pairs={{0,32},{32,64},{64,96},{96,128},{128,160},{160,192},{192,224},{224... | collective-permute-start | bytes 786440 | tf_op jit(solution)/shard_map/ppermute | solution.py:40
  61.2 8.5 %collective-permute-start.13 = (bf16[1,128,1024]{2,1,0:T(8,128)(2,1)S(1)}, bf16[1,128,1024]{2,1,0:T(8,128)(2,1)}, u32[]{:S(2)}, u32[]{:S(2)}) collective-permute-start(bf16[1,128,1024]{2,1,0:T(8,128)(2,1)S(1)} %collective-permute-done.12.refs_7_), channel_id=1, source_target_pairs={{0,224},{32,0},{64,32},{96,64},{128,96},{160,128},{192,160},{224,1... | collective-permute-start | bytes 786440 | tf_op jit(solution)/shard_map/ppermute | solution.py:40
  61.2 0.7 copy-start.1
  61.9 10.5 %collective-permute-start.18 = (bf16[1,128,1024]{2,1,0:T(8,128)(2,1)S(1)}, bf16[1,128,1024]{2,1,0:T(8,128)(2,1)}, u32[]{:S(2)}, u32[]{:S(2)}) collective-permute-start(bf16[1,128,1024]{2,1,0:T(8,128)(2,1)S(1)} %collective-permute-done.17.refs_4_), channel_id=1, source_target_pairs={{0,32},{32,64},{64,96},{96,128},{128,160},{160,192},{192,224},{224... | collective-permute-start | bytes 786440 | tf_op jit(solution)/shard_map/ppermute | solution.py:40
  63.3 0.7 copy-start.3
  66.9 6.2 %collective-permute-start.22 = (bf16[1,128,1024]{2,1,0:T(8,128)(2,1)S(1)}, bf16[1,128,1024]{2,1,0:T(8,128)(2,1)}, u32[]{:S(2)}, u32[]{:S(2)}) collective-permute-start(bf16[1,128,1024]{2,1,0:T(8,128)(2,1)S(1)} %collective-permute-done.21.refs_6_), channel_id=1, source_target_pairs={{0,224},{32,0},{64,32},{96,64},{128,96},{160,128},{192,160},{224,1... | collective-permute-start | bytes 786440 | tf_op jit(solution)/shard_map/ppermute | solution.py:40
  66.9 0.7 copy-start.5
  67.6 19.6 %collective-permute-start.16 = (bf16[2,128,1024]{2,1,0:T(8,128)(2,1)S(1)}, bf16[2,128,1024]{2,1,0:T(8,128)(2,1)S(1)}, u32[]{:S(2)}, u32[]{:S(2)}) collective-permute-start(bf16[2,128,1024]{2,1,0:T(8,128)(2,1)S(1)} %collective-permute-done.14.refs_1_), channel_id=1, source_target_pairs={{0,8},{1,25},{8,16},{9,1},{16,24},{17,9},{24,0},{25,17},{2,10},{3,... | collective-permute-start | bytes 1572872 | tf_op jit(solution)/shard_map/ppermute | solution.py:48
  69.7 8.8 %collective-permute-start.20 = (bf16[1,128,1024]{2,1,0:T(8,128)(2,1)}, bf16[1,128,1024]{2,1,0:T(8,128)(2,1)S(1)}, u32[]{:S(2)}, u32[]{:S(2)}) collective-permute-start(bf16[1,128,1024]{2,1,0:T(8,128)(2,1)} %collective-permute-done.11.refs_9_), channel_id=1, source_target_pairs={{0,32},{32,64},{64,96},{96,128},{128,160},{160,192},{192,224},{224... | collective-permute-start | bytes 786440 | tf_op jit(solution)/shard_map/ppermute | solution.py:40
  71.1 8.6 %collective-permute-start.24 = (bf16[1,128,1024]{2,1,0:T(8,128)(2,1)}, bf16[1,128,1024]{2,1,0:T(8,128)(2,1)S(1)}, u32[]{:S(2)}, u32[]{:S(2)}) collective-permute-start(bf16[1,128,1024]{2,1,0:T(8,128)(2,1)} %collective-permute-done.13.refs_11_), channel_id=1, source_target_pairs={{0,224},{32,0},{64,32},{96,64},{128,96},{160,128},{192,160},{224,1... | collective-permute-start | bytes 786440 | tf_op jit(solution)/shard_map/ppermute | solution.py:40
  72.4 11.7 %collective-permute-start.19 = (bf16[1,128,1024]{2,1,0:T(8,128)(2,1)}, bf16[1,128,1024]{2,1,0:T(8,128)(2,1)S(1)}, u32[]{:S(2)}, u32[]{:S(2)}) collective-permute-start(bf16[1,128,1024]{2,1,0:T(8,128)(2,1)} %collective-permute-done.18.refs_8_), channel_id=1, source_target_pairs={{0,32},{32,64},{64,96},{96,128},{128,160},{160,192},{192,224},{224... | collective-permute-start | bytes 786440 | tf_op jit(solution)/shard_map/ppermute | solution.py:40
  73.1 12.3 %collective-permute-start.23 = (bf16[1,128,1024]{2,1,0:T(8,128)(2,1)}, bf16[1,128,1024]{2,1,0:T(8,128)(2,1)S(1)}, u32[]{:S(2)}, u32[]{:S(2)}) collective-permute-start(bf16[1,128,1024]{2,1,0:T(8,128)(2,1)} %collective-permute-done.22.refs_10_), channel_id=1, source_target_pairs={{0,224},{32,0},{64,32},{96,64},{128,96},{160,128},{192,160},{224,1... | collective-permute-start | bytes 786440 | tf_op jit(solution)/shard_map/ppermute | solution.py:40
  78.5 12.6 %collective-permute-start.27 = (bf16[1,64,1024]{2,1,0:T(8,128)(2,1)S(1)}, bf16[1,64,1024]{2,1,0:T(8,128)(2,1)S(1)}, u32[]{:S(2)}, u32[]{:S(2)}) collective-permute-start(bf16[1,64,1024]{2,1,0:T(8,128)(2,1)S(1)} %slice.32), channel_id=1, source_target_pairs={{0,32},{32,64},{64,96},{96,128},{128,160},{160,192},{192,224},{224... | collective-permute-start | bytes 393224 | tf_op jit(solution)/shard_map/ppermute | solution.py:40
  79.8 11.3 %collective-permute-start.28 = (bf16[1,64,1024]{2,1,0:T(8,128)(2,1)S(1)}, bf16[1,64,1024]{2,1,0:T(8,128)(2,1)S(1)}, u32[]{:S(2)}, u32[]{:S(2)}) collective-permute-start(bf16[1,64,1024]{2,1,0:T(8,128)(2,1)S(1)} %slice.33), channel_id=1, source_target_pairs={{0,224},{32,0},{64,32},{96,64},{128,96},{160,128},{192,160},{224,1... | collective-permute-start | bytes 393224 | tf_op jit(solution)/shard_map/ppermute | solution.py:40
  84.1 7.0 %collective-permute-start.25 = (bf16[1,64,1024]{2,1,0:T(8,128)(2,1)S(1)}, bf16[1,64,1024]{2,1,0:T(8,128)(2,1)S(1)}, u32[]{:S(2)}, u32[]{:S(2)}) collective-permute-start(bf16[1,64,1024]{2,1,0:T(8,128)(2,1)S(1)} %slice.30), channel_id=1, source_target_pairs={{0,32},{32,64},{64,96},{96,128},{128,160},{160,192},{192,224},{224... | collective-permute-start | bytes 393224 | tf_op jit(solution)/shard_map/ppermute | solution.py:40
  85.4 5.7 %collective-permute-start.26 = (bf16[1,64,1024]{2,1,0:T(8,128)(2,1)S(1)}, bf16[1,64,1024]{2,1,0:T(8,128)(2,1)S(1)}, u32[]{:S(2)}, u32[]{:S(2)}) collective-permute-start(bf16[1,64,1024]{2,1,0:T(8,128)(2,1)S(1)} %slice.31), channel_id=1, source_target_pairs={{0,224},{32,0},{64,32},{96,64},{128,96},{160,128},{192,160},{224,1... | collective-permute-start | bytes 393224 | tf_op jit(solution)/shard_map/ppermute | solution.py:40
  87.2 1.3 %copy-start.2 = (bf16[1,128,1024]{2,1,0:T(8,128)(2,1)S(1)}, bf16[1,128,1024]{2,1,0:T(8,128)(2,1)}, u32[]{:S(2)}) copy-start(bf16[1,128,1024]{2,1,0:T(8,128)(2,1)} %copy-done.1) | copy-start | bytes 786436
  87.2 1.3 %copy-start.4 = (bf16[1,128,1024]{2,1,0:T(8,128)(2,1)S(1)}, bf16[1,128,1024]{2,1,0:T(8,128)(2,1)}, u32[]{:S(2)}) copy-start(bf16[1,128,1024]{2,1,0:T(8,128)(2,1)} %copy-done.3) | copy-start | bytes 786436
  87.2 1.3 %copy-start.6 = (bf16[1,128,1024]{2,1,0:T(8,128)(2,1)S(1)}, bf16[1,128,1024]{2,1,0:T(8,128)(2,1)}, u32[]{:S(2)}) copy-start(bf16[1,128,1024]{2,1,0:T(8,128)(2,1)} %copy-done.5) | copy-start | bytes 786436
  93.1 5.3 %collective-permute-start.29 = (f32[16,128,128]{2,1,0:T(8,128)S(1)}, f32[16,128,128]{2,1,0:T(8,128)S(1)}, u32[]{:S(2)}, u32[]{:S(2)}) collective-permute-start(f32[16,128,128]{2,1,0:T(8,128)S(1)} %slice_bitcast_fusion), channel_id=1, source_target_pairs={{0,1},{1,0},{2,3},{3,2},{4,5},{5,4},{6,7},{7,6},{8,9},{9,8},{10,11... | collective-permute-start | bytes 3145736 | tf_op jit(solution)/shard_map/ppermute | solution.py:40

commit v4 on v3

--- a/solution.py
+++ b/solution.py
@@ -97,11 +97,15 @@
 
 
 def half_kernel(core, integrals, *refs):
-    out = refs[-1]
-    done = half(core, integrals, refs[:NX], refs[NX:2 * NX])
+    (*slices, out), earlier = (refs, None) if len(refs) == 5 else (refs[:4] + refs[5:6], refs[4])
+    done = half(core, integrals, slices[:2], slices[2:])
     for p in range(AUX_HERE):
-        at = slice(p % 2 * NOCC, (p % 2 + 1) * NOCC)
-        out[p // 2, :, at] = done[p * BLOCK:(p + 1) * BLOCK]
+        at = slice(p * 2 * SLICE, (p + 1) * 2 * SLICE)
+        out[0, :, at] = done[p * BLOCK:(p + 1) * BLOCK]
+        if earlier is not None:
+            refs[6][1, :, at] = done[p * BLOCK:(p + 1) * BLOCK]
+    if earlier is not None:
+        refs[6][0] = earlier[0]
 
 
 def place_of(place, offset):
@@ -208,10 +212,14 @@
         [info], gathered,
     )
     slices = [picked] + [shift(picked, "x", NX, d) for d in (1, 3, 2)]
-    halfway = call(
-        half_kernel, bf16(2, BLOCK, 2 * CHUNK), [core_at], [loaded] + slices + [swap_cores(m) for m in slices]
-    )
-    halves = [lax.slice_in_dim(halfway, h, h + 1, axis=0) for h in range(2)]
+    others = [swap_cores(m) for m in slices]
+    chunk = bf16(1, BLOCK, 2 * CHUNK)
+    near = call(half_kernel, chunk, [core_at], [loaded] + slices[:2] + others[:2], flops=530000000)
+    far, halfway = call(
+        half_kernel, (chunk, bf16(2, BLOCK, 2 * CHUNK)), [core_at],
+        [loaded] + slices[2:] + others[2:] + [near],
+    )
+    halves = [near, far]
     ups, downs = list(halves), list(halves)
     y_a, y_b = mirrored(halfway, "y", NY, 1), mirrored(halfway, "y", NY, -1)
     y_far = mirrored(y_a, "y", NY, 1)

time: 117 us -> 116 us (level)
    pallas_call x7 -> x8, Pallas kernels: 8.89 us -> 9.06 us  [call(): pl.pallas_call(body, out_shape=out_shape, in_specs=[SMEM] * len(scalars)...]
  transfers between devices with their start and end apart: 31 -> 31, of which waited for: 14 -> 14; matrix products, arithmetic and copies ran while one was open for 0% -> 0% of each run, Pallas kernels for 3% -> 4%
where the time goes in v4:
time: 116 us
  starting transfers between devices  52.2 us (45%)
  waiting for transfers between devices  30.8 us (27%)
  blocking collectives  16.8 us (14%)
  Pallas kernels  9.21 us (8%)
  local copies, waits for them, and re-layouts  5.71 us (5%)
    ppermute x27, starting transfers between devices, shift(): return lax.ppermute(x, axis, [(i, (i + step) % size) for i in range(size)])  38.9 us
    ppermute x27, waiting for transfers between devices, shift(): return lax.ppermute(x, axis, [(i, (i + step) % size) for i in range(size)])  26 us
    all_to_all x1, blocking collectives, shards(): parts = lax.all_to_all(coded, ('y', 'x'), 0, 0, tiled=True)  16.8 us
    pallas_call x8, Pallas kernels, call(): pl.pallas_call(body, out_shape=out_shape, in_specs=[SMEM] * len(scalars)...  9.06 us
    all_to_all x1, starting transfers between devices, shards(): lax.all_to_all(jnp.broadcast_to(piece[None], (NZ, HALF_L, SLICE)), 'z', 0...  9.01 us
    all_to_all x1, waiting for transfers between devices, shards(): lax.all_to_all(jnp.broadcast_to(piece[None], (NZ, HALF_L, SLICE)), 'z', 0...  4.79 us
    ppermute x3, starting transfers between devices, mirrored(): return lax.ppermute(x, (axis, 'core'), pairs)  4.28 us
    unnamed x16, local copies, waits for them, and re-layouts  4.2 us
  transfers between devices with their start and end apart: 31, of which 14 were waited for; matrix products, arithmetic and copies ran while one was open for 0% of the time, Pallas kernels for 4%

profile of v4, /device:TPU:1, one launch (start us, length us, event | category | flops | bytes accessed | tf_op | source)
XLA Modules:
  0.0 115.7 jit_solution(349403303904566545)
XLA Ops:
  0.0 0.7 dynamic_slice.3
  0.7 0.7 broadcast_in_dim.2
  1.4 9.0 %all-to-all-start = ((bf16[8,64,128]{2,1,0:T(8,128)(2,1)}), bf16[8,64,128]{2,1,0:T(8,128)(2,1)S(1)}, u32[]{:S(2)}, u32[]{:S(2)}) async-start(bf16[8,64,128]{2,1,0:T(8,128)(2,1)} %broadcast_in_dim.2), calls=%async_computation | async-start | bytes 262144 | tf_op jit(solution)/shard_map/all_to_all | solution.py:205
  11.1 0.0 copy-start
  11.1 1.6 %copy-done = bf16[16,4,128,128]{3,2,1,0:T(8,128)(2,1)S(1)} copy-done((bf16[16,4,128,128]{3,2,1,0:T(8,128)(2,1)S(1)}, bf16[16,4,128,128]{3,2,1,0:T(8,128)(2,1)}, u32[]{:S(2)}) %copy-start) | copy-done | bytes 2097176
  12.7 0.1 shard_map.46.integrals
  12.8 0.5 copy-done.7
  13.3 0.1 pad_add_fusion.1.info
  13.4 4.8 %all-to-all-done.refs_0_ = bf16[8,64,128]{2,1,0:T(8,128)(2,1)S(1)} async-done(((bf16[8,64,128]{2,1,0:T(8,128)(2,1)}), bf16[8,64,128]{2,1,0:T(8,128)(2,1)S(1)}, u32[]{:S(2)}, u32[]{:S(2)}) %all-to-all-start) | async-done | bytes 131104 | tf_op jit(solution)/shard_map/all_to_all | solution.py:205
  18.2 1.3 %collective-permute-start = (bf16[8,64,128]{2,1,0:T(8,128)(2,1)S(1)}, bf16[8,64,128]{2,1,0:T(8,128)(2,1)S(1)}, u32[]{:S(2)}, u32[]{:S(2)}) collective-permute-start(bf16[8,64,128]{2,1,0:T(8,128)(2,1)S(1)} %all-to-all-done.refs_0_), channel_id=1, source_target_pairs={{0,8},{8,16},{16,24},{24,0},{1,9},{9,17},{17,25},{25,1},{2,10},{10... | collective-permute-start | bytes 393224 | tf_op jit(solution)/shard_map/ppermute | solution.py:40
  19.5 2.6 %collective-permute-start.1 = (bf16[8,64,128]{2,1,0:T(8,128)(2,1)S(1)}, bf16[8,64,128]{2,1,0:T(8,128)(2,1)S(1)}, u32[]{:S(2)}, u32[]{:S(2)}) collective-permute-start(bf16[8,64,128]{2,1,0:T(8,128)(2,1)S(1)} %all-to-all-done.refs_0_), channel_id=1, source_target_pairs={{0,16},{8,24},{16,0},{24,8},{1,17},{9,25},{17,1},{25,9},{2,18},{10... | collective-permute-start | bytes 393224 | tf_op jit(solution)/shard_map/ppermute | solution.py:40
  22.1 1.1 collective-permute-start.2
  23.2 0.1 collective-permute-done.refs_1_
  23.3 2.7 %collective-permute-done.1.refs_2_ = bf16[8,64,128]{2,1,0:T(8,128)(2,1)S(1)} collective-permute-done((bf16[8,64,128]{2,1,0:T(8,128)(2,1)S(1)}, bf16[8,64,128]{2,1,0:T(8,128)(2,1)S(1)}, u32[]{:S(2)}, u32[]{:S(2)}) %collective-permute-start.1) | collective-permute-done | bytes 131104 | tf_op jit(solution)/shard_map/ppermute | solution.py:40
  26.0 0.8 collective-permute-done.2.refs_3_
  26.7 0.7 shard_map.47.refs_0_
  27.5 1.3 %collective-permute-start.7 = (bf16[16,64,128]{2,1,0:T(8,128)(2,1)S(1)}, bf16[16,64,128]{2,1,0:T(8,128)(2,1)S(1)}, u32[]{:S(2)}, u32[]{:S(2)}) collective-permute-start(bf16[16,64,128]{2,1,0:T(8,128)(2,1)S(1)} %shard_map.47.refs_0_), channel_id=1, source_target_pairs={{0,2},{2,4},{4,6},{6,0},{1,3},{3,5},{5,7},{7,1},{8,10},{10,12},{12... | collective-permute-start | bytes 786440 | tf_op jit(solution)/shard_map/ppermute | solution.py:40
  28.8 1.5 %collective-permute-start.3 = (bf16[16,64,128]{2,1,0:T(8,128)(2,1)S(1)}, bf16[16,64,128]{2,1,0:T(8,128)(2,1)S(1)}, u32[]{:S(2)}, u32[]{:S(2)}) collective-permute-start(bf16[16,64,128]{2,1,0:T(8,128)(2,1)S(1)} %shard_map.47.refs_0_), channel_id=1, source_target_pairs={{0,6},{2,0},{4,2},{6,4},{1,7},{3,1},{5,3},{7,5},{8,14},{10,8},{12,... | collective-permute-start | bytes 786440 | tf_op jit(solution)/shard_map/ppermute | solution.py:40
  30.2 1.5 %collective-permute-start.4 = (bf16[16,64,128]{2,1,0:T(8,128)(2,1)S(1)}, bf16[16,64,128]{2,1,0:T(8,128)(2,1)S(1)}, u32[]{:S(2)}, u32[]{:S(2)}) collective-permute-start(bf16[16,64,128]{2,1,0:T(8,128)(2,1)S(1)} %shard_map.47.refs_0_), channel_id=1, source_target_pairs={{0,4},{2,6},{4,0},{6,2},{1,5},{3,7},{5,1},{7,3},{8,12},{10,14},{12... | collective-permute-start | bytes 786440 | tf_op jit(solution)/shard_map/ppermute | solution.py:40
  31.8 4.0 %collective-permute-start.8 = (bf16[16,64,128]{2,1,0:T(8,128)(2,1)S(1)}, bf16[16,64,128]{2,1,0:T(8,128)(2,1)S(1)}, u32[]{:S(2)}, u32[]{:S(2)}) collective-permute-start(bf16[16,64,128]{2,1,0:T(8,128)(2,1)S(1)} %shard_map.47.refs_0_), channel_id=1, source_target_pairs={{0,1},{1,0},{2,3},{3,2},{4,5},{5,4},{6,7},{7,6},{8,9},{9,8},{10,11... | collective-permute-start | bytes 786440 | tf_op jit(solution)/shard_map/ppermute | solution.py:40
  35.8 5.3 %collective-permute-start.9 = (bf16[16,64,128]{2,1,0:T(8,128)(2,1)S(1)}, bf16[16,64,128]{2,1,0:T(8,128)(2,1)S(1)}, u32[]{:S(2)}, u32[]{:S(2)}) collective-permute-start(bf16[16,64,128]{2,1,0:T(8,128)(2,1)S(1)} %collective-permute-done.7.refs_1_), channel_id=1, source_target_pairs={{0,1},{1,0},{2,3},{3,2},{4,5},{5,4},{6,7},{7,6},{8,9},{9,8},{10,11... | collective-permute-start | bytes 786440 | tf_op jit(solution)/shard_map/ppermute | solution.py:40
  41.1 0.0 collective-permute-done.3.refs_0_
  41.1 0.0 collective-permute-start.5
  41.1 0.0 collective-permute-done.4.refs_1_
  41.1 3.0 %collective-permute-start.6 = (bf16[16,64,128]{2,1,0:T(8,128)(2,1)S(1)}, bf16[16,64,128]{2,1,0:T(8,128)(2,1)S(1)}, u32[]{:S(2)}, u32[]{:S(2)}) collective-permute-start(bf16[16,64,128]{2,1,0:T(8,128)(2,1)S(1)} %collective-permute-done.4.refs_1_), channel_id=1, source_target_pairs={{0,1},{1,0},{2,3},{3,2},{4,5},{5,4},{6,7},{7,6},{8,9},{9,8},{10,11... | collective-permute-start | bytes 786440 | tf_op jit(solution)/shard_map/ppermute | solution.py:40
  44.1 0.7 shard_map.48.refs_4_
  44.8 0.4 collective-permute-done.6.refs_3_
  45.2 0.7 shard_map.49
  46.0 0.9 collective-permute-start.10
  46.9 1.8 %collective-permute-start.12 = (bf16[1,128,1024]{2,1,0:T(8,128)(2,1)S(1)}, bf16[1,128,1024]{2,1,0:T(8,128)(2,1)S(1)}, u32[]{:S(2)}, u32[]{:S(2)}) collective-permute-start(bf16[1,128,1024]{2,1,0:T(8,128)(2,1)S(1)} %get-tuple-element.18), channel_id=1, source_target_pairs={{0,224},{32,0},{64,32},{96,64},{128,96},{160,128},{192,160},{224,1... | collective-permute-start | bytes 786440 | tf_op jit(solution)/shard_map/ppermute | solution.py:40
  48.7 2.2 %collective-permute-start.14 = (bf16[2,128,1024]{2,1,0:T(8,128)(2,1)S(1)}, bf16[2,128,1024]{2,1,0:T(8,128)(2,1)S(1)}, u32[]{:S(2)}, u32[]{:S(2)}) collective-permute-start(bf16[2,128,1024]{2,1,0:T(8,128)(2,1)S(1)} %get-tuple-element.17.refs_0_), channel_id=1, source_target_pairs={{0,8},{1,25},{8,16},{9,1},{16,24},{17,9},{24,0},{25,17},{2,10},{3,... | collective-permute-start | bytes 1572872 | tf_op jit(solution)/shard_map/ppermute | solution.py:48
  51.0 3.8 %collective-permute-done.10.refs_5_ = bf16[1,128,1024]{2,1,0:T(8,128)(2,1)S(1)} collective-permute-done((bf16[1,128,1024]{2,1,0:T(8,128)(2,1)S(1)}, bf16[1,128,1024]{2,1,0:T(8,128)(2,1)S(1)}, u32[]{:S(2)}, u32[]{:S(2)}) %collective-permute-start.10) | collective-permute-done | bytes 262176 | tf_op jit(solution)/shard_map/ppermute | solution.py:40
  54.8 0.0 collective-permute-start.21
  54.8 1.5 %collective-permute-start.11 = (bf16[1,128,1024]{2,1,0:T(8,128)(2,1)S(1)}, bf16[1,128,1024]{2,1,0:T(8,128)(2,1)}, u32[]{:S(2)}, u32[]{:S(2)}) collective-permute-start(bf16[1,128,1024]{2,1,0:T(8,128)(2,1)S(1)} %collective-permute-done.10.refs_5_), channel_id=1, source_target_pairs={{0,32},{32,64},{64,96},{96,128},{128,160},{160,192},{192,224},{224... | collective-permute-start | bytes 786440 | tf_op jit(solution)/shard_map/ppermute | solution.py:40
  56.3 4.3 %collective-permute-done.17.refs_4_ = bf16[1,128,1024]{2,1,0:T(8,128)(2,1)S(1)} collective-permute-done((bf16[1,128,1024]{2,1,0:T(8,128)(2,1)S(1)}, bf16[1,128,1024]{2,1,0:T(8,128)(2,1)S(1)}, u32[]{:S(2)}, u32[]{:S(2)}) %collective-permute-start.17) | collective-permute-done | bytes 262176 | tf_op jit(solution)/shard_map/ppermute | solution.py:40
  60.6 0.7 copy-done.1
  61.2 1.5 %collective-permute-start.18 = (bf16[1,128,1024]{2,1,0:T(8,128)(2,1)S(1)}, bf16[1,128,1024]{2,1,0:T(8,128)(2,1)}, u32[]{:S(2)}, u32[]{:S(2)}) collective-permute-start(bf16[1,128,1024]{2,1,0:T(8,128)(2,1)S(1)} %collective-permute-done.17.refs_4_), channel_id=1, source_target_pairs={{0,32},{32,64},{64,96},{96,128},{128,160},{160,192},{192,224},{224... | collective-permute-start | bytes 786440 | tf_op jit(solution)/shard_map/ppermute | solution.py:40
  62.7 0.7 copy-done.3
  63.4 2.9 %collective-permute-done.11.refs_9_ = bf16[1,128,1024]{2,1,0:T(8,128)(2,1)} collective-permute-done((bf16[1,128,1024]{2,1,0:T(8,128)(2,1)S(1)}, bf16[1,128,1024]{2,1,0:T(8,128)(2,1)}, u32[]{:S(2)}, u32[]{:S(2)}) %collective-permute-start.11) | collective-permute-done | bytes 262176 | tf_op jit(solution)/shard_map/ppermute | solution.py:40
  66.3 0.7 copy-done.5
  67.0 2.1 %collective-permute-start.16 = (bf16[2,128,1024]{2,1,0:T(8,128)(2,1)S(1)}, bf16[2,128,1024]{2,1,0:T(8,128)(2,1)S(1)}, u32[]{:S(2)}, u32[]{:S(2)}) collective-permute-start(bf16[2,128,1024]{2,1,0:T(8,128)(2,1)S(1)} %collective-permute-done.14.refs_1_), channel_id=1, source_target_pairs={{0,8},{1,25},{8,16},{9,1},{16,24},{17,9},{24,0},{25,17},{2,10},{3,... | collective-permute-start | bytes 1572872 | tf_op jit(solution)/shard_map/ppermute | solution.py:48
  69.1 1.5 %collective-permute-start.20 = (bf16[1,128,1024]{2,1,0:T(8,128)(2,1)}, bf16[1,128,1024]{2,1,0:T(8,128)(2,1)S(1)}, u32[]{:S(2)}, u32[]{:S(2)}) collective-permute-start(bf16[1,128,1024]{2,1,0:T(8,128)(2,1)} %collective-permute-done.11.refs_9_), channel_id=1, source_target_pairs={{0,32},{32,64},{64,96},{96,128},{128,160},{160,192},{192,224},{224... | collective-permute-start | bytes 786440 | tf_op jit(solution)/shard_map/ppermute | solution.py:40
  70.5 1.2 %collective-permute-start.24 = (bf16[1,128,1024]{2,1,0:T(8,128)(2,1)}, bf16[1,128,1024]{2,1,0:T(8,128)(2,1)S(1)}, u32[]{:S(2)}, u32[]{:S(2)}) collective-permute-start(bf16[1,128,1024]{2,1,0:T(8,128)(2,1)} %collective-permute-done.13.refs_11_), channel_id=1, source_target_pairs={{0,224},{32,0},{64,32},{96,64},{128,96},{160,128},{192,160},{224,1... | collective-permute-start | bytes 786440 | tf_op jit(solution)/shard_map/ppermute | solution.py:40
  71.8 0.3 collective-permute-start.19
  72.0 0.4 collective-permute-done.22.refs_10_
  72.5 2.0 %collective-permute-start.23 = (bf16[1,128,1024]{2,1,0:T(8,128)(2,1)}, bf16[1,128,1024]{2,1,0:T(8,128)(2,1)S(1)}, u32[]{:S(2)}, u32[]{:S(2)}) collective-permute-start(bf16[1,128,1024]{2,1,0:T(8,128)(2,1)} %collective-permute-done.22.refs_10_), channel_id=1, source_target_pairs={{0,224},{32,0},{64,32},{96,64},{128,96},{160,128},{192,160},{224,1... | collective-permute-start | bytes 786440 | tf_op jit(solution)/shard_map/ppermute | solution.py:40
  74.4 3.4 %collective-permute-done.20.refs_5_ = bf16[1,128,1024]{2,1,0:T(8,128)(2,1)S(1)} collective-permute-done((bf16[1,128,1024]{2,1,0:T(8,128)(2,1)}, bf16[1,128,1024]{2,1,0:T(8,128)(2,1)S(1)}, u32[]{:S(2)}, u32[]{:S(2)}) %collective-permute-start.20) | collective-permute-done | bytes 262176 | tf_op jit(solution)/shard_map/ppermute | solution.py:40
  77.9 0.2 collective-permute-start.27
  78.1 1.1 collective-permute-done.24.refs_7_
  79.2 1.6 %collective-permute-start.28 = (bf16[1,64,1024]{2,1,0:T(8,128)(2,1)S(1)}, bf16[1,64,1024]{2,1,0:T(8,128)(2,1)S(1)}, u32[]{:S(2)}, u32[]{:S(2)}) collective-permute-start(bf16[1,64,1024]{2,1,0:T(8,128)(2,1)S(1)} %slice.23), channel_id=1, source_target_pairs={{0,224},{32,0},{64,32},{96,64},{128,96},{160,128},{192,160},{224,1... | collective-permute-start | bytes 393224 | tf_op jit(solution)/shard_map/ppermute | solution.py:40
  80.7 2.8 %collective-permute-done.19.refs_4_ = bf16[1,128,1024]{2,1,0:T(8,128)(2,1)S(1)} collective-permute-done((bf16[1,128,1024]{2,1,0:T(8,128)(2,1)}, bf16[1,128,1024]{2,1,0:T(8,128)(2,1)S(1)}, u32[]{:S(2)}, u32[]{:S(2)}) %collective-permute-start.19) | collective-permute-done | bytes 262176 | tf_op jit(solution)/shard_map/ppermute | solution.py:40
  83.5 0.2 collective-permute-start.25
  83.7 1.1 collective-permute-done.23.refs_6_
  84.8 1.8 %collective-permute-start.26 = (bf16[1,64,1024]{2,1,0:T(8,128)(2,1)S(1)}, bf16[1,64,1024]{2,1,0:T(8,128)(2,1)S(1)}, u32[]{:S(2)}, u32[]{:S(2)}) collective-permute-start(bf16[1,64,1024]{2,1,0:T(8,128)(2,1)S(1)} %slice.21), channel_id=1, source_target_pairs={{0,224},{32,0},{64,32},{96,64},{128,96},{160,128},{192,160},{224,1... | collective-permute-start | bytes 393224 | tf_op jit(solution)/shard_map/ppermute | solution.py:40
  86.6 0.1 pad_add_fusion.place
  86.6 1.2 %shard_map.50.refs_12_ = f32[2,16,128,128]{3,2,1,0:T(8,128)S(1)} custom-call(s32[3]{0:T(128)S(1)} %pad_add_fusion.place, bf16[2,128,1024]{2,1,0:T(8,128)(2,1)S(1)} %get-tuple-element.17.refs_0_, bf16[2,128,1024]{2,1,0:T(8,128)(2,1)S(1)} %collective-permute-done.14.refs_1_, bf16[2,128,1024]{2,1,0:T(8,128)(2,1)S(1)} %collective-permute-done.15.refs_2_, ...), custom_call_target="tpu_custom_call" | custom-call | flops 270000000 | bytes 12000000 | tf_op jit(solution)/shard_map/pallas_call | solution.py:24
  87.9 2.5 %shard_map.51.refs_12_ = f32[2,16,128,128]{3,2,1,0:T(8,128)S(1)} custom-call(s32[3]{0:T(128)S(1)} %pad_add_fusion.place, bf16[2,128,1024]{2,1,0:T(8,128)(2,1)S(1)} %get-tuple-element.17.refs_0_, bf16[2,128,1024]{2,1,0:T(8,128)(2,1)S(1)} %collective-permute-done.14.refs_1_, ...), custom_call_target="tpu_custom_call", output_to_operand_aliasing={{}: (13, {})} | custom-call | flops 1080000000 | bytes 12000000 | tf_op jit(solution)/shard_map/pallas_call | solution.py:24
  90.5 1.8 %shard_map.52.kept = f32[2,16,128,128]{3,2,1,0:T(8,128)S(1)} custom-call(s32[3]{0:T(128)S(1)} %pad_add_fusion.place, bf16[2,128,1024]{2,1,0:T(8,128)(2,1)S(1)} %get-tuple-element.17.refs_0_, bf16[2,128,1024]{2,1,0:T(8,128)(2,1)S(1)} %collective-permute-done.14.refs_1_, ...), custom_call_target="tpu_custom_call", output_to_operand_aliasing={{}: (13, {})} | custom-call | tf_op jit(solution)/shard_map/pallas_call | solution.py:24
  92.4 0.1 slice_bitcast_fusion
  92.4 3.0 %collective-permute-start.29 = (f32[16,128,128]{2,1,0:T(8,128)S(1)}, f32[16,128,128]{2,1,0:T(8,128)S(1)}, u32[]{:S(2)}, u32[]{:S(2)}) collective-permute-start(f32[16,128,128]{2,1,0:T(8,128)S(1)} %slice_bitcast_fusion), channel_id=1, source_target_pairs={{0,1},{1,0},{2,3},{3,2},{4,5},{5,4},{6,7},{7,6},{8,9},{9,8},{10,11... | collective-permute-start | bytes 3145736 | tf_op jit(solution)/shard_map/ppermute | solution.py:40
  95.4 2.3 %collective-permute-done.29.got = f32[16,128,128]{2,1,0:T(8,128)S(1)} collective-permute-done((f32[16,128,128]{2,1,0:T(8,128)S(1)}, f32[16,128,128]{2,1,0:T(8,128)S(1)}, u32[]{:S(2)}, u32[]{:S(2)}) %collective-permute-start.29) | collective-permute-done | bytes 1048608 | tf_op jit(solution)/shard_map/ppermute | solution.py:40
  97.7 0.4 shard_map.53
  98.1 16.8 %all_to_all.10.parts = s16[16,144,128]{2,1,0:T(8,128)(2,1)S(1)} all-to-all(s16[16,144,128]{2,1,0:T(8,128)(2,1)S(1)} %shard_map.53), channel_id=1, replica_groups=mesh['z'=8,'y'=4,'x'=4,'core'=2] {'y','x'}, dimensions={0} | all-to-all | bytes 1179648 | tf_op jit(solution)/shard_map/all_to_all | solution.py:256
  114.9 0.8 shard_map.54
  (33 shorter events, 0.1 us)
Async XLA Ops:
  1.4 16.8 %all-to-all-start = ((bf16[8,64,128]{2,1,0:T(8,128)(2,1)}), bf16[8,64,128]{2,1,0:T(8,128)(2,1)S(1)}, u32[]{:S(2)}, u32[]{:S(2)}) async-start(bf16[8,64,128]{2,1,0:T(8,128)(2,1)} %broadcast_in_dim.2), calls=%async_computation | async-start | bytes 262144 | tf_op jit(solution)/shard_map/all_to_all | solution.py:205
  11.1 1.6 %copy-start = (bf16[16,4,128,128]{3,2,1,0:T(8,128)(2,1)S(1)}, bf16[16,4,128,128]{3,2,1,0:T(8,128)(2,1)}, u32[]{:S(2)}) copy-start(bf16[16,4,128,128]{3,2,1,0:T(8,128)(2,1)} %source.1) | copy-start | bytes 6291460
  12.7 0.7 copy-start.7
  18.2 5.1 %collective-permute-start = (bf16[8,64,128]{2,1,0:T(8,128)(2,1)S(1)}, bf16[8,64,128]{2,1,0:T(8,128)(2,1)S(1)}, u32[]{:S(2)}, u32[]{:S(2)}) collective-permute-start(bf16[8,64,128]{2,1,0:T(8,128)(2,1)S(1)} %all-to-all-done.refs_0_), channel_id=1, source_target_pairs={{0,8},{8,16},{16,24},{24,0},{1,9},{9,17},{17,25},{25,1},{2,10},{10... | collective-permute-start | bytes 393224 | tf_op jit(solution)/shard_map/ppermute | solution.py:40
  19.5 6.5 %collective-permute-start.1 = (bf16[8,64,128]{2,1,0:T(8,128)(2,1)S(1)}, bf16[8,64,128]{2,1,0:T(8,128)(2,1)S(1)}, u32[]{:S(2)}, u32[]{:S(2)}) collective-permute-start(bf16[8,64,128]{2,1,0:T(8,128)(2,1)S(1)} %all-to-all-done.refs_0_), channel_id=1, source_target_pairs={{0,16},{8,24},{16,0},{24,8},{1,17},{9,25},{17,1},{25,9},{2,18},{10... | collective-permute-start | bytes 393224 | tf_op jit(solution)/shard_map/ppermute | solution.py:40
  22.1 4.6 %collective-permute-start.2 = (bf16[8,64,128]{2,1,0:T(8,128)(2,1)S(1)}, bf16[8,64,128]{2,1,0:T(8,128)(2,1)S(1)}, u32[]{:S(2)}, u32[]{:S(2)}) collective-permute-start(bf16[8,64,128]{2,1,0:T(8,128)(2,1)S(1)} %all-to-all-done.refs_0_), channel_id=1, source_target_pairs={{0,24},{8,0},{16,8},{24,16},{1,25},{9,1},{17,9},{25,17},{2,26},{10... | collective-permute-start | bytes 393224 | tf_op jit(solution)/shard_map/ppermute | solution.py:40
  27.5 8.3 %collective-permute-start.7 = (bf16[16,64,128]{2,1,0:T(8,128)(2,1)S(1)}, bf16[16,64,128]{2,1,0:T(8,128)(2,1)S(1)}, u32[]{:S(2)}, u32[]{:S(2)}) collective-permute-start(bf16[16,64,128]{2,1,0:T(8,128)(2,1)S(1)} %shard_map.47.refs_0_), channel_id=1, source_target_pairs={{0,2},{2,4},{4,6},{6,0},{1,3},{3,5},{5,7},{7,1},{8,10},{10,12},{12... | collective-permute-start | bytes 786440 | tf_op jit(solution)/shard_map/ppermute | solution.py:40
  28.8 12.4 %collective-permute-start.3 = (bf16[16,64,128]{2,1,0:T(8,128)(2,1)S(1)}, bf16[16,64,128]{2,1,0:T(8,128)(2,1)S(1)}, u32[]{:S(2)}, u32[]{:S(2)}) collective-permute-start(bf16[16,64,128]{2,1,0:T(8,128)(2,1)S(1)} %shard_map.47.refs_0_), channel_id=1, source_target_pairs={{0,6},{2,0},{4,2},{6,4},{1,7},{3,1},{5,3},{7,5},{8,14},{10,8},{12,... | collective-permute-start | bytes 786440 | tf_op jit(solution)/shard_map/ppermute | solution.py:40
  30.2 10.9 %collective-permute-start.4 = (bf16[16,64,128]{2,1,0:T(8,128)(2,1)S(1)}, bf16[16,64,128]{2,1,0:T(8,128)(2,1)S(1)}, u32[]{:S(2)}, u32[]{:S(2)}) collective-permute-start(bf16[16,64,128]{2,1,0:T(8,128)(2,1)S(1)} %shard_map.47.refs_0_), channel_id=1, source_target_pairs={{0,4},{2,6},{4,0},{6,2},{1,5},{3,7},{5,1},{7,3},{8,12},{10,14},{12... | collective-permute-start | bytes 786440 | tf_op jit(solution)/shard_map/ppermute | solution.py:40
  31.8 12.3 %collective-permute-start.8 = (bf16[16,64,128]{2,1,0:T(8,128)(2,1)S(1)}, bf16[16,64,128]{2,1,0:T(8,128)(2,1)S(1)}, u32[]{:S(2)}, u32[]{:S(2)}) collective-permute-start(bf16[16,64,128]{2,1,0:T(8,128)(2,1)S(1)} %shard_map.47.refs_0_), channel_id=1, source_target_pairs={{0,1},{1,0},{2,3},{3,2},{4,5},{5,4},{6,7},{7,6},{8,9},{9,8},{10,11... | collective-permute-start | bytes 786440 | tf_op jit(solution)/shard_map/ppermute | solution.py:40
  35.8 8.3 %collective-permute-start.9 = (bf16[16,64,128]{2,1,0:T(8,128)(2,1)S(1)}, bf16[16,64,128]{2,1,0:T(8,128)(2,1)S(1)}, u32[]{:S(2)}, u32[]{:S(2)}) collective-permute-start(bf16[16,64,128]{2,1,0:T(8,128)(2,1)S(1)} %collective-permute-done.7.refs_1_), channel_id=1, source_target_pairs={{0,1},{1,0},{2,3},{3,2},{4,5},{5,4},{6,7},{7,6},{8,9},{9,8},{10,11... | collective-permute-start | bytes 786440 | tf_op jit(solution)/shard_map/ppermute | solution.py:40
  41.1 3.7 %collective-permute-start.5 = (bf16[16,64,128]{2,1,0:T(8,128)(2,1)S(1)}, bf16[16,64,128]{2,1,0:T(8,128)(2,1)S(1)}, u32[]{:S(2)}, u32[]{:S(2)}) collective-permute-start(bf16[16,64,128]{2,1,0:T(8,128)(2,1)S(1)} %collective-permute-done.3.refs_0_), channel_id=1, source_target_pairs={{0,1},{1,0},{2,3},{3,2},{4,5},{5,4},{6,7},{7,6},{8,9},{9,8},{10,11... | collective-permute-start | bytes 786440 | tf_op jit(solution)/shard_map/ppermute | solution.py:40
  41.1 4.1 %collective-permute-start.6 = (bf16[16,64,128]{2,1,0:T(8,128)(2,1)S(1)}, bf16[16,64,128]{2,1,0:T(8,128)(2,1)S(1)}, u32[]{:S(2)}, u32[]{:S(2)}) collective-permute-start(bf16[16,64,128]{2,1,0:T(8,128)(2,1)S(1)} %collective-permute-done.4.refs_1_), channel_id=1, source_target_pairs={{0,1},{1,0},{2,3},{3,2},{4,5},{5,4},{6,7},{7,6},{8,9},{9,8},{10,11... | collective-permute-start | bytes 786440 | tf_op jit(solution)/shard_map/ppermute | solution.py:40
  46.0 8.8 %collective-permute-start.10 = (bf16[1,128,1024]{2,1,0:T(8,128)(2,1)S(1)}, bf16[1,128,1024]{2,1,0:T(8,128)(2,1)S(1)}, u32[]{:S(2)}, u32[]{:S(2)}) collective-permute-start(bf16[1,128,1024]{2,1,0:T(8,128)(2,1)S(1)} %get-tuple-element.18), channel_id=1, source_target_pairs={{0,32},{32,64},{64,96},{96,128},{128,160},{160,192},{192,224},{224... | collective-permute-start | bytes 786440 | tf_op jit(solution)/shard_map/ppermute | solution.py:40
  46.9 7.9 %collective-permute-start.12 = (bf16[1,128,1024]{2,1,0:T(8,128)(2,1)S(1)}, bf16[1,128,1024]{2,1,0:T(8,128)(2,1)S(1)}, u32[]{:S(2)}, u32[]{:S(2)}) collective-permute-start(bf16[1,128,1024]{2,1,0:T(8,128)(2,1)S(1)} %get-tuple-element.18), channel_id=1, source_target_pairs={{0,224},{32,0},{64,32},{96,64},{128,96},{160,128},{192,160},{224,1... | collective-permute-start | bytes 786440 | tf_op jit(solution)/shard_map/ppermute | solution.py:40
  48.7 18.3 %collective-permute-start.14 = (bf16[2,128,1024]{2,1,0:T(8,128)(2,1)S(1)}, bf16[2,128,1024]{2,1,0:T(8,128)(2,1)S(1)}, u32[]{:S(2)}, u32[]{:S(2)}) collective-permute-start(bf16[2,128,1024]{2,1,0:T(8,128)(2,1)S(1)} %get-tuple-element.17.refs_0_), channel_id=1, source_target_pairs={{0,8},{1,25},{8,16},{9,1},{16,24},{17,9},{24,0},{25,17},{2,10},{3,... | collective-permute-start | bytes 1572872 | tf_op jit(solution)/shard_map/ppermute | solution.py:48
  51.0 9.6 %collective-permute-start.17 = (bf16[1,128,1024]{2,1,0:T(8,128)(2,1)S(1)}, bf16[1,128,1024]{2,1,0:T(8,128)(2,1)S(1)}, u32[]{:S(2)}, u32[]{:S(2)}) collective-permute-start(bf16[1,128,1024]{2,1,0:T(8,128)(2,1)S(1)} %shard_map.48.refs_4_), channel_id=1, source_target_pairs={{0,32},{32,64},{64,96},{96,128},{128,160},{160,192},{192,224},{224... | collective-permute-start | bytes 786440 | tf_op jit(solution)/shard_map/ppermute | solution.py:40
  51.0 18.1 %collective-permute-start.15 = (bf16[2,128,1024]{2,1,0:T(8,128)(2,1)S(1)}, bf16[2,128,1024]{2,1,0:T(8,128)(2,1)S(1)}, u32[]{:S(2)}, u32[]{:S(2)}) collective-permute-start(bf16[2,128,1024]{2,1,0:T(8,128)(2,1)S(1)} %get-tuple-element.17.refs_0_), channel_id=1, source_target_pairs={{0,24},{1,9},{8,0},{9,17},{16,8},{17,25},{24,16},{25,1},{2,26},{3,... | collective-permute-start | bytes 1572872 | tf_op jit(solution)/shard_map/ppermute | solution.py:48
  54.8 6.5 %collective-permute-start.21 = (bf16[1,128,1024]{2,1,0:T(8,128)(2,1)S(1)}, bf16[1,128,1024]{2,1,0:T(8,128)(2,1)S(1)}, u32[]{:S(2)}, u32[]{:S(2)}) collective-permute-start(bf16[1,128,1024]{2,1,0:T(8,128)(2,1)S(1)} %shard_map.48.refs_4_), channel_id=1, source_target_pairs={{0,224},{32,0},{64,32},{96,64},{128,96},{160,128},{192,160},{224,1... | collective-permute-start | bytes 786440 | tf_op jit(solution)/shard_map/ppermute | solution.py:40
  54.8 11.5 %collective-permute-start.11 = (bf16[1,128,1024]{2,1,0:T(8,128)(2,1)S(1)}, bf16[1,128,1024]{2,1,0:T(8,128)(2,1)}, u32[]{:S(2)}, u32[]{:S(2)}) collective-permute-start(bf16[1,128,1024]{2,1,0:T(8,128)(2,1)S(1)} %collective-permute-done.10.refs_5_), channel_id=1, source_target_pairs={{0,32},{32,64},{64,96},{96,128},{128,160},{160,192},{192,224},{224... | collective-permute-start | bytes 786440 | tf_op jit(solution)/shard_map/ppermute | solution.py:40
  60.6 8.5 %collective-permute-start.13 = (bf16[1,128,1024]{2,1,0:T(8,128)(2,1)S(1)}, bf16[1,128,1024]{2,1,0:T(8,128)(2,1)}, u32[]{:S(2)}, u32[]{:S(2)}) collective-permute-start(bf16[1,128,1024]{2,1,0:T(8,128)(2,1)S(1)} %collective-permute-done.12.refs_7_), channel_id=1, source_target_pairs={{0,224},{32,0},{64,32},{96,64},{128,96},{160,128},{192,160},{224,1... | collective-permute-start | bytes 786440 | tf_op jit(solution)/shard_map/ppermute | solution.py:40
  60.6 0.7 copy-start.1
  61.2 10.5 %collective-permute-start.18 = (bf16[1,128,1024]{2,1,0:T(8,128)(2,1)S(1)}, bf16[1,128,1024]{2,1,0:T(8,128)(2,1)}, u32[]{:S(2)}, u32[]{:S(2)}) collective-permute-start(bf16[1,128,1024]{2,1,0:T(8,128)(2,1)S(1)} %collective-permute-done.17.refs_4_), channel_id=1, source_target_pairs={{0,32},{32,64},{64,96},{96,128},{128,160},{160,192},{192,224},{224... | collective-permute-start | bytes 786440 | tf_op jit(solution)/shard_map/ppermute | solution.py:40
  62.7 0.7 copy-start.3
  66.3 6.2 %collective-permute-start.22 = (bf16[1,128,1024]{2,1,0:T(8,128)(2,1)S(1)}, bf16[1,128,1024]{2,1,0:T(8,128)(2,1)}, u32[]{:S(2)}, u32[]{:S(2)}) collective-permute-start(bf16[1,128,1024]{2,1,0:T(8,128)(2,1)S(1)} %collective-permute-done.21.refs_6_), channel_id=1, source_target_pairs={{0,224},{32,0},{64,32},{96,64},{128,96},{160,128},{192,160},{224,1... | collective-permute-start | bytes 786440 | tf_op jit(solution)/shard_map/ppermute | solution.py:40
  66.3 0.7 copy-start.5
  67.0 19.6 %collective-permute-start.16 = (bf16[2,128,1024]{2,1,0:T(8,128)(2,1)S(1)}, bf16[2,128,1024]{2,1,0:T(8,128)(2,1)S(1)}, u32[]{:S(2)}, u32[]{:S(2)}) collective-permute-start(bf16[2,128,1024]{2,1,0:T(8,128)(2,1)S(1)} %collective-permute-done.14.refs_1_), channel_id=1, source_target_pairs={{0,8},{1,25},{8,16},{9,1},{16,24},{17,9},{24,0},{25,17},{2,10},{3,... | collective-permute-start | bytes 1572872 | tf_op jit(solution)/shard_map/ppermute | solution.py:48
  69.1 8.8 %collective-permute-start.20 = (bf16[1,128,1024]{2,1,0:T(8,128)(2,1)}, bf16[1,128,1024]{2,1,0:T(8,128)(2,1)S(1)}, u32[]{:S(2)}, u32[]{:S(2)}) collective-permute-start(bf16[1,128,1024]{2,1,0:T(8,128)(2,1)} %collective-permute-done.11.refs_9_), channel_id=1, source_target_pairs={{0,32},{32,64},{64,96},{96,128},{128,160},{160,192},{192,224},{224... | collective-permute-start | bytes 786440 | tf_op jit(solution)/shard_map/ppermute | solution.py:40
  70.5 8.6 %collective-permute-start.24 = (bf16[1,128,1024]{2,1,0:T(8,128)(2,1)}, bf16[1,128,1024]{2,1,0:T(8,128)(2,1)S(1)}, u32[]{:S(2)}, u32[]{:S(2)}) collective-permute-start(bf16[1,128,1024]{2,1,0:T(8,128)(2,1)} %collective-permute-done.13.refs_11_), channel_id=1, source_target_pairs={{0,224},{32,0},{64,32},{96,64},{128,96},{160,128},{192,160},{224,1... | collective-permute-start | bytes 786440 | tf_op jit(solution)/shard_map/ppermute | solution.py:40
  71.8 11.7 %collective-permute-start.19 = (bf16[1,128,1024]{2,1,0:T(8,128)(2,1)}, bf16[1,128,1024]{2,1,0:T(8,128)(2,1)S(1)}, u32[]{:S(2)}, u32[]{:S(2)}) collective-permute-start(bf16[1,128,1024]{2,1,0:T(8,128)(2,1)} %collective-permute-done.18.refs_8_), channel_id=1, source_target_pairs={{0,32},{32,64},{64,96},{96,128},{128,160},{160,192},{192,224},{224... | collective-permute-start | bytes 786440 | tf_op jit(solution)/shard_map/ppermute | solution.py:40
  72.5 12.3 %collective-permute-start.23 = (bf16[1,128,1024]{2,1,0:T(8,128)(2,1)}, bf16[1,128,1024]{2,1,0:T(8,128)(2,1)S(1)}, u32[]{:S(2)}, u32[]{:S(2)}) collective-permute-start(bf16[1,128,1024]{2,1,0:T(8,128)(2,1)} %collective-permute-done.22.refs_10_), channel_id=1, source_target_pairs={{0,224},{32,0},{64,32},{96,64},{128,96},{160,128},{192,160},{224,1... | collective-permute-start | bytes 786440 | tf_op jit(solution)/shard_map/ppermute | solution.py:40
  77.9 12.6 %collective-permute-start.27 = (bf16[1,64,1024]{2,1,0:T(8,128)(2,1)S(1)}, bf16[1,64,1024]{2,1,0:T(8,128)(2,1)S(1)}, u32[]{:S(2)}, u32[]{:S(2)}) collective-permute-start(bf16[1,64,1024]{2,1,0:T(8,128)(2,1)S(1)} %slice.22), channel_id=1, source_target_pairs={{0,32},{32,64},{64,96},{96,128},{128,160},{160,192},{192,224},{224... | collective-permute-start | bytes 393224 | tf_op jit(solution)/shard_map/ppermute | solution.py:40
  79.2 11.3 %collective-permute-start.28 = (bf16[1,64,1024]{2,1,0:T(8,128)(2,1)S(1)}, bf16[1,64,1024]{2,1,0:T(8,128)(2,1)S(1)}, u32[]{:S(2)}, u32[]{:S(2)}) collective-permute-start(bf16[1,64,1024]{2,1,0:T(8,128)(2,1)S(1)} %slice.23), channel_id=1, source_target_pairs={{0,224},{32,0},{64,32},{96,64},{128,96},{160,128},{192,160},{224,1... | collective-permute-start | bytes 393224 | tf_op jit(solution)/shard_map/ppermute | solution.py:40
  83.5 7.0 %collective-permute-start.25 = (bf16[1,64,1024]{2,1,0:T(8,128)(2,1)S(1)}, bf16[1,64,1024]{2,1,0:T(8,128)(2,1)S(1)}, u32[]{:S(2)}, u32[]{:S(2)}) collective-permute-start(bf16[1,64,1024]{2,1,0:T(8,128)(2,1)S(1)} %slice.20), channel_id=1, source_target_pairs={{0,32},{32,64},{64,96},{96,128},{128,160},{160,192},{192,224},{224... | collective-permute-start | bytes 393224 | tf_op jit(solution)/shard_map/ppermute | solution.py:40
  84.8 5.7 %collective-permute-start.26 = (bf16[1,64,1024]{2,1,0:T(8,128)(2,1)S(1)}, bf16[1,64,1024]{2,1,0:T(8,128)(2,1)S(1)}, u32[]{:S(2)}, u32[]{:S(2)}) collective-permute-start(bf16[1,64,1024]{2,1,0:T(8,128)(2,1)S(1)} %slice.21), channel_id=1, source_target_pairs={{0,224},{32,0},{64,32},{96,64},{128,96},{160,128},{192,160},{224,1... | collective-permute-start | bytes 393224 | tf_op jit(solution)/shard_map/ppermute | solution.py:40
  86.6 1.3 %copy-start.2 = (bf16[1,128,1024]{2,1,0:T(8,128)(2,1)S(1)}, bf16[1,128,1024]{2,1,0:T(8,128)(2,1)}, u32[]{:S(2)}) copy-start(bf16[1,128,1024]{2,1,0:T(8,128)(2,1)} %copy-done.1) | copy-start | bytes 786436
  86.6 1.3 %copy-start.4 = (bf16[1,128,1024]{2,1,0:T(8,128)(2,1)S(1)}, bf16[1,128,1024]{2,1,0:T(8,128)(2,1)}, u32[]{:S(2)}) copy-start(bf16[1,128,1024]{2,1,0:T(8,128)(2,1)} %copy-done.3) | copy-start | bytes 786436
  86.6 1.3 %copy-start.6 = (bf16[1,128,1024]{2,1,0:T(8,128)(2,1)S(1)}, bf16[1,128,1024]{2,1,0:T(8,128)(2,1)}, u32[]{:S(2)}) copy-start(bf16[1,128,1024]{2,1,0:T(8,128)(2,1)} %copy-done.5) | copy-start | bytes 786436
  92.4 5.3 %collective-permute-start.29 = (f32[16,128,128]{2,1,0:T(8,128)S(1)}, f32[16,128,128]{2,1,0:T(8,128)S(1)}, u32[]{:S(2)}, u32[]{:S(2)}) collective-permute-start(f32[16,128,128]{2,1,0:T(8,128)S(1)} %slice_bitcast_fusion), channel_id=1, source_target_pairs={{0,1},{1,0},{2,3},{3,2},{4,5},{5,4},{6,7},{7,6},{8,9},{9,8},{10,11... | collective-permute-start | bytes 3145736 | tf_op jit(solution)/shard_map/ppermute | solution.py:40

commit v5 on v4

--- a/solution.py
+++ b/solution.py
@@ -103,9 +103,9 @@
         at = slice(p * 2 * SLICE, (p + 1) * 2 * SLICE)
         out[0, :, at] = done[p * BLOCK:(p + 1) * BLOCK]
         if earlier is not None:
-            refs[6][1, :, at] = done[p * BLOCK:(p + 1) * BLOCK]
+            refs[6][0, :, at] = done[p * BLOCK:(p + 1) * BLOCK]
     if earlier is not None:
-        refs[6][0] = earlier[0]
+        refs[6][1] = earlier[0]
 
 
 def place_of(place, offset):
@@ -219,7 +219,7 @@
         half_kernel, (chunk, bf16(2, BLOCK, 2 * CHUNK)), [core_at],
         [loaded] + slices[2:] + others[2:] + [near],
     )
-    halves = [near, far]
+    halves = [far, near]
     ups, downs = list(halves), list(halves)
     y_a, y_b = mirrored(halfway, "y", NY, 1), mirrored(halfway, "y", NY, -1)
     y_far = mirrored(y_a, "y", NY, 1)
@@ -228,7 +228,7 @@
         for h in range(2):
             up, down = shift(ups[h], "z", NZ, 1), shift(downs[h], "z", NZ, -1)
             if h == 1 and step == 1:
-                up, down, y_a, y_b = lax.optimization_barrier((up, down, y_a, y_b))
+                up, down, y_b = lax.optimization_barrier((up, down, y_b))
             ups[h], downs[h] = up, down
         columns.append([(ups[0], ups[1]), (downs[0], downs[1])])
     last = []

time: 116 us -> 116 us (level)
  starting transfers between devices: 52.2 us -> 55.7 us
  waiting for transfers between devices: 30.8 us -> 28.1 us
    ppermute x27, starting transfers between devices: 38.9 us -> 43.8 us  [shift(): return lax.ppermute(x, axis, [(i, (i + step) % size) for i in range(size)])]
    ppermute x27, waiting for transfers between devices: 26 us -> 23.3 us  [shift(): return lax.ppermute(x, axis, [(i, (i + step) % size) for i in range(size)])]
    ppermute x3, starting transfers between devices: 4.28 us -> 2.83 us  [mirrored(): return lax.ppermute(x, (axis, 'core'), pairs)]
  transfers between devices with their start and end apart: 31 -> 31, of which waited for: 14 -> 13; matrix products, arithmetic and copies ran while one was open for 0% -> 0% of each run, Pallas kernels for 4% -> 5%
where the time goes in v5:
time: 116 us
  starting transfers between devices  55.7 us (48%)
  waiting for transfers between devices  28.1 us (24%)
  blocking collectives  16.4 us (14%)
  Pallas kernels  9.22 us (8%)
  local copies, waits for them, and re-layouts  5.71 us (5%)
    ppermute x27, starting transfers between devices, shift(): return lax.ppermute(x, axis, [(i, (i + step) % size) for i in range(size)])  43.8 us
    ppermute x27, waiting for transfers between devices, shift(): return lax.ppermute(x, axis, [(i, (i + step) % size) for i in range(size)])  23.3 us
    all_to_all x1, blocking collectives, shards(): parts = lax.all_to_all(coded, ('y', 'x'), 0, 0, tiled=True)  16.4 us
    pallas_call x8, Pallas kernels, call(): pl.pallas_call(body, out_shape=out_shape, in_specs=[SMEM] * len(scalars)...  9.07 us
    all_to_all x1, starting transfers between devices, shards(): lax.all_to_all(jnp.broadcast_to(piece[None], (NZ, HALF_L, SLICE)), 'z', 0...  9.01 us
    all_to_all x1, waiting for transfers between devices, shards(): lax.all_to_all(jnp.broadcast_to(piece[None], (NZ, HALF_L, SLICE)), 'z', 0...  4.79 us
    unnamed x16, local copies, waits for them, and re-layouts  4.2 us
    ppermute x3, starting transfers between devices, mirrored(): return lax.ppermute(x, (axis, 'core'), pairs)  2.83 us
  transfers between devices with their start and end apart: 31, of which 13 were waited for; matrix products, arithmetic and copies ran while one was open for 0% of the time, Pallas kernels for 5%

profile of v5, /device:TPU:1, one launch (start us, length us, event | category | flops | bytes accessed | tf_op | source)
XLA Modules:
  0.0 116.1 jit_solution(17719419299310911203)
XLA Ops:
  0.0 0.7 dynamic_slice.3
  0.7 0.7 broadcast_in_dim.2
  1.4 9.0 %all-to-all-start = ((bf16[8,64,128]{2,1,0:T(8,128)(2,1)}), bf16[8,64,128]{2,1,0:T(8,128)(2,1)S(1)}, u32[]{:S(2)}, u32[]{:S(2)}) async-start(bf16[8,64,128]{2,1,0:T(8,128)(2,1)} %broadcast_in_dim.2), calls=%async_computation | async-start | bytes 262144 | tf_op jit(solution)/shard_map/all_to_all | solution.py:205
  11.1 0.0 copy-start
  11.1 1.6 %copy-done = bf16[16,4,128,128]{3,2,1,0:T(8,128)(2,1)S(1)} copy-done((bf16[16,4,128,128]{3,2,1,0:T(8,128)(2,1)S(1)}, bf16[16,4,128,128]{3,2,1,0:T(8,128)(2,1)}, u32[]{:S(2)}) %copy-start) | copy-done | bytes 2097176
  12.7 0.1 shard_map.46.integrals
  12.8 0.5 copy-done.7
  13.3 0.1 pad_add_fusion.1.info
  13.4 4.8 %all-to-all-done.refs_0_ = bf16[8,64,128]{2,1,0:T(8,128)(2,1)S(1)} async-done(((bf16[8,64,128]{2,1,0:T(8,128)(2,1)}), bf16[8,64,128]{2,1,0:T(8,128)(2,1)S(1)}, u32[]{:S(2)}, u32[]{:S(2)}) %all-to-all-start) | async-done | bytes 131104 | tf_op jit(solution)/shard_map/all_to_all | solution.py:205
  18.2 1.3 %collective-permute-start = (bf16[8,64,128]{2,1,0:T(8,128)(2,1)S(1)}, bf16[8,64,128]{2,1,0:T(8,128)(2,1)S(1)}, u32[]{:S(2)}, u32[]{:S(2)}) collective-permute-start(bf16[8,64,128]{2,1,0:T(8,128)(2,1)S(1)} %all-to-all-done.refs_0_), channel_id=1, source_target_pairs={{0,8},{8,16},{16,24},{24,0},{1,9},{9,17},{17,25},{25,1},{2,10},{10... | collective-permute-start | bytes 393224 | tf_op jit(solution)/shard_map/ppermute | solution.py:40
  19.5 2.6 %collective-permute-start.1 = (bf16[8,64,128]{2,1,0:T(8,128)(2,1)S(1)}, bf16[8,64,128]{2,1,0:T(8,128)(2,1)S(1)}, u32[]{:S(2)}, u32[]{:S(2)}) collective-permute-start(bf16[8,64,128]{2,1,0:T(8,128)(2,1)S(1)} %all-to-all-done.refs_0_), channel_id=1, source_target_pairs={{0,16},{8,24},{16,0},{24,8},{1,17},{9,25},{17,1},{25,9},{2,18},{10... | collective-permute-start | bytes 393224 | tf_op jit(solution)/shard_map/ppermute | solution.py:40
  22.1 1.1 collective-permute-start.2
  23.2 0.1 collective-permute-done.refs_1_
  23.3 2.7 %collective-permute-done.1.refs_2_ = bf16[8,64,128]{2,1,0:T(8,128)(2,1)S(1)} collective-permute-done((bf16[8,64,128]{2,1,0:T(8,128)(2,1)S(1)}, bf16[8,64,128]{2,1,0:T(8,128)(2,1)S(1)}, u32[]{:S(2)}, u32[]{:S(2)}) %collective-permute-start.1) | collective-permute-done | bytes 131104 | tf_op jit(solution)/shard_map/ppermute | solution.py:40
  26.0 0.8 collective-permute-done.2.refs_3_
  26.7 0.7 shard_map.47.refs_0_
  27.5 1.3 %collective-permute-start.7 = (bf16[16,64,128]{2,1,0:T(8,128)(2,1)S(1)}, bf16[16,64,128]{2,1,0:T(8,128)(2,1)S(1)}, u32[]{:S(2)}, u32[]{:S(2)}) collective-permute-start(bf16[16,64,128]{2,1,0:T(8,128)(2,1)S(1)} %shard_map.47.refs_0_), channel_id=1, source_target_pairs={{0,2},{2,4},{4,6},{6,0},{1,3},{3,5},{5,7},{7,1},{8,10},{10,12},{12... | collective-permute-start | bytes 786440 | tf_op jit(solution)/shard_map/ppermute | solution.py:40
  28.8 1.5 %collective-permute-start.3 = (bf16[16,64,128]{2,1,0:T(8,128)(2,1)S(1)}, bf16[16,64,128]{2,1,0:T(8,128)(2,1)S(1)}, u32[]{:S(2)}, u32[]{:S(2)}) collective-permute-start(bf16[16,64,128]{2,1,0:T(8,128)(2,1)S(1)} %shard_map.47.refs_0_), channel_id=1, source_target_pairs={{0,6},{2,0},{4,2},{6,4},{1,7},{3,1},{5,3},{7,5},{8,14},{10,8},{12,... | collective-permute-start | bytes 786440 | tf_op jit(solution)/shard_map/ppermute | solution.py:40
  30.2 1.5 %collective-permute-start.4 = (bf16[16,64,128]{2,1,0:T(8,128)(2,1)S(1)}, bf16[16,64,128]{2,1,0:T(8,128)(2,1)S(1)}, u32[]{:S(2)}, u32[]{:S(2)}) collective-permute-start(bf16[16,64,128]{2,1,0:T(8,128)(2,1)S(1)} %shard_map.47.refs_0_), channel_id=1, source_target_pairs={{0,4},{2,6},{4,0},{6,2},{1,5},{3,7},{5,1},{7,3},{8,12},{10,14},{12... | collective-permute-start | bytes 786440 | tf_op jit(solution)/shard_map/ppermute | solution.py:40
  31.8 4.0 %collective-permute-start.8 = (bf16[16,64,128]{2,1,0:T(8,128)(2,1)S(1)}, bf16[16,64,128]{2,1,0:T(8,128)(2,1)S(1)}, u32[]{:S(2)}, u32[]{:S(2)}) collective-permute-start(bf16[16,64,128]{2,1,0:T(8,128)(2,1)S(1)} %shard_map.47.refs_0_), channel_id=1, source_target_pairs={{0,1},{1,0},{2,3},{3,2},{4,5},{5,4},{6,7},{7,6},{8,9},{9,8},{10,11... | collective-permute-start | bytes 786440 | tf_op jit(solution)/shard_map/ppermute | solution.py:40
  35.8 0.0 collective-permute-done.7.refs_1_
  35.8 5.3 %collective-permute-start.9 = (bf16[16,64,128]{2,1,0:T(8,128)(2,1)S(1)}, bf16[16,64,128]{2,1,0:T(8,128)(2,1)S(1)}, u32[]{:S(2)}, u32[]{:S(2)}) collective-permute-start(bf16[16,64,128]{2,1,0:T(8,128)(2,1)S(1)} %collective-permute-done.7.refs_1_), channel_id=1, source_target_pairs={{0,1},{1,0},{2,3},{3,2},{4,5},{5,4},{6,7},{7,6},{8,9},{9,8},{10,11... | collective-permute-start | bytes 786440 | tf_op jit(solution)/shard_map/ppermute | solution.py:40
  41.1 0.0 collective-permute-start.5
  41.1 3.0 %collective-permute-start.6 = (bf16[16,64,128]{2,1,0:T(8,128)(2,1)S(1)}, bf16[16,64,128]{2,1,0:T(8,128)(2,1)S(1)}, u32[]{:S(2)}, u32[]{:S(2)}) collective-permute-start(bf16[16,64,128]{2,1,0:T(8,128)(2,1)S(1)} %collective-permute-done.4.refs_1_), channel_id=1, source_target_pairs={{0,1},{1,0},{2,3},{3,2},{4,5},{5,4},{6,7},{7,6},{8,9},{9,8},{10,11... | collective-permute-start | bytes 786440 | tf_op jit(solution)/shard_map/ppermute | solution.py:40
  44.1 0.7 shard_map.48.refs_4_
  44.8 0.9 collective-permute-start.11
  45.8 0.7 shard_map.49
  46.5 0.1 collective-permute-start.15
  46.6 2.7 %collective-permute-start.10 = (bf16[2,128,1024]{2,1,0:T(8,128)(2,1)S(1)}, bf16[2,128,1024]{2,1,0:T(8,128)(2,1)S(1)}, u32[]{:S(2)}, u32[]{:S(2)}) collective-permute-start(bf16[2,128,1024]{2,1,0:T(8,128)(2,1)S(1)} %get-tuple-element.16.refs_0_), channel_id=1, source_target_pairs={{0,8},{1,25},{8,16},{9,1},{16,24},{17,9},{24,0},{25,17},{2,10},{3,... | collective-permute-start | bytes 1572872 | tf_op jit(solution)/shard_map/ppermute | solution.py:48
  49.3 1.9 %collective-permute-start.13 = (bf16[1,128,1024]{2,1,0:T(8,128)(2,1)S(1)}, bf16[1,128,1024]{2,1,0:T(8,128)(2,1)S(1)}, u32[]{:S(2)}, u32[]{:S(2)}) collective-permute-start(bf16[1,128,1024]{2,1,0:T(8,128)(2,1)S(1)} %shard_map.48.refs_4_), channel_id=1, source_target_pairs={{0,224},{32,0},{64,32},{96,64},{128,96},{160,128},{192,160},{224,1... | collective-permute-start | bytes 786440 | tf_op jit(solution)/shard_map/ppermute | solution.py:40
  51.1 2.9 %collective-permute-done.11.refs_5_ = bf16[1,128,1024]{2,1,0:T(8,128)(2,1)S(1)} collective-permute-done((bf16[1,128,1024]{2,1,0:T(8,128)(2,1)S(1)}, bf16[1,128,1024]{2,1,0:T(8,128)(2,1)S(1)}, u32[]{:S(2)}, u32[]{:S(2)}) %collective-permute-start.11) | collective-permute-done | bytes 262176 | tf_op jit(solution)/shard_map/ppermute | solution.py:40
  54.1 0.0 collective-permute-start.21
  54.1 3.1 %collective-permute-done.13.refs_7_ = bf16[1,128,1024]{2,1,0:T(8,128)(2,1)S(1)} collective-permute-done((bf16[1,128,1024]{2,1,0:T(8,128)(2,1)S(1)}, bf16[1,128,1024]{2,1,0:T(8,128)(2,1)S(1)}, u32[]{:S(2)}, u32[]{:S(2)}) %collective-permute-start.13) | collective-permute-done | bytes 262176 | tf_op jit(solution)/shard_map/ppermute | solution.py:40
  57.1 0.2 collective-permute-start.12
  57.3 2.5 %collective-permute-done.17.refs_4_ = bf16[1,128,1024]{2,1,0:T(8,128)(2,1)S(1)} collective-permute-done((bf16[1,128,1024]{2,1,0:T(8,128)(2,1)S(1)}, bf16[1,128,1024]{2,1,0:T(8,128)(2,1)S(1)}, u32[]{:S(2)}, u32[]{:S(2)}) %collective-permute-start.17) | collective-permute-done | bytes 262176 | tf_op jit(solution)/shard_map/ppermute | solution.py:40
  59.8 0.3 collective-permute-start.14
  60.2 0.7 copy-done.1
  60.9 1.9 %collective-permute-done.21.refs_6_ = bf16[1,128,1024]{2,1,0:T(8,128)(2,1)S(1)} collective-permute-done((bf16[1,128,1024]{2,1,0:T(8,128)(2,1)S(1)}, bf16[1,128,1024]{2,1,0:T(8,128)(2,1)S(1)}, u32[]{:S(2)}, u32[]{:S(2)}) %collective-permute-start.21) | collective-permute-done | bytes 262176 | tf_op jit(solution)/shard_map/ppermute | solution.py:40
  62.8 0.3 collective-permute-start.18
  63.1 0.7 copy-done.3
  63.8 2.7 %collective-permute-start.22 = (bf16[1,128,1024]{2,1,0:T(8,128)(2,1)S(1)}, bf16[1,128,1024]{2,1,0:T(8,128)(2,1)}, u32[]{:S(2)}, u32[]{:S(2)}) collective-permute-start(bf16[1,128,1024]{2,1,0:T(8,128)(2,1)S(1)} %collective-permute-done.21.refs_6_), channel_id=1, source_target_pairs={{0,224},{32,0},{64,32},{96,64},{128,96},{160,128},{192,160},{224,1... | collective-permute-start | bytes 786440 | tf_op jit(solution)/shard_map/ppermute | solution.py:40
  66.5 0.7 copy-done.5
  67.2 0.1 collective-permute-start.16
  67.3 0.7 collective-permute-done.14.refs_11_
  68.0 0.7 collective-permute-start.20
  68.7 2.8 %collective-permute-start.24 = (bf16[1,128,1024]{2,1,0:T(8,128)(2,1)}, bf16[1,128,1024]{2,1,0:T(8,128)(2,1)S(1)}, u32[]{:S(2)}, u32[]{:S(2)}) collective-permute-start(bf16[1,128,1024]{2,1,0:T(8,128)(2,1)} %collective-permute-done.14.refs_11_), channel_id=1, source_target_pairs={{0,224},{32,0},{64,32},{96,64},{128,96},{160,128},{192,160},{224,1... | collective-permute-start | bytes 786440 | tf_op jit(solution)/shard_map/ppermute | solution.py:40
  71.5 2.1 %collective-permute-done.22.refs_10_ = bf16[1,128,1024]{2,1,0:T(8,128)(2,1)} collective-permute-done((bf16[1,128,1024]{2,1,0:T(8,128)(2,1)S(1)}, bf16[1,128,1024]{2,1,0:T(8,128)(2,1)}, u32[]{:S(2)}, u32[]{:S(2)}) %collective-permute-start.22) | collective-permute-done | bytes 262176 | tf_op jit(solution)/shard_map/ppermute | solution.py:40
  73.6 3.5 %collective-permute-start.23 = (bf16[1,128,1024]{2,1,0:T(8,128)(2,1)}, bf16[1,128,1024]{2,1,0:T(8,128)(2,1)S(1)}, u32[]{:S(2)}, u32[]{:S(2)}) collective-permute-start(bf16[1,128,1024]{2,1,0:T(8,128)(2,1)} %collective-permute-done.22.refs_10_), channel_id=1, source_target_pairs={{0,224},{32,0},{64,32},{96,64},{128,96},{160,128},{192,160},{224,1... | collective-permute-start | bytes 786440 | tf_op jit(solution)/shard_map/ppermute | solution.py:40
  77.1 0.1 collective-permute-start.27
  77.2 2.1 %collective-permute-done.24.refs_7_ = bf16[1,128,1024]{2,1,0:T(8,128)(2,1)S(1)} collective-permute-done((bf16[1,128,1024]{2,1,0:T(8,128)(2,1)}, bf16[1,128,1024]{2,1,0:T(8,128)(2,1)S(1)}, u32[]{:S(2)}, u32[]{:S(2)}) %collective-permute-start.24) | collective-permute-done | bytes 262176 | tf_op jit(solution)/shard_map/ppermute | solution.py:40
  79.3 3.4 %collective-permute-start.28 = (bf16[1,64,1024]{2,1,0:T(8,128)(2,1)S(1)}, bf16[1,64,1024]{2,1,0:T(8,128)(2,1)S(1)}, u32[]{:S(2)}, u32[]{:S(2)}) collective-permute-start(bf16[1,64,1024]{2,1,0:T(8,128)(2,1)S(1)} %slice.23), channel_id=1, source_target_pairs={{0,224},{32,0},{64,32},{96,64},{128,96},{160,128},{192,160},{224,1... | collective-permute-start | bytes 393224 | tf_op jit(solution)/shard_map/ppermute | solution.py:40
  82.7 0.1 collective-permute-start.25
  82.8 2.1 %collective-permute-done.23.refs_6_ = bf16[1,128,1024]{2,1,0:T(8,128)(2,1)S(1)} collective-permute-done((bf16[1,128,1024]{2,1,0:T(8,128)(2,1)}, bf16[1,128,1024]{2,1,0:T(8,128)(2,1)S(1)}, u32[]{:S(2)}, u32[]{:S(2)}) %collective-permute-start.23) | collective-permute-done | bytes 262176 | tf_op jit(solution)/shard_map/ppermute | solution.py:40
  85.0 3.6 %collective-permute-start.26 = (bf16[1,64,1024]{2,1,0:T(8,128)(2,1)S(1)}, bf16[1,64,1024]{2,1,0:T(8,128)(2,1)S(1)}, u32[]{:S(2)}, u32[]{:S(2)}) collective-permute-start(bf16[1,64,1024]{2,1,0:T(8,128)(2,1)S(1)} %slice.21), channel_id=1, source_target_pairs={{0,224},{32,0},{64,32},{96,64},{128,96},{160,128},{192,160},{224,1... | collective-permute-start | bytes 393224 | tf_op jit(solution)/shard_map/ppermute | solution.py:40
  88.6 0.1 pad_add_fusion.place
  88.7 1.2 %shard_map.50.refs_12_ = f32[2,16,128,128]{3,2,1,0:T(8,128)S(1)} custom-call(s32[3]{0:T(128)S(1)} %pad_add_fusion.place, bf16[2,128,1024]{2,1,0:T(8,128)(2,1)S(1)} %get-tuple-element.16.refs_0_, bf16[2,128,1024]{2,1,0:T(8,128)(2,1)S(1)} %collective-permute-done.10.refs_1_, bf16[2,128,1024]{2,1,0:T(8,128)(2,1)S(1)} %collective-permute-done.15.refs_2_, ...), custom_call_target="tpu_custom_call" | custom-call | flops 270000000 | bytes 12000000 | tf_op jit(solution)/shard_map/pallas_call | solution.py:24
  89.9 2.5 %shard_map.51.refs_12_ = f32[2,16,128,128]{3,2,1,0:T(8,128)S(1)} custom-call(s32[3]{0:T(128)S(1)} %pad_add_fusion.place, bf16[2,128,1024]{2,1,0:T(8,128)(2,1)S(1)} %get-tuple-element.16.refs_0_, bf16[2,128,1024]{2,1,0:T(8,128)(2,1)S(1)} %collective-permute-done.10.refs_1_, ...), custom_call_target="tpu_custom_call", output_to_operand_aliasing={{}: (13, {})} | custom-call | flops 1080000000 | bytes 12000000 | tf_op jit(solution)/shard_map/pallas_call | solution.py:24
  92.5 1.8 %shard_map.52.kept = f32[2,16,128,128]{3,2,1,0:T(8,128)S(1)} custom-call(s32[3]{0:T(128)S(1)} %pad_add_fusion.place, bf16[2,128,1024]{2,1,0:T(8,128)(2,1)S(1)} %get-tuple-element.16.refs_0_, bf16[2,128,1024]{2,1,0:T(8,128)(2,1)S(1)} %collective-permute-done.10.refs_1_, ...), custom_call_target="tpu_custom_call", output_to_operand_aliasing={{}: (13, {})} | custom-call | tf_op jit(solution)/shard_map/pallas_call | solution.py:24
  94.4 0.1 slice_bitcast_fusion
  94.5 1.7 %collective-permute-start.29 = (f32[16,128,128]{2,1,0:T(8,128)S(1)}, f32[16,128,128]{2,1,0:T(8,128)S(1)}, u32[]{:S(2)}, u32[]{:S(2)}) collective-permute-start(f32[16,128,128]{2,1,0:T(8,128)S(1)} %slice_bitcast_fusion), channel_id=1, source_target_pairs={{0,1},{1,0},{2,3},{3,2},{4,5},{5,4},{6,7},{7,6},{8,9},{9,8},{10,11... | collective-permute-start | bytes 3145736 | tf_op jit(solution)/shard_map/ppermute | solution.py:40
  96.2 2.3 %collective-permute-done.29.got = f32[16,128,128]{2,1,0:T(8,128)S(1)} collective-permute-done((f32[16,128,128]{2,1,0:T(8,128)S(1)}, f32[16,128,128]{2,1,0:T(8,128)S(1)}, u32[]{:S(2)}, u32[]{:S(2)}) %collective-permute-start.29) | collective-permute-done | bytes 1048608 | tf_op jit(solution)/shard_map/ppermute | solution.py:40
  98.5 0.4 shard_map.53
  98.9 16.4 %all_to_all.10.parts = s16[16,144,128]{2,1,0:T(8,128)(2,1)S(1)} all-to-all(s16[16,144,128]{2,1,0:T(8,128)(2,1)S(1)} %shard_map.53), channel_id=1, replica_groups=mesh['z'=8,'y'=4,'x'=4,'core'=2] {'y','x'}, dimensions={0} | all-to-all | bytes 1179648 | tf_op jit(solution)/shard_map/all_to_all | solution.py:256
  115.3 0.8 shard_map.54
  (33 shorter events, 0.1 us)
Async XLA Ops:
  1.4 16.8 %all-to-all-start = ((bf16[8,64,128]{2,1,0:T(8,128)(2,1)}), bf16[8,64,128]{2,1,0:T(8,128)(2,1)S(1)}, u32[]{:S(2)}, u32[]{:S(2)}) async-start(bf16[8,64,128]{2,1,0:T(8,128)(2,1)} %broadcast_in_dim.2), calls=%async_computation | async-start | bytes 262144 | tf_op jit(solution)/shard_map/all_to_all | solution.py:205
  11.1 1.6 %copy-start = (bf16[16,4,128,128]{3,2,1,0:T(8,128)(2,1)S(1)}, bf16[16,4,128,128]{3,2,1,0:T(8,128)(2,1)}, u32[]{:S(2)}) copy-start(bf16[16,4,128,128]{3,2,1,0:T(8,128)(2,1)} %source.1) | copy-start | bytes 6291460
  12.7 0.7 copy-start.7
  18.2 5.1 %collective-permute-start = (bf16[8,64,128]{2,1,0:T(8,128)(2,1)S(1)}, bf16[8,64,128]{2,1,0:T(8,128)(2,1)S(1)}, u32[]{:S(2)}, u32[]{:S(2)}) collective-permute-start(bf16[8,64,128]{2,1,0:T(8,128)(2,1)S(1)} %all-to-all-done.refs_0_), channel_id=1, source_target_pairs={{0,8},{8,16},{16,24},{24,0},{1,9},{9,17},{17,25},{25,1},{2,10},{10... | collective-permute-start | bytes 393224 | tf_op jit(solution)/shard_map/ppermute | solution.py:40
  19.5 6.5 %collective-permute-start.1 = (bf16[8,64,128]{2,1,0:T(8,128)(2,1)S(1)}, bf16[8,64,128]{2,1,0:T(8,128)(2,1)S(1)}, u32[]{:S(2)}, u32[]{:S(2)}) collective-permute-start(bf16[8,64,128]{2,1,0:T(8,128)(2,1)S(1)} %all-to-all-done.refs_0_), channel_id=1, source_target_pairs={{0,16},{8,24},{16,0},{24,8},{1,17},{9,25},{17,1},{25,9},{2,18},{10... | collective-permute-start | bytes 393224 | tf_op jit(solution)/shard_map/ppermute | solution.py:40
  22.1 4.6 %collective-permute-start.2 = (bf16[8,64,128]{2,1,0:T(8,128)(2,1)S(1)}, bf16[8,64,128]{2,1,0:T(8,128)(2,1)S(1)}, u32[]{:S(2)}, u32[]{:S(2)}) collective-permute-start(bf16[8,64,128]{2,1,0:T(8,128)(2,1)S(1)} %all-to-all-done.refs_0_), channel_id=1, source_target_pairs={{0,24},{8,0},{16,8},{24,16},{1,25},{9,1},{17,9},{25,17},{2,26},{10... | collective-permute-start | bytes 393224 | tf_op jit(solution)/shard_map/ppermute | solution.py:40
  27.5 8.3 %collective-permute-start.7 = (bf16[16,64,128]{2,1,0:T(8,128)(2,1)S(1)}, bf16[16,64,128]{2,1,0:T(8,128)(2,1)S(1)}, u32[]{:S(2)}, u32[]{:S(2)}) collective-permute-start(bf16[16,64,128]{2,1,0:T(8,128)(2,1)S(1)} %shard_map.47.refs_0_), channel_id=1, source_target_pairs={{0,2},{2,4},{4,6},{6,0},{1,3},{3,5},{5,7},{7,1},{8,10},{10,12},{12... | collective-permute-start | bytes 786440 | tf_op jit(solution)/shard_map/ppermute | solution.py:40
  28.8 12.4 %collective-permute-start.3 = (bf16[16,64,128]{2,1,0:T(8,128)(2,1)S(1)}, bf16[16,64,128]{2,1,0:T(8,128)(2,1)S(1)}, u32[]{:S(2)}, u32[]{:S(2)}) collective-permute-start(bf16[16,64,128]{2,1,0:T(8,128)(2,1)S(1)} %shard_map.47.refs_0_), channel_id=1, source_target_pairs={{0,6},{2,0},{4,2},{6,4},{1,7},{3,1},{5,3},{7,5},{8,14},{10,8},{12,... | collective-permute-start | bytes 786440 | tf_op jit(solution)/shard_map/ppermute | solution.py:40
  30.2 10.9 %collective-permute-start.4 = (bf16[16,64,128]{2,1,0:T(8,128)(2,1)S(1)}, bf16[16,64,128]{2,1,0:T(8,128)(2,1)S(1)}, u32[]{:S(2)}, u32[]{:S(2)}) collective-permute-start(bf16[16,64,128]{2,1,0:T(8,128)(2,1)S(1)} %shard_map.47.refs_0_), channel_id=1, source_target_pairs={{0,4},{2,6},{4,0},{6,2},{1,5},{3,7},{5,1},{7,3},{8,12},{10,14},{12... | collective-permute-start | bytes 786440 | tf_op jit(solution)/shard_map/ppermute | solution.py:40
  31.8 12.3 %collective-permute-start.8 = (bf16[16,64,128]{2,1,0:T(8,128)(2,1)S(1)}, bf16[16,64,128]{2,1,0:T(8,128)(2,1)S(1)}, u32[]{:S(2)}, u32[]{:S(2)}) collective-permute-start(bf16[16,64,128]{2,1,0:T(8,128)(2,1)S(1)} %shard_map.47.refs_0_), channel_id=1, source_target_pairs={{0,1},{1,0},{2,3},{3,2},{4,5},{5,4},{6,7},{7,6},{8,9},{9,8},{10,11... | collective-permute-start | bytes 786440 | tf_op jit(solution)/shard_map/ppermute | solution.py:40
  35.8 8.3 %collective-permute-start.9 = (bf16[16,64,128]{2,1,0:T(8,128)(2,1)S(1)}, bf16[16,64,128]{2,1,0:T(8,128)(2,1)S(1)}, u32[]{:S(2)}, u32[]{:S(2)}) collective-permute-start(bf16[16,64,128]{2,1,0:T(8,128)(2,1)S(1)} %collective-permute-done.7.refs_1_), channel_id=1, source_target_pairs={{0,1},{1,0},{2,3},{3,2},{4,5},{5,4},{6,7},{7,6},{8,9},{9,8},{10,11... | collective-permute-start | bytes 786440 | tf_op jit(solution)/shard_map/ppermute | solution.py:40
  41.1 4.6 %collective-permute-start.5 = (bf16[16,64,128]{2,1,0:T(8,128)(2,1)S(1)}, bf16[16,64,128]{2,1,0:T(8,128)(2,1)S(1)}, u32[]{:S(2)}, u32[]{:S(2)}) collective-permute-start(bf16[16,64,128]{2,1,0:T(8,128)(2,1)S(1)} %collective-permute-done.3.refs_0_), channel_id=1, source_target_pairs={{0,1},{1,0},{2,3},{3,2},{4,5},{5,4},{6,7},{7,6},{8,9},{9,8},{10,11... | collective-permute-start | bytes 786440 | tf_op jit(solution)/shard_map/ppermute | solution.py:40
  41.1 4.6 %collective-permute-start.6 = (bf16[16,64,128]{2,1,0:T(8,128)(2,1)S(1)}, bf16[16,64,128]{2,1,0:T(8,128)(2,1)S(1)}, u32[]{:S(2)}, u32[]{:S(2)}) collective-permute-start(bf16[16,64,128]{2,1,0:T(8,128)(2,1)S(1)} %collective-permute-done.4.refs_1_), channel_id=1, source_target_pairs={{0,1},{1,0},{2,3},{3,2},{4,5},{5,4},{6,7},{7,6},{8,9},{9,8},{10,11... | collective-permute-start | bytes 786440 | tf_op jit(solution)/shard_map/ppermute | solution.py:40
  44.8 9.2 %collective-permute-start.11 = (bf16[1,128,1024]{2,1,0:T(8,128)(2,1)S(1)}, bf16[1,128,1024]{2,1,0:T(8,128)(2,1)S(1)}, u32[]{:S(2)}, u32[]{:S(2)}) collective-permute-start(bf16[1,128,1024]{2,1,0:T(8,128)(2,1)S(1)} %shard_map.48.refs_4_), channel_id=1, source_target_pairs={{0,32},{32,64},{64,96},{96,128},{128,160},{160,192},{192,224},{224... | collective-permute-start | bytes 786440 | tf_op jit(solution)/shard_map/ppermute | solution.py:40
  46.5 17.3 %collective-permute-start.15 = (bf16[2,128,1024]{2,1,0:T(8,128)(2,1)S(1)}, bf16[2,128,1024]{2,1,0:T(8,128)(2,1)S(1)}, u32[]{:S(2)}, u32[]{:S(2)}) collective-permute-start(bf16[2,128,1024]{2,1,0:T(8,128)(2,1)S(1)} %get-tuple-element.16.refs_0_), channel_id=1, source_target_pairs={{0,24},{1,9},{8,0},{9,17},{16,8},{17,25},{24,16},{25,1},{2,26},{3,... | collective-permute-start | bytes 1572872 | tf_op jit(solution)/shard_map/ppermute | solution.py:48
  46.6 20.6 %collective-permute-start.10 = (bf16[2,128,1024]{2,1,0:T(8,128)(2,1)S(1)}, bf16[2,128,1024]{2,1,0:T(8,128)(2,1)S(1)}, u32[]{:S(2)}, u32[]{:S(2)}) collective-permute-start(bf16[2,128,1024]{2,1,0:T(8,128)(2,1)S(1)} %get-tuple-element.16.refs_0_), channel_id=1, source_target_pairs={{0,8},{1,25},{8,16},{9,1},{16,24},{17,9},{24,0},{25,17},{2,10},{3,... | collective-permute-start | bytes 1572872 | tf_op jit(solution)/shard_map/ppermute | solution.py:48
  49.3 7.9 %collective-permute-start.13 = (bf16[1,128,1024]{2,1,0:T(8,128)(2,1)S(1)}, bf16[1,128,1024]{2,1,0:T(8,128)(2,1)S(1)}, u32[]{:S(2)}, u32[]{:S(2)}) collective-permute-start(bf16[1,128,1024]{2,1,0:T(8,128)(2,1)S(1)} %shard_map.48.refs_4_), channel_id=1, source_target_pairs={{0,224},{32,0},{64,32},{96,64},{128,96},{160,128},{192,160},{224,1... | collective-permute-start | bytes 786440 | tf_op jit(solution)/shard_map/ppermute | solution.py:40
  51.1 8.7 %collective-permute-start.17 = (bf16[1,128,1024]{2,1,0:T(8,128)(2,1)S(1)}, bf16[1,128,1024]{2,1,0:T(8,128)(2,1)S(1)}, u32[]{:S(2)}, u32[]{:S(2)}) collective-permute-start(bf16[1,128,1024]{2,1,0:T(8,128)(2,1)S(1)} %get-tuple-element.18), channel_id=1, source_target_pairs={{0,32},{32,64},{64,96},{96,128},{128,160},{160,192},{192,224},{224... | collective-permute-start | bytes 786440 | tf_op jit(solution)/shard_map/ppermute | solution.py:40
  54.1 8.7 %collective-permute-start.21 = (bf16[1,128,1024]{2,1,0:T(8,128)(2,1)S(1)}, bf16[1,128,1024]{2,1,0:T(8,128)(2,1)S(1)}, u32[]{:S(2)}, u32[]{:S(2)}) collective-permute-start(bf16[1,128,1024]{2,1,0:T(8,128)(2,1)S(1)} %get-tuple-element.18), channel_id=1, source_target_pairs={{0,224},{32,0},{64,32},{96,64},{128,96},{160,128},{192,160},{224,1... | collective-permute-start | bytes 786440 | tf_op jit(solution)/shard_map/ppermute | solution.py:40
  57.1 10.2 %collective-permute-start.12 = (bf16[1,128,1024]{2,1,0:T(8,128)(2,1)S(1)}, bf16[1,128,1024]{2,1,0:T(8,128)(2,1)}, u32[]{:S(2)}, u32[]{:S(2)}) collective-permute-start(bf16[1,128,1024]{2,1,0:T(8,128)(2,1)S(1)} %collective-permute-done.11.refs_5_), channel_id=1, source_target_pairs={{0,32},{32,64},{64,96},{96,128},{128,160},{160,192},{192,224},{224... | collective-permute-start | bytes 786440 | tf_op jit(solution)/shard_map/ppermute | solution.py:40
  59.8 8.1 %collective-permute-start.14 = (bf16[1,128,1024]{2,1,0:T(8,128)(2,1)S(1)}, bf16[1,128,1024]{2,1,0:T(8,128)(2,1)}, u32[]{:S(2)}, u32[]{:S(2)}) collective-permute-start(bf16[1,128,1024]{2,1,0:T(8,128)(2,1)S(1)} %collective-permute-done.13.refs_7_), channel_id=1, source_target_pairs={{0,224},{32,0},{64,32},{96,64},{128,96},{160,128},{192,160},{224,1... | collective-permute-start | bytes 786440 | tf_op jit(solution)/shard_map/ppermute | solution.py:40
  60.2 0.7 copy-start.1
  62.8 8.8 %collective-permute-start.18 = (bf16[1,128,1024]{2,1,0:T(8,128)(2,1)S(1)}, bf16[1,128,1024]{2,1,0:T(8,128)(2,1)}, u32[]{:S(2)}, u32[]{:S(2)}) collective-permute-start(bf16[1,128,1024]{2,1,0:T(8,128)(2,1)S(1)} %collective-permute-done.17.refs_4_), channel_id=1, source_target_pairs={{0,32},{32,64},{64,96},{96,128},{128,160},{160,192},{192,224},{224... | collective-permute-start | bytes 786440 | tf_op jit(solution)/shard_map/ppermute | solution.py:40
  63.1 0.7 copy-start.3
  63.8 9.8 %collective-permute-start.22 = (bf16[1,128,1024]{2,1,0:T(8,128)(2,1)S(1)}, bf16[1,128,1024]{2,1,0:T(8,128)(2,1)}, u32[]{:S(2)}, u32[]{:S(2)}) collective-permute-start(bf16[1,128,1024]{2,1,0:T(8,128)(2,1)S(1)} %collective-permute-done.21.refs_6_), channel_id=1, source_target_pairs={{0,224},{32,0},{64,32},{96,64},{128,96},{160,128},{192,160},{224,1... | collective-permute-start | bytes 786440 | tf_op jit(solution)/shard_map/ppermute | solution.py:40
  66.5 0.7 copy-start.5
  67.2 21.4 %collective-permute-start.16 = (bf16[2,128,1024]{2,1,0:T(8,128)(2,1)S(1)}, bf16[2,128,1024]{2,1,0:T(8,128)(2,1)S(1)}, u32[]{:S(2)}, u32[]{:S(2)}) collective-permute-start(bf16[2,128,1024]{2,1,0:T(8,128)(2,1)S(1)} %collective-permute-done.10.refs_1_), channel_id=1, source_target_pairs={{0,8},{1,25},{8,16},{9,1},{16,24},{17,9},{24,0},{25,17},{2,10},{3,... | collective-permute-start | bytes 1572872 | tf_op jit(solution)/shard_map/ppermute | solution.py:48
  68.0 9.1 %collective-permute-start.20 = (bf16[1,128,1024]{2,1,0:T(8,128)(2,1)}, bf16[1,128,1024]{2,1,0:T(8,128)(2,1)S(1)}, u32[]{:S(2)}, u32[]{:S(2)}) collective-permute-start(bf16[1,128,1024]{2,1,0:T(8,128)(2,1)} %collective-permute-done.12.refs_9_), channel_id=1, source_target_pairs={{0,32},{32,64},{64,96},{96,128},{128,160},{160,192},{192,224},{224... | collective-permute-start | bytes 786440 | tf_op jit(solution)/shard_map/ppermute | solution.py:40
  68.7 10.6 %collective-permute-start.24 = (bf16[1,128,1024]{2,1,0:T(8,128)(2,1)}, bf16[1,128,1024]{2,1,0:T(8,128)(2,1)S(1)}, u32[]{:S(2)}, u32[]{:S(2)}) collective-permute-start(bf16[1,128,1024]{2,1,0:T(8,128)(2,1)} %collective-permute-done.14.refs_11_), channel_id=1, source_target_pairs={{0,224},{32,0},{64,32},{96,64},{128,96},{160,128},{192,160},{224,1... | collective-permute-start | bytes 786440 | tf_op jit(solution)/shard_map/ppermute | solution.py:40
  71.5 11.2 %collective-permute-start.19 = (bf16[1,128,1024]{2,1,0:T(8,128)(2,1)}, bf16[1,128,1024]{2,1,0:T(8,128)(2,1)S(1)}, u32[]{:S(2)}, u32[]{:S(2)}) collective-permute-start(bf16[1,128,1024]{2,1,0:T(8,128)(2,1)} %collective-permute-done.18.refs_8_), channel_id=1, source_target_pairs={{0,32},{32,64},{64,96},{96,128},{128,160},{160,192},{192,224},{224... | collective-permute-start | bytes 786440 | tf_op jit(solution)/shard_map/ppermute | solution.py:40
  73.6 11.3 %collective-permute-start.23 = (bf16[1,128,1024]{2,1,0:T(8,128)(2,1)}, bf16[1,128,1024]{2,1,0:T(8,128)(2,1)S(1)}, u32[]{:S(2)}, u32[]{:S(2)}) collective-permute-start(bf16[1,128,1024]{2,1,0:T(8,128)(2,1)} %collective-permute-done.22.refs_10_), channel_id=1, source_target_pairs={{0,224},{32,0},{64,32},{96,64},{128,96},{160,128},{192,160},{224,1... | collective-permute-start | bytes 786440 | tf_op jit(solution)/shard_map/ppermute | solution.py:40
  77.1 15.3 %collective-permute-start.27 = (bf16[1,64,1024]{2,1,0:T(8,128)(2,1)S(1)}, bf16[1,64,1024]{2,1,0:T(8,128)(2,1)S(1)}, u32[]{:S(2)}, u32[]{:S(2)}) collective-permute-start(bf16[1,64,1024]{2,1,0:T(8,128)(2,1)S(1)} %slice.22), channel_id=1, source_target_pairs={{0,32},{32,64},{64,96},{96,128},{128,160},{160,192},{192,224},{224... | collective-permute-start | bytes 393224 | tf_op jit(solution)/shard_map/ppermute | solution.py:40
  79.3 13.1 %collective-permute-start.28 = (bf16[1,64,1024]{2,1,0:T(8,128)(2,1)S(1)}, bf16[1,64,1024]{2,1,0:T(8,128)(2,1)S(1)}, u32[]{:S(2)}, u32[]{:S(2)}) collective-permute-start(bf16[1,64,1024]{2,1,0:T(8,128)(2,1)S(1)} %slice.23), channel_id=1, source_target_pairs={{0,224},{32,0},{64,32},{96,64},{128,96},{160,128},{192,160},{224,1... | collective-permute-start | bytes 393224 | tf_op jit(solution)/shard_map/ppermute | solution.py:40
  82.7 9.8 %collective-permute-start.25 = (bf16[1,64,1024]{2,1,0:T(8,128)(2,1)S(1)}, bf16[1,64,1024]{2,1,0:T(8,128)(2,1)S(1)}, u32[]{:S(2)}, u32[]{:S(2)}) collective-permute-start(bf16[1,64,1024]{2,1,0:T(8,128)(2,1)S(1)} %slice.20), channel_id=1, source_target_pairs={{0,32},{32,64},{64,96},{96,128},{128,160},{160,192},{192,224},{224... | collective-permute-start | bytes 393224 | tf_op jit(solution)/shard_map/ppermute | solution.py:40
  85.0 7.6 %collective-permute-start.26 = (bf16[1,64,1024]{2,1,0:T(8,128)(2,1)S(1)}, bf16[1,64,1024]{2,1,0:T(8,128)(2,1)S(1)}, u32[]{:S(2)}, u32[]{:S(2)}) collective-permute-start(bf16[1,64,1024]{2,1,0:T(8,128)(2,1)S(1)} %slice.21), channel_id=1, source_target_pairs={{0,224},{32,0},{64,32},{96,64},{128,96},{160,128},{192,160},{224,1... | collective-permute-start | bytes 393224 | tf_op jit(solution)/shard_map/ppermute | solution.py:40
  88.6 1.3 %copy-start.2 = (bf16[1,128,1024]{2,1,0:T(8,128)(2,1)S(1)}, bf16[1,128,1024]{2,1,0:T(8,128)(2,1)}, u32[]{:S(2)}) copy-start(bf16[1,128,1024]{2,1,0:T(8,128)(2,1)} %copy-done.1) | copy-start | bytes 786436
  88.6 1.3 %copy-start.4 = (bf16[1,128,1024]{2,1,0:T(8,128)(2,1)S(1)}, bf16[1,128,1024]{2,1,0:T(8,128)(2,1)}, u32[]{:S(2)}) copy-start(bf16[1,128,1024]{2,1,0:T(8,128)(2,1)} %copy-done.3) | copy-start | bytes 786436
  88.6 1.3 %copy-start.6 = (bf16[1,128,1024]{2,1,0:T(8,128)(2,1)S(1)}, bf16[1,128,1024]{2,1,0:T(8,128)(2,1)}, u32[]{:S(2)}) copy-start(bf16[1,128,1024]{2,1,0:T(8,128)(2,1)} %copy-done.5) | copy-start | bytes 786436
  94.5 4.0 %collective-permute-start.29 = (f32[16,128,128]{2,1,0:T(8,128)S(1)}, f32[16,128,128]{2,1,0:T(8,128)S(1)}, u32[]{:S(2)}, u32[]{:S(2)}) collective-permute-start(f32[16,128,128]{2,1,0:T(8,128)S(1)} %slice_bitcast_fusion), channel_id=1, source_target_pairs={{0,1},{1,0},{2,3},{3,2},{4,5},{5,4},{6,7},{7,6},{8,9},{9,8},{10,11... | collective-permute-start | bytes 3145736 | tf_op jit(solution)/shard_map/ppermute | solution.py:40
